TPU v7x, 32 devices: a whole 2x2x4 slice. The times are simulated.
32 devices in a mesh: expert: 8 (over z, x), tensor: 4 (over y, core).
Axes of the slice: x: 2, y: 2, z: 4, core: 2. Of those that a mesh axis runs over, the one named last changes fastest.
Arguments:
- inputs: bfloat16 [8192, 1536], P('expert'), may hold values from -6 to 6
- routes: int32 [8192, 4], P('expert'), may hold values from 0 to 7, all different within a row; in each aligned block of 1024 rows (0 to 1023, 1024 to 2047, ...) at most 768 rows name the same one
- cotangent: bfloat16 [8192, 1536], P('expert'), may hold values from -6 to 6
- first_gain: float32 [1536], replicated, may hold values from 0.5 to 1.5
- second_gain: float32 [1536], replicated, may hold values from 0.5 to 1.5
- w_query: bfloat16 [1536, 1536], P(None, 'tensor'), may hold values from -0.15625 to 0.15625
- w_key: bfloat16 [1536, 256], replicated, may hold values from -0.15625 to 0.15625
- w_value: bfloat16 [1536, 256], replicated, may hold values from -0.15625 to 0.15625
- w_output: bfloat16 [1536, 1536], P('tensor'), may hold values from -0.47851562 to 0.47851562
- w_router: bfloat16 [1536, 8], replicated, may hold values from -0.076660156 to 0.076660156
- w_gate: bfloat16 [8, 1536, 768], P('expert', None, 'tensor'), may hold values from -0.15625 to 0.15625
- w_up: bfloat16 [8, 1536, 768], P('expert', None, 'tensor'), may hold values from -0.15625 to 0.15625
- w_down: bfloat16 [8, 768, 1536], P('expert', 'tensor'), may hold values from -3 to 3
Outputs:
- layer_out: bfloat16 [8192, 1536], P('expert')
- grad_inputs: bfloat16 [8192, 1536], P('expert')
- grad_first: float32 [1536], replicated
- grad_second: float32 [1536], replicated
- grad_query: float32 [1536, 1536], P(None, 'tensor')
- grad_key: float32 [1536, 256], replicated
- grad_value: float32 [1536, 256], replicated
- grad_output: float32 [1536, 1536], P('tensor')
- grad_router: float32 [1536, 8], replicated
- grad_gate: float32 [8, 1536, 768], P('expert', None, 'tensor')
- grad_up: float32 [8, 1536, 768], P('expert', None, 'tensor')
- grad_down: float32 [8, 768, 1536], P('expert', 'tensor')
Inputs may be any that keep to these rules, and one draw needn't show every extreme that they name: `routes`: each row names 4 different experts. Within the rows of one device (aligned blocks of 1024 rows) no expert is named by more than 768 rows, a bound that some block reaches.
All inputs are finite; a program needn't handle non-finite values.
Results may differ from a plain program's by a relative error of at most 0.019.
Values may be sent and summed in bfloat16 or wider, within the bound.
A program may use at most 320 MiB of HBM per device.

v0:
```python
import jax
import jax.numpy as jnp
from jax import lax
from jax.sharding import PartitionSpec as P

HEADS = 12
KV = 2
HD = 128


EPSILON = 1e-06
ROPE_BASE = 10000.0
NEGATIVE = -1e30


def rms_norm(values, gain):
    inverse = lax.rsqrt(jnp.mean(values * values, axis=-1, keepdims=True) + EPSILON)
    normed = values * inverse
    return (normed * gain, normed, inverse)


def norm_backward(upstream, normed, inverse, gain):
    scaled = upstream * gain
    through = inverse * (scaled - normed * jnp.mean(scaled * normed, axis=-1, keepdims=True))
    return (through, jnp.sum(upstream * normed, axis=0))


def rotary_tables(length, head_size):
    half_size = head_size // 2
    positions = jnp.arange(length, dtype=jnp.float32)[:, None]
    frequency = ROPE_BASE ** (-jnp.arange(half_size, dtype=jnp.float32) * 2.0 / head_size)
    angles = positions * frequency[None, :]
    return (jnp.cos(angles), jnp.sin(angles))


def rotate(values, cos_table, sin_table):
    half_size = values.shape[-1] // 2
    leading = values[..., :half_size]
    trailing = values[..., half_size:]
    return jnp.concatenate(
        [leading * cos_table - trailing * sin_table, trailing * cos_table + leading * sin_table],
        axis=-1,
    )


def unrotate(gradient, cos_table, sin_table):
    half_size = gradient.shape[-1] // 2
    leading = gradient[..., :half_size]
    trailing = gradient[..., half_size:]
    return jnp.concatenate(
        [leading * cos_table + trailing * sin_table, trailing * cos_table - leading * sin_table],
        axis=-1,
    )


def block_scores(query_block, start, key_rot, score_scale):
    raw_scores = (
        jnp.einsum("qhd,kd->hqk", query_block, key_rot, preferred_element_type=jnp.float32)
        * score_scale
    )
    rows_at = start + jnp.arange(query_block.shape[0], dtype=jnp.int32)
    cols_at = jnp.arange(key_rot.shape[0], dtype=jnp.int32)
    allowed = cols_at[None, :] <= rows_at[:, None]
    return jnp.where(allowed[None], raw_scores, NEGATIVE)


def deliver(buffer):
    return lax.all_to_all(buffer, "expert", split_axis=0, concat_axis=0, tiled=True)


def shards(
    inputs,
    routes,
    cotangent,
    first_gain,
    second_gain,
    w_query,
    w_key,
    w_value,
    w_output,
    w_router,
    w_gate,
    w_up,
    w_down,
):
    length, model_width = inputs.shape
    head_size = HD
    local_heads = w_query.shape[1] // head_size
    group_size = HEADS // KV
    tensor_rank = lax.axis_index("tensor")
    kv_head = tensor_rank * local_heads // group_size
    score_scale = HD ** (-0.5)
    block_rows = min(512, length)
    blocks = length // block_rows
    starts = jnp.arange(blocks, dtype=jnp.int32) * block_rows
    cos_table, sin_table = rotary_tables(length, head_size)
    residual = inputs.astype(jnp.float32)
    grad_out = cotangent.astype(jnp.float32)
    first_out, first_normed, first_inverse = rms_norm(residual, first_gain)
    attn_in = first_out.astype(jnp.bfloat16)
    key_weight = lax.dynamic_slice_in_dim(w_key, kv_head * head_size, head_size, 1)
    value_weight = lax.dynamic_slice_in_dim(w_value, kv_head * head_size, head_size, 1)
    query_proj = jnp.dot(attn_in, w_query, preferred_element_type=jnp.float32).reshape(
        length, local_heads, head_size
    )
    query_rot = rotate(query_proj, cos_table[:, None, :], sin_table[:, None, :]).astype(
        jnp.bfloat16
    )
    key_proj = jnp.dot(attn_in, key_weight, preferred_element_type=jnp.float32)
    key_rot = rotate(key_proj, cos_table, sin_table).astype(jnp.bfloat16)
    value_low = jnp.dot(attn_in, value_weight, preferred_element_type=jnp.float32).astype(
        jnp.bfloat16
    )
    query_blocks = query_rot.reshape(blocks, block_rows, local_heads, head_size)

    def forward_block(packed):
        query_block, start = packed
        scores = block_scores(query_block, start, key_rot, score_scale)
        row_peak = jnp.max(scores, axis=-1, keepdims=True)
        exponent = jnp.exp(scores - row_peak)
        row_total = jnp.sum(exponent, axis=-1, keepdims=True)
        soft_low = (exponent / row_total).astype(jnp.bfloat16)
        context = jnp.einsum("hqk,kd->qhd", soft_low, value_low, preferred_element_type=jnp.float32)
        return (context, (row_peak + jnp.log(row_total))[..., 0])

    contexts, logsum = lax.map(forward_block, (query_blocks, starts))
    attn_low = contexts.reshape(length, local_heads * head_size).astype(jnp.bfloat16)
    attn_part = jnp.dot(attn_low, w_output, preferred_element_type=jnp.float32)
    attn_total = lax.psum(attn_part, "tensor")
    after_attn = residual + attn_total
    second_out, second_normed, second_inverse = rms_norm(after_attn, second_gain)
    expert_in = second_out.astype(jnp.bfloat16)
    experts_all = w_router.shape[1]
    logits = jnp.dot(expert_in, w_router, preferred_element_type=jnp.float32)
    logit_peak = jnp.max(logits, axis=-1, keepdims=True)
    logit_exp = jnp.exp(logits - logit_peak)
    router_probs = logit_exp / jnp.sum(logit_exp, axis=-1, keepdims=True)
    one_hot = (
        routes[:, :, None] == jnp.arange(experts_all, dtype=jnp.int32)[None, None, :]
    ).astype(jnp.float32)
    gate_probs = jnp.einsum("ske,se->sk", one_hot, router_probs, precision=lax.Precision.HIGHEST)
    top_count = routes.shape[1]
    pair_count = length * top_count
    capacity = 3 * length * top_count // (2 * experts_all)
    flat_routes = routes.reshape(pair_count)
    route_hits = (flat_routes[:, None] == jnp.arange(experts_all, dtype=jnp.int32)[None, :]).astype(
        jnp.int32
    )
    before = jnp.cumsum(route_hits, axis=0) - route_hits
    position = jnp.sum(before * route_hits, axis=1)
    slot_index = flat_routes * capacity + position
    slot_pair = (
        jnp.zeros((experts_all * capacity,), jnp.int32)
        .at[slot_index]
        .set(jnp.arange(pair_count, dtype=jnp.int32))
    )
    slot_token = slot_pair // top_count
    slot_filled = (
        jnp.zeros((experts_all * capacity,), jnp.bfloat16)
        .at[slot_index]
        .set(jnp.ones((pair_count,), jnp.bfloat16))
    )
    dispatched = (expert_in[slot_token] * slot_filled[:, None]).reshape(
        experts_all, capacity, model_width
    )
    received = deliver(dispatched).reshape(experts_all * capacity, model_width)
    gate_local = w_gate[0]
    up_local = w_up[0]
    down_local = w_down[0]
    gate_pre = jnp.dot(received, gate_local, preferred_element_type=jnp.float32)
    up_pre = jnp.dot(received, up_local, preferred_element_type=jnp.float32)
    sigmoid_gate = jax.nn.sigmoid(gate_pre)
    activated = gate_pre * sigmoid_gate
    hidden_low = (activated * up_pre).astype(jnp.bfloat16)
    expert_part = jnp.dot(hidden_low, down_local, preferred_element_type=jnp.float32).astype(
        jnp.bfloat16
    )
    returned = lax.all_to_all(
        expert_part.reshape(experts_all, capacity, model_width),
        "expert",
        split_axis=0,
        concat_axis=0,
        tiled=True,
    )
    per_choice = returned.reshape(experts_all * capacity, model_width)[slot_index].reshape(
        length, top_count, model_width
    )
    moe_part = jnp.zeros((length, model_width), jnp.float32)
    gate_columns = []
    for column in range(top_count):
        choice_rows = per_choice[:, column].astype(jnp.float32)
        moe_part = moe_part + gate_probs[:, column : column + 1] * choice_rows
        gate_columns.append(jnp.sum(choice_rows * grad_out, axis=1))
    gate_part = jnp.stack(gate_columns, axis=1)
    moe_total, gate_grads = lax.psum((moe_part, gate_part), "tensor")
    layer_out = (after_attn + moe_total).astype(jnp.bfloat16)
    dprobs = jnp.einsum("ske,sk->se", one_hot, gate_grads, precision=lax.Precision.HIGHEST)
    dlogits = (
        router_probs * (dprobs - jnp.sum(router_probs * dprobs, axis=-1, keepdims=True))
    ).astype(jnp.bfloat16)
    choice_grads = (
        (gate_probs[:, :, None] * grad_out[:, None, :])
        .astype(jnp.bfloat16)
        .reshape(pair_count, model_width)
    )
    grad_buffer = (choice_grads[slot_pair] * slot_filled[:, None]).reshape(
        experts_all, capacity, model_width
    )
    received_grads = deliver(grad_buffer).reshape(experts_all * capacity, model_width)
    hidden_grad = jnp.dot(received_grads, down_local.T, preferred_element_type=jnp.float32)
    up_grad = (hidden_grad * activated).astype(jnp.bfloat16)
    gate_grad = (
        hidden_grad * up_pre * sigmoid_gate * (1.0 + gate_pre * (1.0 - sigmoid_gate))
    ).astype(jnp.bfloat16)
    grad_down_local = jnp.dot(hidden_low.T, received_grads, preferred_element_type=jnp.float32)
    grad_gate_local = jnp.dot(received.T, gate_grad, preferred_element_type=jnp.float32)
    grad_up_local = jnp.dot(received.T, up_grad, preferred_element_type=jnp.float32)
    row_grads = (
        jnp.dot(gate_grad, gate_local.T, preferred_element_type=jnp.float32)
        + jnp.dot(up_grad, up_local.T, preferred_element_type=jnp.float32)
    ).astype(jnp.bfloat16)
    back_grads = lax.all_to_all(
        row_grads.reshape(experts_all, capacity, model_width),
        "expert",
        split_axis=0,
        concat_axis=0,
        tiled=True,
    )
    pair_grads = back_grads.reshape(experts_all * capacity, model_width)[slot_index].reshape(
        length, top_count, model_width
    )
    input_part = jnp.zeros((length, model_width), jnp.float32)
    for column in range(top_count):
        input_part = input_part + pair_grads[:, column].astype(jnp.float32)
    expert_grad_in = lax.psum(input_part, "tensor")
    expert_grad_in = expert_grad_in + jnp.dot(
        dlogits, w_router.T, preferred_element_type=jnp.float32
    )
    grad_router_local = jnp.dot(expert_in.T, dlogits, preferred_element_type=jnp.float32)
    through_second, grad_second_local = norm_backward(
        expert_grad_in, second_normed, second_inverse, second_gain
    )
    grad_after = grad_out + through_second
    attn_grad_low = grad_after.astype(jnp.bfloat16)
    grad_output_local = jnp.dot(attn_low.T, attn_grad_low, preferred_element_type=jnp.float32)
    context_grad = jnp.dot(attn_grad_low, w_output.T, preferred_element_type=jnp.float32).astype(
        jnp.bfloat16
    )
    grad_blocks = context_grad.reshape(blocks, block_rows, local_heads, head_size)

    def backward_block(packed):
        query_block, grad_block, start, logsum_block = packed
        scores = block_scores(query_block, start, key_rot, score_scale)
        soft_weights = jnp.exp(scores - logsum_block[..., None])
        soft_low = soft_weights.astype(jnp.bfloat16)
        dprobs_block = jnp.einsum(
            "qhd,kd->hqk", grad_block, value_low, preferred_element_type=jnp.float32
        )
        row_delta = jnp.sum(soft_weights * dprobs_block, axis=-1, keepdims=True)
        dscores = (soft_weights * (dprobs_block - row_delta)).astype(jnp.bfloat16)
        dquery = (
            jnp.einsum("hqk,kd->qhd", dscores, key_rot, preferred_element_type=jnp.float32)
            * score_scale
        )
        key_grad_part = (
            jnp.einsum("hqk,qhd->kd", dscores, query_block, preferred_element_type=jnp.float32)
            * score_scale
        )
        value_grad_part = jnp.einsum(
            "hqk,qhd->kd", soft_low, grad_block, preferred_element_type=jnp.float32
        )
        return (dquery, key_grad_part, value_grad_part)

    dquery_blocks, key_parts, value_parts = lax.map(
        backward_block, (query_blocks, grad_blocks, starts, logsum)
    )
    query_grad = (
        unrotate(
            dquery_blocks.reshape(length, local_heads, head_size),
            cos_table[:, None, :],
            sin_table[:, None, :],
        )
        .astype(jnp.bfloat16)
        .reshape(length, local_heads * head_size)
    )
    key_grad = unrotate(jnp.sum(key_parts, axis=0), cos_table, sin_table).astype(jnp.bfloat16)
    value_grad = jnp.sum(value_parts, axis=0).astype(jnp.bfloat16)
    grad_query_local = jnp.dot(attn_in.T, query_grad, preferred_element_type=jnp.float32)
    grad_key_head = jnp.dot(attn_in.T, key_grad, preferred_element_type=jnp.float32)
    grad_value_head = jnp.dot(attn_in.T, value_grad, preferred_element_type=jnp.float32)
    input_attn_part = jnp.dot(query_grad, w_query.T, preferred_element_type=jnp.float32)
    input_attn_part = input_attn_part + jnp.dot(
        key_grad, key_weight.T, preferred_element_type=jnp.float32
    )
    input_attn_part = input_attn_part + jnp.dot(
        value_grad, value_weight.T, preferred_element_type=jnp.float32
    )
    attn_grad_in = lax.psum(input_attn_part, "tensor")
    through_first, grad_first_local = norm_backward(
        attn_grad_in, first_normed, first_inverse, first_gain
    )
    grad_inputs = (grad_after + through_first).astype(jnp.bfloat16)
    grad_key_full = lax.dynamic_update_slice_in_dim(
        jnp.zeros(w_key.shape, jnp.float32), grad_key_head, kv_head * head_size, 1
    )
    grad_value_full = lax.dynamic_update_slice_in_dim(
        jnp.zeros(w_value.shape, jnp.float32), grad_value_head, kv_head * head_size, 1
    )
    is_lead = (tensor_rank == 0).astype(jnp.float32)
    grad_query, grad_output = lax.psum((grad_query_local, grad_output_local), "expert")
    grad_key, grad_value, grad_first, grad_second, grad_router = lax.psum(
        (
            grad_key_full,
            grad_value_full,
            grad_first_local * is_lead,
            grad_second_local * is_lead,
            grad_router_local * is_lead,
        ),
        ("expert", "tensor"),
    )
    return (
        layer_out,
        grad_inputs,
        grad_first,
        grad_second,
        grad_query,
        grad_key,
        grad_value,
        grad_output,
        grad_router,
        grad_gate_local[None],
        grad_up_local[None],
        grad_down_local[None],
    )


def solution(mesh):
    in_specs = (
        P("expert", None),
        P("expert", None),
        P("expert", None),
        P(),
        P(),
        P(None, "tensor"),
        P(),
        P(),
        P("tensor", None),
        P(),
        P("expert", None, "tensor"),
        P("expert", None, "tensor"),
        P("expert", "tensor", None),
    )
    out_specs = (
        P("expert", None),
        P("expert", None),
        P(),
        P(),
        P(None, "tensor"),
        P(),
        P(),
        P("tensor", None),
        P(),
        P("expert", None, "tensor"),
        P("expert", None, "tensor"),
        P("expert", "tensor", None),
    )
    return jax.shard_map(shards, mesh=mesh, in_specs=in_specs, out_specs=out_specs, check_vma=False)
```

profile of v0, /device:TPU:1, one launch (start us, length us, event | category | flops | bytes accessed | tf_op | source)
XLA Modules:
  0.0 3001.9 jit_solution(2387740647105900930)
XLA Ops:
  36.5 16.4 while.26
  56.5 4.5 fusion.126
  65.9 28.6 scatter_custom_fusion.1
  94.6 15.5 scatter_custom_fusion
  110.8 71.8 %all-reduce.10.cloned.1.call-done = f32[1024,1536]{1,0:T(8,128)} async-done(((f32[1024,1536]{1,0:T(8,128)}), f32[1024,1536]{1,0:T(8,128)}) %all-reduce.10.cloned.1.call-update) | async-done | bytes 6291472 | tf_op jit(solution)/shard_map/psum | solution.py:129
  182.6 4.6 multiply_reduce_fusion.2
  192.1 39.6 %gather_fusion = bf16[6144,1536]{1,0:T(8,128)(2,1)} fusion(bf16[1024,1536]{1,0:T(8,128)(2,1)} %multiply_convert_fusion.1, s32[6144]{0:T(1024)S(1)} %get-tuple-element.280), kind=kCustom, calls=%fused_computation | custom fusion | bytes 37773312 | tf_op jit(solution)/shard_map/gather | solution.py:163
  231.8 10.3 broadcast_multiply_fusion.1
  242.1 412.6 %all_to_all.20 = bf16[8,768,1536]{2,1,0:T(8,128)(2,1)S(1)} all-to-all(bf16[8,768,1536]{2,1,0:T(8,128)(2,1)S(1)} %broadcast_multiply_fusion.1), channel_id=1, replica_groups=mesh['expert'=8,'tensor'=4] {'expert'}, dimensions={0} | all-to-all | bytes 37748736 | tf_op jit(solution)/shard_map/all_to_all | solution.py:68
  654.7 7.9 fusion.86
  662.6 10.1 multiply_convert_fusion.4
  672.8 11.0 convolution_convert_fusion
  683.8 5.9 all-to-all-start.1
  689.7 12.9 mul.527
  702.6 29.3 mul.528
  734.7 361.0 %all-to-all-done.1 = bf16[8,768,1536]{2,1,0:T(8,128)(2,1)} async-done(((bf16[8,768,1536]{2,1,0:T(8,128)(2,1)}), bf16[8,768,1536]{2,1,0:T(8,128)(2,1)}, u32[]{:S(2)}, u32[]{:S(2)}) %all-to-all-start.1) | async-done | bytes 18874400 | tf_op jit(solution)/shard_map/all_to_all | solution.py:178
  1095.7 34.1 %gather_fusion.1 = bf16[4096,1536]{1,0:T(8,128)(2,1)} fusion(bf16[6144,1536]{1,0:T(8,128)(2,1)} %bitcast.35, s32[4096]{0:T(1024)S(1)} %broadcast_clamp_fusion), kind=kCustom, calls=%fused_computation.1 | custom fusion | bytes 25182208 | tf_op jit(solution)/shard_map/gather | solution.py:185
  1129.8 21.0 reshape.295
  1150.8 34.2 %fusion.121 = (bf16[1024,1,1536]{2,1,0:T(2,128)(2,1)}, bf16[1024,1,1536]{2,1,0:T(2,128)(2,1)}, bf16[1024,1,1536]{2,1,0:T(2,128)(2,1)}, bf16[1024,1,1536]{2,1,0:T(2,128)(2,1)}) fusion(bf16[1024,4,1536]{2,1,0:T(4,128)(2,1)} %reshape.295), kind=kLoop, calls=%fused_computation.221 | loop fusion | bytes 25165824 | tf_op jit(solution)/shard_map/slice | solution.py:191
  1185.0 12.8 fusion.58
  1197.8 10.8 psum.87
  1210.5 13.6 multiply_convert_fusion
  1224.1 43.6 %gather_fusion.2 = bf16[6144,1536]{1,0:T(8,128)(2,1)} fusion(bf16[4096,1536]{1,0:T(8,128)(2,1)} %multiply_convert_fusion, s32[6144]{0:T(1024)S(1)} %copy-done.62), kind=kCustom, calls=%fused_computation.2 | custom fusion | bytes 37773312 | tf_op jit(solution)/shard_map/gather | solution.py:206
  1267.7 10.3 broadcast_multiply_fusion
  1278.0 411.8 %all_to_all.21 = bf16[8,768,1536]{2,1,0:T(8,128)(2,1)} all-to-all(bf16[8,768,1536]{2,1,0:T(8,128)(2,1)S(1)} %broadcast_multiply_fusion), channel_id=1, replica_groups=mesh['expert'=8,'tensor'=4] {'expert'}, dimensions={0} | all-to-all | bytes 37748736 | tf_op jit(solution)/shard_map/all_to_all | solution.py:68
  1689.8 19.8 multiply_convert_fusion.2
  1709.6 14.8 fusion.84
  1724.4 21.1 add_convert_fusion
  1745.5 415.6 %all_to_all.22 = bf16[8,768,1536]{2,1,0:T(8,128)(2,1)} all-to-all(bf16[8,768,1536]{2,1,0:T(8,128)(2,1)} %bitcast.310), channel_id=1, replica_groups=mesh['expert'=8,'tensor'=4] {'expert'}, dimensions={0} | all-to-all | bytes 37748736 | tf_op jit(solution)/shard_map/all_to_all | solution.py:222
  2161.1 34.1 %gather_fusion.3 = bf16[4096,1536]{1,0:T(8,128)(2,1)} fusion(bf16[6144,1536]{1,0:T(8,128)(2,1)} %bitcast.308, s32[4096]{0:T(1024)S(1)} %copy-done.55), kind=kCustom, calls=%fused_computation.3 | custom fusion | bytes 25182208 | tf_op jit(solution)/shard_map/gather | solution.py:229
  2195.1 21.1 reshape.299
  2216.2 34.2 %fusion.120 = (bf16[1024,1,1536]{2,1,0:T(2,128)(2,1)}, bf16[1024,1,1536]{2,1,0:T(2,128)(2,1)}, bf16[1024,1,1536]{2,1,0:T(2,128)(2,1)}, bf16[1024,1,1536]{2,1,0:T(2,128)(2,1)}) fusion(bf16[1024,4,1536]{2,1,0:T(4,128)(2,1)} %reshape.299), kind=kLoop, calls=%fused_computation.220 | loop fusion | bytes 25165824 | tf_op jit(solution)/shard_map/slice | solution.py:234
  2250.4 13.1 add_bitcast_fusion
  2265.7 15.8 fusion.57
  2281.5 101.2 %all-reduce.12.cloned.1.call-done = f32[1024,1536]{1,0:T(8,128)} async-done(((f32[1024,1536]{1,0:T(8,128)}), f32[1024,1536]{1,0:T(8,128)}) %all-reduce.12.cloned.1.call-update) | async-done | bytes 6291472 | tf_op jit(solution)/shard_map/psum | solution.py:235
  2382.8 6.6 multiply_reduce_fusion
  2400.1 25.5 while.27
  2432.4 5.8 fusion.127
  2454.6 12.2 convolution_bitcast_fusion.3
  2470.1 5.8 fusion.71
  2475.9 10.0 convolution_bitcast_fusion.1
  2485.9 9.6 convolution_bitcast_fusion.2
  2495.5 172.6 %all-reduce.18.cloned.1.call-done = (f32[1024,1536]{1,0:T(8,128)}, f32[1024,1536]{1,0:T(8,128)}) async-done(((f32[1024,1536]{1,0:T(8,128)}, f32[1024,1536]{1,0:T(8,128)}), (f32[1024,1536]{1,0:T(8,128)}, f32[1024,1536]{1,0:T(8,128)})) %all-reduce.18.cloned.1.call-update) | async-done | bytes 12582928 | tf_op jit(solution)/shard_map/psum | solution.py:195
  2668.1 4.7 fusion.68
  2672.8 40.5 %all-reduce = (f32[1536]{0:T(1024)}, f32[1536]{0:T(1024)}, f32[1536,8]{0,1:T(8,128)}) all-reduce(f32[1536]{0:T(1024)S(1)} %broadcast_multiply_fusion.4, f32[1536]{0:T(1024)S(1)} %broadcast_multiply_fusion.3, f32[1536,8]{0,1:T(8,128)S(1)} %copy-done.45), channel_id=1, replica_groups=mesh['expert'=8,'tensor'=4] {'expert','tensor'}, use_global_device_ids=true, to_apply=%region_31.32 | all-reduce | flops 15360 | bytes 122880 | tf_op jit(solution)/shard_map/psum | solution.py:311
  2713.3 13.0 fusion.67
  2726.3 85.1 %all-reduce.14.cloned.1.call-done = (f32[1536,256]{1,0:T(8,128)}, f32[1536,256]{1,0:T(8,128)}) async-done(((f32[1536,256]{1,0:T(8,128)}, f32[1536,256]{1,0:T(8,128)}), (f32[1536,256]{1,0:T(8,128)}, f32[1536,256]{1,0:T(8,128)})) %all-reduce.14.cloned.1.call-update) | async-done | bytes 3145744 | tf_op jit(solution)/shard_map/psum | solution.py:311
  2811.4 174.9 %all-reduce.16.cloned.1.call-done = (f32[1536,384]{1,0:T(8,128)}, f32[384,1536]{1,0:T(8,128)}) async-done(((f32[1536,384]{1,0:T(8,128)}, f32[384,1536]{1,0:T(8,128)}), (f32[1536,384]{1,0:T(8,128)}, f32[384,1536]{1,0:T(8,128)})) %all-reduce.16.cloned.1.call-update) | async-done | bytes 4718608 | tf_op jit(solution)/shard_map/psum | solution.py:310
  (302 shorter events, 136.7 us)
Async XLA Ops:
  7.2 49.3 %copy-start = (bf16[384,1536]{1,0:T(8,128)(2,1)S(1)}, bf16[384,1536]{1,0:T(8,128)(2,1)}, u32[]{:S(2)}) copy-start(bf16[384,1536]{1,0:T(8,128)(2,1)} %param.25) | copy-start | bytes 3538948
  7.2 5.7 copy-start.52
  7.2 175.4 %all-reduce.10.cloned.1.call-start = ((), (), s32[]{:S(2)}) async-start(), calls=%async_computation.4 | async-start | bytes 12582912 | tf_op jit(solution)/shard_map/psum | solution.py:129
  7.3 8.4 copy-start.72
  17.6 10.9 copy-start.22
  17.8 10.7 copy-start.23
  52.9 8.1 copy-start.5
  52.9 8.1 copy-start.7
  52.9 8.1 copy-start.16
  52.9 8.1 copy-start.58
  52.9 8.1 copy-start.73
  94.6 137.2 %copy-start.56 = (bf16[8,768]{1,0:T(8,128)(2,1)}, bf16[8,768]{1,0:T(8,128)(2,1)S(1)}, u32[]{:S(2)}) copy-start(bf16[8,768]{1,0:T(8,128)(2,1)S(1)} %mul.510) | copy-start | bytes 36868
  110.8 79.1 %copy-start.63 = (f32[1536]{0:T(1024)S(1)}, f32[1536]{0:T(1024)}, u32[]{:S(2)}) copy-start(f32[1536]{0:T(1024)} %param.21) | copy-start | bytes 18436
  242.1 412.6 %copy-start.43 = (bf16[1,1536,192]{1,2,0:T(8,128)(2,1)S(1)}, bf16[1,1536,192]{1,2,0:T(8,128)(2,1)}, u32[]{:S(2)}) copy-start(bf16[1,1536,192]{1,2,0:T(8,128)(2,1)} %param.27) | copy-start | bytes 1769476
  654.7 7.9 copy-start.13
  662.6 10.2 copy-start.41
  683.8 411.9 %all-to-all-start.1 = ((bf16[8,768,1536]{2,1,0:T(8,128)(2,1)}), bf16[8,768,1536]{2,1,0:T(8,128)(2,1)}, u32[]{:S(2)}, u32[]{:S(2)}) async-start(bf16[8,768,1536]{2,1,0:T(8,128)(2,1)} %bitcast.309), calls=%async_computation.1 | async-start | bytes 37748736 | tf_op jit(solution)/shard_map/all_to_all | solution.py:178
  689.7 1693.1 %all-reduce.12.cloned.1.call-start = ((), (), s32[]{:S(2)}) async-start(), calls=%async_computation.5 | async-start | bytes 12582912 | tf_op jit(solution)/shard_map/psum | solution.py:235
  702.6 29.3 copy-start.60
  731.8 397.9 %copy-start.54 = (s32[4096]{0:T(1024)}, s32[4096]{0:T(1024)S(1)}, u32[]{:S(2)}) copy-start(s32[4096]{0:T(1024)S(1)} %broadcast_clamp_fusion) | copy-start | bytes 49156
  1185.0 23.7 copy-start.51
  1210.2 13.9 copy-start.11
  1210.5 13.6 copy-start.62
  1224.1 43.6 %copy-start.57 = (bf16[8,768]{1,0:T(8,128)(2,1)S(1)}, bf16[8,768]{1,0:T(8,128)(2,1)}, u32[]{:S(2)}) copy-start(bf16[8,768]{1,0:T(8,128)(2,1)} %copy-done.56) | copy-start | bytes 36868
  1277.9 411.8 %copy-start.42 = (bf16[1,192,1536]{2,1,0:T(8,128)(2,1)S(1)}, bf16[1,192,1536]{2,1,0:T(8,128)(2,1)}, u32[]{:S(2)}) copy-start(bf16[1,192,1536]{2,1,0:T(8,128)(2,1)} %param.29) | copy-start | bytes 1769476
  1689.8 19.8 copy-start.44
  1709.5 14.8 copy-start.24
  1709.6 14.8 copy-start.26
  1745.5 415.6 %copy-start.55 = (s32[4096]{0:T(1024)S(1)}, s32[4096]{0:T(1024)}, u32[]{:S(2)}) copy-start(s32[4096]{0:T(1024)} %copy-done.54) | copy-start | bytes 49156
  2263.6 404.5 %all-reduce.18.cloned.1.call-start = ((), (), s32[]{:S(2)}) async-start(), calls=%async_computation.8 | async-start | bytes 25165824 | tf_op jit(solution)/shard_map/psum | solution.py:195
  2265.7 117.0 %copy-start.61 = (bf16[1536,8]{0,1:T(8,128)(2,1)S(1)}, bf16[1536,8]{0,1:T(8,128)(2,1)}, u32[]{:S(2)}) copy-start(bf16[1536,8]{0,1:T(8,128)(2,1)} %param.26) | copy-start | bytes 73732
  2265.7 117.0 %copy-start.64 = (f32[1536]{0:T(1024)S(1)}, f32[1536]{0:T(1024)}, u32[]{:S(2)}) copy-start(f32[1536]{0:T(1024)} %param.21) | copy-start | bytes 18436
  2265.7 117.0 %copy-start.67 = (f32[1024]{0:T(1024)S(1)}, f32[1024]{0:T(1024)}, u32[]{:S(2)}) copy-start(f32[1024]{0:T(1024)} %copy-done.66) | copy-start | bytes 12292
  2382.8 6.6 copy-start.10
  2431.5 6.7 copy-start.37
  2432.4 5.8 copy-start.34
  2438.3 8.4 copy-start.28
  2446.7 364.7 %all-reduce.14.cloned.1.call-start = ((), (), s32[]{:S(2)}) async-start(), calls=%async_computation.6 | async-start | bytes 6291456 | tf_op jit(solution)/shard_map/psum | solution.py:311
  2454.6 531.7 %all-reduce.16.cloned.1.call-start = ((), (), s32[]{:S(2)}) async-start(), calls=%async_computation.7 | async-start | bytes 9437184 | tf_op jit(solution)/shard_map/psum | solution.py:310
  2454.6 12.2 copy-start.4
  2470.1 5.8 copy-start.27
  2475.9 10.0 copy-start.25
  2485.9 9.6 copy-start.70
  2485.9 182.2 %copy-start.65 = (f32[1536]{0:T(1024)S(1)}, f32[1536]{0:T(1024)}, u32[]{:S(2)}) copy-start(f32[1536]{0:T(1024)} %param.20) | copy-start | bytes 18436
  2485.9 182.2 %copy-start.69 = (f32[1024]{0:T(1024)S(1)}, f32[1024]{0:T(1024)}, u32[]{:S(2)}) copy-start(f32[1024]{0:T(1024)} %copy-done.68) | copy-start | bytes 12292
  2495.5 177.3 %copy-start.45 = (f32[1536,8]{0,1:T(8,128)S(1)}, f32[1536,8]{0,1:T(8,128)}, u32[]{:S(2)}) copy-start(f32[1536,8]{0,1:T(8,128)} %convolution_multiply_fusion.1) | copy-start | bytes 147460
  2811.4 180.9 %copy-start.31 = (f32[1536,256]{1,0:T(8,128)S(1)}, f32[1536,256]{1,0:T(8,128)}, u32[]{:S(2)}) copy-start(f32[1536,256]{1,0:T(8,128)} %get-tuple-element.465) | copy-start | bytes 4718596
  2986.3 7.2 copy-start.30
  (43 other events, 114.7 us)
Sparse Core Ops, SparseCore 0:
  61.1 121.4 all-reduce.9
  2263.7 118.9 all-reduce.11
  2446.8 221.2 all-reduce.17
  2674.2 137.1 all-reduce.13
  2815.9 170.3 all-reduce.15
where the time goes:
time: 3010 us; the launch traced here: 3000 us
  blocking collectives  1290 us (43%)
  waiting for transfers between devices  967 us (32%)
  local copies, waits for them, and re-layouts  396 us (13%)
  matrix products  187 us (6%)
  other arithmetic  139 us (5%)
    all_to_all x2, blocking collectives, deliver(): lax.all_to_all(buffer, 'expert', split_axis=0, concat_axis=0, tiled=True)  824 us
    all_to_all x1, blocking collectives, shards(): lax.all_to_all(row_grads.reshape(experts_all, capacity, model_width), 'ex...  416 us
    all_to_all x1, waiting for transfers between devices, shards(): lax.all_to_all(expert_part.reshape(experts_all, capacity, model_width), '...  361 us
    psum x1, waiting for transfers between devices, shards(): lax.psum((grad_query_local, grad_output_local), 'expert')  175 us
    psum x1, waiting for transfers between devices, shards(): moe_total, gate_grads = lax.psum((moe_part, gate_part), 'tensor')  173 us
    psum x1, waiting for transfers between devices, shards(): expert_grad_in = lax.psum(input_part, 'tensor')  101 us
    psum x1, waiting for transfers between devices, shards(): lax.psum((grad_key_full, grad_value_full, grad_first_local * is_lead, gra...  85.1 us
    psum x1, waiting for transfers between devices, shards(): attn_total = lax.psum(attn_part, 'tensor')  71.8 us
  transfers between devices with their start and end apart: 6, of which 6 were waited for; matrix products, arithmetic and copies ran while one was open for 6% of the time, Pallas kernels for 0%

commit v1 on v0

v1 whole, which is shorter than its diff:
```python
import jax
import jax.numpy as jnp
from jax import lax
from jax.sharding import PartitionSpec as P

HEADS = 12
KV = 2
HD = 128
EPSILON = 1e-06
ROPE_BASE = 10000.0
NEGATIVE = -1e30
F32 = jnp.float32
BF16 = jnp.bfloat16


def dot(left, right, left_dim, right_dim):
    return lax.dot_general(
        left, right, (((left_dim,), (right_dim,)), ((), ())), preferred_element_type=F32
    )


def rms_norm(values, gain):
    inverse = lax.rsqrt(jnp.mean(values * values, axis=-1, keepdims=True) + EPSILON)
    normed = values * inverse
    return normed * gain, normed, inverse


def norm_backward(upstream, normed, inverse, gain):
    scaled = upstream * gain
    through = inverse * (scaled - normed * jnp.mean(scaled * normed, axis=-1, keepdims=True))
    return through, jnp.sum(upstream * normed, axis=0)


def rotary_tables(length, head_size):
    half_size = head_size // 2
    positions = jnp.arange(length, dtype=F32)[:, None]
    frequency = ROPE_BASE ** (-jnp.arange(half_size, dtype=F32) * 2.0 / head_size)
    angles = positions * frequency[None, :]
    return jnp.cos(angles), jnp.sin(angles)


def rotate(values, cos_table, sin_table):
    half = values.shape[-1] // 2
    a, b = values[..., :half], values[..., half:]
    return jnp.concatenate([a * cos_table - b * sin_table, b * cos_table + a * sin_table], axis=-1)


def unrotate(values, cos_table, sin_table):
    half = values.shape[-1] // 2
    a, b = values[..., :half], values[..., half:]
    return jnp.concatenate([a * cos_table + b * sin_table, b * cos_table - a * sin_table], axis=-1)


def causal(scores):
    rows = lax.broadcasted_iota(jnp.int32, scores.shape[-2:], 0)
    cols = lax.broadcasted_iota(jnp.int32, scores.shape[-2:], 1)
    return jnp.where(cols <= rows, scores, NEGATIVE)


class Links:
    def __init__(self, experts, tensors):
        self.experts, self.tensors = experts, tensors
        self.line = experts // 2
        self.tensor = lax.axis_index("tensor")
        expert = lax.axis_index("expert")
        self.place, self.side = expert // 2, expert % 2

    def over_tensor(self, values, bit):
        return lax.ppermute(values, "tensor", [(i, i ^ bit) for i in range(self.tensors)])

    def over_pair(self, values):
        return lax.ppermute(values, "expert", [(i, i ^ 1) for i in range(self.experts)])

    def along(self, values, step, reach=1):
        places = [p for p in range(self.line) if 0 <= p + step * reach < self.line]
        pairs = [(2 * p + s, 2 * (p + step) + s) for p in places for s in range(2)]
        return lax.ppermute(values, "expert", pairs)

    def relative(self, values):
        rows = values.shape[0] // 4
        return jnp.concatenate(
            [lax.dynamic_slice_in_dim(values, (self.tensor ^ r) * rows, rows, 0) for r in range(4)], 0
        )

    def scatter_sum(self, pieces, sent_as=BF16):
        rows = pieces[0].shape[0]
        sent = jnp.concatenate([pieces[1], pieces[3]], 0).astype(sent_as)
        got = self.over_tensor(sent, 1)
        other = (pieces[2] + got[rows:].astype(F32)).astype(sent_as)
        mine = pieces[0] + got[:rows].astype(F32)
        return mine + self.over_tensor(other, 2).astype(F32)

    def gather(self, quarter):
        rows = quarter.shape[0]
        both = jnp.concatenate([quarter, self.over_tensor(quarter, 2)], 0)
        rest = self.over_tensor(both, 1)
        return jnp.concatenate([both[:rows], rest[:rows], both[rows:], rest[rows:]], 0)


def nearest_first(line):
    tables = []
    for place in range(line):
        offsets = [p - place for p in range(line) if p != place]
        tables.append(sorted(offsets, key=lambda o: (abs(o), -o)))
    return tables


def pick(place, options):
    chosen = options[0][0]
    for values, places in options[1:]:
        wanted = place == places[0]
        for p in places[1:]:
            wanted = jnp.logical_or(wanted, place == p)
        chosen = jnp.where(wanted, values, chosen)
    return chosen


def quarters(values):
    rows = values.shape[0] // 4
    return [values[r * rows : (r + 1) * rows] for r in range(4)]


def shards(
    experts,
    tensors,
    inputs,
    routes,
    cotangent,
    first_gain,
    second_gain,
    w_query,
    w_key,
    w_value,
    w_output,
    w_router,
    w_gate,
    w_up,
    w_down,
):
    links = Links(experts, tensors)
    line, place, side = links.line, links.place, links.side
    length, width = inputs.shape
    heads = w_query.shape[1] // HD
    hidden = w_gate.shape[2]
    group = HEADS // KV
    kv_head = links.tensor * heads // group
    scale = HD ** (-0.5)
    order = nearest_first(line)

    own_weights = jnp.concatenate([w_gate[0].T, w_up[0].T, w_down[0]], 0)
    short = line <= 4
    if short:
        arrived = {0: own_weights}
        for step in range(1, line):
            arrived[-step] = links.along(arrived[1 - step] if step > 1 else own_weights, 1)
            arrived[step] = links.along(arrived[step - 1] if step > 1 else own_weights, -1)
        weights = [own_weights]
        for slot in range(line - 1):
            takers = {}
            for p in range(line):
                takers.setdefault(order[p][slot], []).append(p)
            weights.append(pick(place, [(arrived[o], ps) for o, ps in takers.items()]))
    else:
        sides = [[2 * p + s for p in range(line)] for s in range(2)]
        weights = lax.all_gather(own_weights, "expert", axis_index_groups=sides)

    grad_rel = links.relative(cotangent)
    rows = length // 4
    half = links.over_pair(jnp.concatenate([grad_rel[:rows], grad_rel[2 * rows : 3 * rows]], 0))
    rest = links.over_tensor(half, 1)
    grad_pair = jnp.concatenate([half[:rows], rest[:rows], half[rows:], rest[rows:]], 0)
    routes_rel = links.relative(routes)
    routes_both = jnp.concatenate([routes_rel, links.over_pair(routes_rel)], 0)
    grad_both = jnp.concatenate([grad_rel, grad_pair], 0)

    cos_table, sin_table = rotary_tables(length, HD)
    residual = inputs.astype(F32)
    first_out, _, _ = rms_norm(residual, first_gain)
    attn_in = first_out.astype(BF16)
    key_weight = lax.dynamic_slice_in_dim(w_key, kv_head * HD, HD, 1)
    value_weight = lax.dynamic_slice_in_dim(w_value, kv_head * HD, HD, 1)
    query_rot = rotate(
        dot(attn_in, w_query, 1, 0).reshape(length, heads, HD), cos_table[:, None], sin_table[:, None]
    ).astype(BF16)
    key_rot = rotate(dot(attn_in, key_weight, 1, 0), cos_table, sin_table).astype(BF16)
    value_low = dot(attn_in, value_weight, 1, 0).astype(BF16)
    probs, contexts = [], []
    for head in range(heads):
        scores = causal(dot(query_rot[:, head], key_rot, 1, 1) * scale)
        peak = jnp.max(scores, axis=-1, keepdims=True)
        exponent = jnp.exp(scores - peak)
        prob = exponent / jnp.sum(exponent, axis=-1, keepdims=True)
        probs.append(prob)
        contexts.append(dot(prob.astype(BF16), value_low, 1, 0))
    context = jnp.concatenate(contexts, 1).astype(BF16)
    context_rel = links.relative(context)
    attn = links.scatter_sum([dot(piece, w_output, 1, 0) for piece in quarters(context_rel)])

    def own_quarter(values):
        return lax.dynamic_slice_in_dim(values, links.tensor * rows, rows, 0)

    after = own_quarter(inputs).astype(F32) + attn
    second_out, second_normed, second_inverse = rms_norm(after, second_gain)
    expert_in = second_out.astype(BF16)
    tokens_pair = links.over_pair(expert_in)
    tokens_own = links.gather(expert_in)
    tokens = jnp.concatenate([tokens_own, links.gather(tokens_pair)], 0)

    logits = dot(w_router, tokens, 0, 1)
    logit_exp = jnp.exp(logits - jnp.max(logits, axis=0, keepdims=True))
    router_probs = logit_exp / jnp.sum(logit_exp, axis=0, keepdims=True)
    names = jnp.arange(experts, dtype=jnp.int32)[:, None, None]
    named = jnp.any(routes_both.T[None] == names, axis=1).astype(F32)
    gates = router_probs * named

    def one_expert(weight, position):
        name = position * 2 + side
        gate = lax.dynamic_slice_in_dim(gates, name, 1, 0)
        gate_up, down = weight[: 2 * hidden], weight[2 * hidden :]
        pre = dot(gate_up, tokens, 1, 1)
        back = dot(down, grad_both, 1, 1)
        gate_pre, up_pre = pre[:hidden], pre[hidden:]
        sigmoid = jax.nn.sigmoid(gate_pre)
        activated = gate_pre * sigmoid
        hid = (activated * up_pre).astype(BF16).astype(F32)
        gate_row = jnp.sum(hid * back, axis=0, keepdims=True) * lax.dynamic_slice_in_dim(named, name, 1, 0)
        gated = (hid * gate).astype(BF16)
        grad_hidden = back * gate
        grad_pre = jnp.concatenate(
            [
                grad_hidden * up_pre * sigmoid * (1.0 + gate_pre * (1.0 - sigmoid)),
                grad_hidden * activated,
            ],
            0,
        ).astype(BF16)
        weight_grad = jnp.concatenate([dot(grad_pre, tokens, 1, 0), dot(gated, grad_both, 1, 0)], 0)
        return dot(gated, down, 0, 0), dot(grad_pre, gate_up, 0, 0), gate_row, weight_grad

    moe = jnp.zeros(tokens.shape, F32)
    grad_tokens = jnp.zeros(tokens.shape, F32)
    if short:
        gate_rows, weight_grads = [], []
        for slot in range(line):
            offsets = jnp.asarray([0 if slot == 0 else order[p][slot - 1] for p in range(line)], jnp.int32)
            moe_part, grad_part, gate_row, weight_grad = one_expert(weights[slot], place + offsets[place])
            moe, grad_tokens = moe + moe_part, grad_tokens + grad_part
            gate_rows.append(gate_row)
            weight_grads.append(weight_grad)
        gate_sums = jnp.concatenate(gate_rows, 0)
    else:

        def step(totals, weight_at):
            moe_part, grad_part, gate_row, weight_grad = one_expert(*weight_at)
            return (totals[0] + moe_part, totals[1] + grad_part), (gate_row[0], weight_grad.astype(BF16))

        (moe, grad_tokens), (gate_sums, weight_grads) = lax.scan(
            step, (moe, grad_tokens), (weights, jnp.arange(line, dtype=jnp.int32))
        )

    grad_pair_quarter = links.scatter_sum(quarters(grad_tokens[length:])).astype(BF16)
    grad_own_quarter = links.scatter_sum(quarters(grad_tokens[:length]))
    grad_expert_in = grad_own_quarter + links.over_pair(grad_pair_quarter).astype(F32)

    gate_sums = jnp.concatenate([gate_sums[:, :length], gate_sums[:, length:]], 0)
    gate_sums = links.scatter_sum([gate_sums[:, r * rows : (r + 1) * rows] for r in range(4)], F32)
    gate_own, gate_other = gate_sums[:line], links.over_pair(gate_sums[line:])
    slot_of = jnp.asarray(
        [
            [q if not short else 0 if q == p else 1 + order[p].index(q - p) for q in range(line)]
            for p in range(line)
        ],
        jnp.int32,
    )
    dprobs = []
    for q in range(line):
        slot = slot_of[place, q]
        mine = lax.dynamic_slice_in_dim(gate_own, slot, 1, 0)
        theirs = lax.dynamic_slice_in_dim(gate_other, slot, 1, 0)
        dprobs += [jnp.where(side == 0, mine, theirs), jnp.where(side == 0, theirs, mine)]
    dprobs = jnp.concatenate(dprobs, 0)
    quarter_probs = router_probs[:, :rows]
    dlogits = (
        quarter_probs * (dprobs - jnp.sum(quarter_probs * dprobs, axis=0, keepdims=True))
    ).astype(BF16)
    grad_expert_in = grad_expert_in + dot(dlogits, w_router, 0, 1)
    grad_router = dot(expert_in, dlogits, 0, 1)
    through_second, grad_second = norm_backward(
        grad_expert_in, second_normed, second_inverse, second_gain
    )
    grad_after = own_quarter(cotangent).astype(F32) + through_second
    grad_after_low = links.gather(grad_after.astype(BF16))

    moe_pair = links.scatter_sum(quarters(moe[length:])).astype(BF16)
    moe_own = links.scatter_sum(quarters(moe[:length]))
    layer_out = links.relative(
        links.gather((after + moe_own + links.over_pair(moe_pair).astype(F32)).astype(BF16))
    )

    def flow(step):
        got = None
        for reach in range(line - 1, 0, -1):
            takers = {}
            for p in range(line):
                if 0 <= p + step * reach < line:
                    takers.setdefault(1 + order[p].index(step * reach), []).append(p)
            total = pick(place, [(weight_grads[s], ps) for s, ps in takers.items()])
            if got is not None:
                total = total + got.astype(F32)
            got = links.along(total.astype(BF16), step, reach)
        return got.astype(F32)

    if short:
        expert_grads = weight_grads[0]
        if line > 1:
            expert_grads = expert_grads + flow(1) + flow(-1)
    else:
        expert_grads = lax.psum_scatter(
            weight_grads, "expert", scatter_dimension=0, axis_index_groups=sides
        ).astype(F32)

    grad_output = dot(context_rel, grad_after_low, 0, 0)
    grad_output = lax.psum(grad_output.astype(BF16), "expert").astype(F32)
    grad_context = links.relative(dot(grad_after_low, w_output, 1, 1).astype(BF16))
    grad_heads = grad_context.reshape(length, heads, HD)
    query_grads = []
    key_grad = jnp.zeros((length, HD), F32)
    value_grad = jnp.zeros((length, HD), F32)
    for head in range(heads):
        dprob = dot(grad_heads[:, head], value_low, 1, 1)
        delta = jnp.sum(probs[head] * dprob, axis=-1, keepdims=True)
        dscore = (probs[head] * (dprob - delta)).astype(BF16)
        query_grads.append(dot(dscore, key_rot, 1, 0) * scale)
        key_grad = key_grad + dot(dscore, query_rot[:, head], 0, 0) * scale
        value_grad = value_grad + dot(probs[head].astype(BF16), grad_heads[:, head], 0, 0)
    query_grad = jnp.concatenate(
        [unrotate(g, cos_table, sin_table).astype(BF16) for g in query_grads], 1
    )
    key_grad = unrotate(key_grad, cos_table, sin_table).astype(BF16)
    value_grad = value_grad.astype(BF16)
    attn_weights = jnp.concatenate([w_query, key_weight, value_weight], 1)
    attn_grads = jnp.concatenate([query_grad, key_grad, value_grad], 1)
    grad_attn_in = links.scatter_sum(
        [dot(piece, attn_weights, 1, 1) for piece in quarters(links.relative(attn_grads))]
    )
    attn_weight_grads = dot(attn_in, attn_grads, 0, 0)
    query_width = heads * HD
    kv_grads = attn_weight_grads[:, query_width:]
    kv_grads = kv_grads + links.over_tensor(kv_grads.astype(BF16), 1).astype(F32)
    kv_grads = kv_grads.astype(BF16)
    summed = lax.psum(
        jnp.concatenate([attn_weight_grads[:, :query_width].astype(BF16), kv_grads], 1), "expert"
    )
    grad_query = summed[:, :query_width].astype(F32)
    kv_mine = summed[:, query_width:]
    kv_theirs = links.over_tensor(kv_mine, 2)
    first_head = kv_head == 0
    kv_low = jnp.where(first_head, kv_mine, kv_theirs).astype(F32)
    kv_high = jnp.where(first_head, kv_theirs, kv_mine).astype(F32)
    grad_key = jnp.concatenate([kv_low[:, :HD], kv_high[:, :HD]], 1)
    grad_value = jnp.concatenate([kv_low[:, HD:], kv_high[:, HD:]], 1)

    quarter_in = own_quarter(inputs).astype(F32)
    _, first_normed, first_inverse = rms_norm(quarter_in, first_gain)
    through_first, grad_first = norm_backward(
        grad_attn_in, first_normed, first_inverse, first_gain
    )
    grad_inputs = links.relative(links.gather((grad_after + through_first).astype(BF16)))
    grad_first, grad_second, grad_router = lax.psum(
        (grad_first, grad_second, grad_router), ("expert", "tensor")
    )
    return (
        layer_out,
        grad_inputs,
        grad_first,
        grad_second,
        grad_query,
        grad_key,
        grad_value,
        grad_output,
        grad_router,
        expert_grads[:hidden].T[None],
        expert_grads[hidden : 2 * hidden].T[None],
        expert_grads[2 * hidden :][None],
    )


def solution(mesh):
    experts, tensors = mesh.shape["expert"], mesh.shape["tensor"]
    in_specs = (
        P("expert", None),
        P("expert", None),
        P("expert", None),
        P(),
        P(),
        P(None, "tensor"),
        P(),
        P(),
        P("tensor", None),
        P(),
        P("expert", None, "tensor"),
        P("expert", None, "tensor"),
        P("expert", "tensor", None),
    )
    out_specs = (
        P("expert", None),
        P("expert", None),
        P(),
        P(),
        P(None, "tensor"),
        P(),
        P(),
        P("tensor", None),
        P(),
        P("expert", None, "tensor"),
        P("expert", None, "tensor"),
        P("expert", "tensor", None),
    )

    def run(*arrays):
        return shards(experts, tensors, *arrays)

    return jax.shard_map(run, mesh=mesh, in_specs=in_specs, out_specs=out_specs, check_vma=False)
```

time: 3010 us -> 730 us (0.24)
  blocking collectives: 1290 us -> 49.2 us
  waiting for transfers between devices: 967 us -> 206 us
  local copies, waits for them, and re-layouts: 396 us -> 48 us
  starting transfers between devices: 6.1 us -> 69.6 us
  other arithmetic: 139 us -> 98.5 us
    all_to_all x3 -> x0, blocking collectives: 1240 us -> none  [the longest x2 824 us: deliver(): lax.all_to_all(buffer, 'expert', split_axis=0, concat_axis=0, tiled=True)]
    psum x5 -> x1, waiting for transfers between devices: 606 us -> 30.8 us  [shards(): lax.psum(jnp.concatenate([attn_weight_grads[:, :query_width].astype(BF16)...]
    all_to_all x1 -> x0, waiting for transfers between devices: 361 us -> none  [shards(): lax.all_to_all(expert_part.reshape(experts_all, capacity, model_width), '...]
    ppermute x0 -> x45, waiting for transfers between devices: none -> 175 us  [the longest x12 101 us: along(): return lax.ppermute(values, 'expert', pairs)]
    gather x4 -> x0, local copies, waits for them, and re-layouts: 151 us -> none  [the longest x1 43.6 us: shards(): choice_grads[slot_pair] * slot_filled[:, None]]
    ppermute x0 -> x45, starting transfers between devices: none -> 69.5 us  [the longest x27 32.5 us: over_tensor(): lax.ppermute(values, 'tensor', [(i, i ^ bit) for i in range(self.tensors)])]
    slice x6 -> x12, local copies, waits for them, and re-layouts: 71.3 us -> 11 us  [the longest x2 4.25 us: quarters(): return [values[r * rows:(r + 1) * rows] for r in range(4)]]
    scatter x2 -> x0, local copies, waits for them, and re-layouts: 44.1 us -> none  [the longest x1 28.6 us: shards(): slot_filled = jnp.zeros((experts_all * capacity,), jnp.bfloat16).at[slot_...]
  transfers between devices with their start and end apart: 6 -> 46, of which waited for: 6 -> 14; matrix products, arithmetic and copies ran while one was open for 6% -> 44% of each run, Pallas kernels for 0% -> 2%
where the time goes in v1:
time: 730 us; the launch traced here: 723 us
  matrix products  212 us (29%)
  waiting for transfers between devices  206 us (28%)
  other arithmetic  98.5 us (13%)
  starting transfers between devices  69.6 us (10%)
  blocking collectives  49.2 us (7%)
  local copies, waits for them, and re-layouts  48 us (7%)
  between operations  26.4 us (4%)
  Pallas kernels  13.4 us (2%)
    dot_general x56, matrix products, dot(): lax.dot_general(left, right, (((left_dim,), (right_dim,)), ((), ())), pre...  212 us
    ppermute x12, waiting for transfers between devices, along(): return lax.ppermute(values, 'expert', pairs)  101 us
    ppermute x27, waiting for transfers between devices, over_tensor(): lax.ppermute(values, 'tensor', [(i, i ^ bit) for i in range(self.tensors)])  49.5 us
    psum x1, blocking collectives, shards(): lax.psum((grad_first, grad_second, grad_router), ('expert', 'tensor'))  49.2 us
    ppermute x27, starting transfers between devices, over_tensor(): lax.ppermute(values, 'tensor', [(i, i ^ bit) for i in range(self.tensors)])  32.5 us
    ppermute x12, starting transfers between devices, along(): return lax.ppermute(values, 'expert', pairs)  32.2 us
    psum x1, waiting for transfers between devices, shards(): lax.psum(jnp.concatenate([attn_weight_grads[:, :query_width].astype(BF16)...  30.8 us
    ppermute x6, waiting for transfers between devices, over_pair(): lax.ppermute(values, 'expert', [(i, i ^ 1) for i in range(self.experts)])  25.2 us
  transfers between devices with their start and end apart: 46, of which 14 were waited for; matrix products, arithmetic and copies ran while one was open for 44% of the time, Pallas kernels for 2%

profile of v1, /device:TPU:1, one launch (start us, length us, event | category | flops | bytes accessed | tf_op | source)
XLA Modules:
  0.0 722.6 jit_solution(12002883315912294404)
XLA Ops:
  10.1 5.4 collective-permute-start.8
  37.4 4.5 online-softmax
  42.9 4.5 online-softmax.1
  48.5 4.5 online-softmax.2
  87.7 9.5 %collective-permute-done.7 = s32[1024,4]{0,1:T(4,128)} collective-permute-done((s32[1024,4]{0,1:T(4,128)S(1)}, s32[1024,4]{0,1:T(4,128)}, u32[]{:S(2)}, u32[]{:S(2)}) %collective-permute-start.7) | collective-permute-done | bytes 16416 | tf_op jit(solution)/shard_map/ppermute | solution.py:72
  108.0 4.1 collective-permute-start.10
  114.0 8.5 %collective-permute-done.2 = bf16[256,1536]{1,0:T(8,128)(2,1)S(1)} collective-permute-done((bf16[256,1536]{1,0:T(8,128)(2,1)S(1)}, bf16[256,1536]{1,0:T(8,128)(2,1)S(1)}, u32[]{:S(2)}, u32[]{:S(2)}) %collective-permute-start.2) | collective-permute-done | bytes 786464 | tf_op jit(solution)/shard_map/ppermute | solution.py:69
  128.7 21.0 %collective-permute-done.10 = bf16[576,1536]{1,0:T(8,128)(2,1)S(1)} collective-permute-done((bf16[576,1536]{1,0:T(8,128)(2,1)}, bf16[576,1536]{1,0:T(8,128)(2,1)S(1)}, u32[]{:S(2)}, u32[]{:S(2)}) %collective-permute-start.10) | collective-permute-done | bytes 1769504 | tf_op jit(solution)/shard_map/ppermute | solution.py:77
  149.7 4.1 collective-permute-start.12
  158.3 31.8 %collective-permute-done.12 = bf16[576,1536]{1,0:T(8,128)(2,1)S(1)} collective-permute-done((bf16[576,1536]{1,0:T(8,128)(2,1)S(1)}, bf16[576,1536]{1,0:T(8,128)(2,1)S(1)}, u32[]{:S(2)}, u32[]{:S(2)}) %collective-permute-start.12) | collective-permute-done | bytes 1769504 | tf_op jit(solution)/shard_map/ppermute | solution.py:77
  190.1 4.1 collective-permute-done.13
  205.8 5.5 multiply_convert_fusion.4
  211.3 5.0 fusion.91
  221.0 3.9 collective-permute-start.39
  232.5 6.3 multiply_convert_fusion.8
  238.8 4.0 fusion.80
  242.9 6.6 fusion.74
  252.1 6.4 multiply_convert_fusion.6
  258.6 6.9 multiply_convert_fusion.10
  269.0 6.5 fusion.82
  275.5 6.4 fusion.70
  282.0 21.6 %fusion.202 = (bf16[2048,1536]{1,0:T(8,128)(2,1)}, f32[2048,1536]{1,0:T(8,128)}) fusion(bf16[576,1536]{1,0:T(8,128)(2,1)S(1)} %get-tuple-element.119, bf16[192,2048]{1,0:T(8,128)(2,1)} %copy-done.62, bf16[192,2048]{1,0:T(8,128)(2,1)} %copy-done.61, f32[2048,1536]{1,0:T(8,128)} %fusion.70, f32[2048,1536]{1,0:T(8,128)} %fusion.82, f32[2048,1536]{1,0:T(8,128)} %fusion.74), kind=kOutput, calls=%fused_computation.409 | convolution fusion | flops 2431647744 | bytes 59375616 | tf_op jit(solution)/shard_map/dot_general | solution.py:17
  308.6 7.6 %fusion.100 = f32[2048,1536]{1,0:T(8,128)} fusion(bf16[192,2048]{1,0:T(8,128)(2,1)S(1)} %copy-done.58, f32[2048]{0:T(1024)S(1)} %bitcast.152, bf16[576,1536]{1,0:T(8,128)(2,1)} %copy-done.19), kind=kOutput, calls=%fused_computation.224 | convolution fusion | flops 1209139200 | bytes 13967360 | tf_op jit(solution)/shard_map/dot_general | solution.py:17
  316.2 7.5 %fusion.96 = f32[2048,1536]{1,0:T(8,128)} fusion(bf16[192,2048]{1,0:T(8,128)(2,1)S(1)} %copy-done.56, f32[2048]{0:T(1024)S(1)} %bitcast.149, bf16[576,1536]{1,0:T(8,128)(2,1)} %copy-done.18), kind=kOutput, calls=%fused_computation.222 | convolution fusion | flops 1209139200 | bytes 13967360 | tf_op jit(solution)/shard_map/dot_general | solution.py:17
  323.7 6.5 fusion.104
  330.2 20.5 %fusion.206 = (bf16[2048,1536]{1,0:T(8,128)(2,1)}, f32[2048,1536]{1,0:T(8,128)}) fusion(bf16[576,1536]{1,0:T(8,128)(2,1)S(1)} %get-tuple-element.119, bf16[192,2048]{1,0:T(8,128)(2,1)} %copy-done.60, f32[2048]{0:T(1024)} %bitcast.157, f32[2048,1536]{1,0:T(8,128)} %fusion.96, f32[2048,1536]{1,0:T(8,128)} %fusion.104, f32[2048,1536]{1,0:T(8,128)} %fusion.100), kind=kOutput, calls=%fused_computation.413 | convolution fusion | flops 1221722112 | bytes 58007552 | tf_op jit(solution)/shard_map/dot_general | solution.py:17
  353.0 7.1 fusion.79
  360.2 4.0 fusion.81
  364.2 3.7 fusion.38
  368.2 5.2 fusion.98
  376.6 10.7 %collective-permute-done.29 = f32[8,256]{1,0:T(8,128)S(1)} collective-permute-done((f32[8,256]{1,0:T(8,128)S(1)}, f32[8,256]{1,0:T(8,128)S(1)}, u32[]{:S(2)}, u32[]{:S(2)}) %collective-permute-start.29) | collective-permute-done | bytes 8224 | tf_op jit(solution)/shard_map/ppermute | solution.py:69
  393.8 15.6 %collective-permute-done.30 = f32[4,256]{1,0:T(4,128)S(1)} collective-permute-done((f32[4,256]{1,0:T(4,128)S(1)}, f32[4,256]{1,0:T(4,128)S(1)}, u32[]{:S(2)}, u32[]{:S(2)}) %collective-permute-start.30) | collective-permute-done | bytes 4128 | tf_op jit(solution)/shard_map/ppermute | solution.py:72
  413.0 3.7 multiply_reduce_fusion.3
  419.0 4.2 fusion.94
  423.3 4.5 fusion.45
  428.4 8.1 %collective-permute-done.31 = bf16[256,1536]{1,0:T(8,128)(2,1)S(1)} collective-permute-done((bf16[256,1536]{1,0:T(8,128)(2,1)S(1)}, bf16[256,1536]{1,0:T(8,128)(2,1)S(1)}, u32[]{:S(2)}, u32[]{:S(2)}) %collective-permute-start.31) | collective-permute-done | bytes 786464 | tf_op jit(solution)/shard_map/ppermute | solution.py:69
  438.9 5.2 fusion.102
  445.3 4.1 add_convert_fusion.3
  457.0 4.0 convolution_convert_fusion.5
  502.7 4.1 add_convert_fusion.2
  520.4 13.4 %collective-permute-done.34 = bf16[256,1536]{1,0:T(8,128)(2,1)} collective-permute-done((bf16[256,1536]{1,0:T(8,128)(2,1)}, bf16[256,1536]{1,0:T(8,128)(2,1)}, u32[]{:S(2)}, u32[]{:S(2)}) %collective-permute-start.34) | collective-permute-done | bytes 786464 | tf_op jit(solution)/shard_map/ppermute | solution.py:69
  533.8 4.2 fusion.33
  538.1 4.3 fusion.32
  543.6 19.6 %collective-permute-done.41 = bf16[576,1536]{1,0:T(8,128)(2,1)} collective-permute-done((bf16[576,1536]{1,0:T(8,128)(2,1)}, bf16[576,1536]{1,0:T(8,128)(2,1)}, u32[]{:S(2)}, u32[]{:S(2)}) %collective-permute-start.41) | collective-permute-done | bytes 1769504 | tf_op jit(solution)/shard_map/ppermute | solution.py:77
  563.3 24.0 %collective-permute-done.44 = bf16[576,1536]{1,0:T(8,128)(2,1)} collective-permute-done((bf16[576,1536]{1,0:T(8,128)(2,1)}, bf16[576,1536]{1,0:T(8,128)(2,1)}, u32[]{:S(2)}, u32[]{:S(2)}) %collective-permute-start.44) | collective-permute-done | bytes 1769504 | tf_op jit(solution)/shard_map/ppermute | solution.py:77
  593.4 49.2 %all-reduce = (f32[1536]{0:T(1024)}, f32[1536]{0:T(1024)}, f32[1536,8]{0,1:T(8,128)}) all-reduce(f32[1536]{0:T(1024)S(1)} %copy-done.133, f32[1536]{0:T(1024)S(1)} %copy-done.114, f32[1536,8]{0,1:T(8,128)S(1)} %copy-done.94), channel_id=1, replica_groups=mesh['expert'=8,'tensor'=4] {'expert','tensor'}, use_global_device_ids=true, to_apply=%region_23.24 | all-reduce | flops 15360 | bytes 122880 | tf_op jit(solution)/shard_map/psum | solution.py:368
  646.6 30.8 %all-reduce.4.cloned.1.call-done = (bf16[1536,640]{0,1:T(8,128)(2,1)}, bf16[384,1536]{1,0:T(8,128)(2,1)}) async-done(((bf16[1536,640]{0,1:T(8,128)(2,1)}, bf16[384,1536]{1,0:T(8,128)(2,1)}), (bf16[1536,640]{0,1:T(8,128)(2,1)}, bf16[384,1536]{1,0:T(8,128)(2,1)})) %all-reduce.4.cloned.1.call-update) | async-done | bytes 3145744 | tf_op jit(solution)/shard_map/psum | solution.py:350
  689.6 8.8 %collective-permute-done.38 = bf16[1536,256]{0,1:T(8,128)(2,1)} collective-permute-done((bf16[1536,256]{0,1:T(8,128)(2,1)}, bf16[1536,256]{0,1:T(8,128)(2,1)}, u32[]{:S(2)}, u32[]{:S(2)}) %collective-permute-start.38) | collective-permute-done | bytes 786464 | tf_op jit(solution)/shard_map/ppermute | solution.py:69
  (515 shorter events, 234.7 us)
Async XLA Ops:
  7.2 670.2 %all-reduce.4.cloned.1.call-start = ((), (), s32[]{:S(2)}) async-start(), calls=%async_computation | async-start | bytes 6291456 | tf_op jit(solution)/shard_map/psum | solution.py:350
  10.1 97.9 %collective-permute-start.8 = (bf16[576,1536]{1,0:T(8,128)(2,1)}, bf16[576,1536]{1,0:T(8,128)(2,1)}, u32[]{:S(2)}, u32[]{:S(2)}) collective-permute-start(bf16[576,1536]{1,0:T(8,128)(2,1)} %pad_maximum_fusion.10), channel_id=1, source_target_pairs={{0,8},{4,12},{8,16},{12,20},{16,24},{20,28},{1,9},{5,13},{9,17},{1... | collective-permute-start | bytes 5308424 | tf_op jit(solution)/shard_map/ppermute | solution.py:77
  15.4 96.7 %collective-permute-start.9 = (bf16[576,1536]{1,0:T(8,128)(2,1)}, bf16[576,1536]{1,0:T(8,128)(2,1)}, u32[]{:S(2)}, u32[]{:S(2)}) collective-permute-start(bf16[576,1536]{1,0:T(8,128)(2,1)} %pad_maximum_fusion.10), channel_id=1, source_target_pairs={{8,0},{12,4},{16,8},{20,12},{24,16},{28,20},{9,1},{13,5},{17,9},{2... | collective-permute-start | bytes 5308424 | tf_op jit(solution)/shard_map/ppermute | solution.py:77
  55.7 11.8 %collective-permute-start = (bf16[512,1536]{1,0:T(8,128)(2,1)S(1)}, bf16[512,1536]{1,0:T(8,128)(2,1)S(1)}, u32[]{:S(2)}, u32[]{:S(2)}) collective-permute-start(bf16[512,1536]{1,0:T(8,128)(2,1)S(1)} %pad_maximum_fusion.11), channel_id=1, source_target_pairs={{0,1},{1,0},{2,3},{3,2},{4,5},{5,4},{6,7},{7,6},{8,9},{9,8},{10,11... | collective-permute-start | bytes 4718600 | tf_op jit(solution)/shard_map/ppermute | solution.py:69
  61.6 36.9 %collective-permute-start.21 = (bf16[512,1536]{1,0:T(8,128)(2,1)}, bf16[512,1536]{1,0:T(8,128)(2,1)}, u32[]{:S(2)}, u32[]{:S(2)}) collective-permute-start(bf16[512,1536]{1,0:T(8,128)(2,1)} %pad_maximum_fusion.17), channel_id=1, source_target_pairs={{0,4},{4,0},{8,12},{12,8},{16,20},{20,16},{24,28},{28,24},{1,5},{5... | collective-permute-start | bytes 4718600 | tf_op jit(solution)/shard_map/ppermute | solution.py:72
  62.9 34.3 %collective-permute-start.7 = (s32[1024,4]{0,1:T(4,128)S(1)}, s32[1024,4]{0,1:T(4,128)}, u32[]{:S(2)}, u32[]{:S(2)}) collective-permute-start(s32[1024,4]{0,1:T(4,128)S(1)} %pad_add_fusion), channel_id=1, source_target_pairs={{0,4},{4,0},{8,12},{12,8},{16,20},{20,16},{24,28},{28,24},{1,5},{5... | collective-permute-start | bytes 49160 | tf_op jit(solution)/shard_map/ppermute | solution.py:72
  68.3 32.2 %collective-permute-start.1 = (bf16[256,1536]{1,0:T(8,128)(2,1)S(1)}, bf16[256,1536]{1,0:T(8,128)(2,1)}, u32[]{:S(2)}, u32[]{:S(2)}) collective-permute-start(bf16[256,1536]{1,0:T(8,128)(2,1)S(1)} %add_convert_fusion.6), channel_id=1, source_target_pairs={{0,2},{1,3},{2,0},{3,1},{4,6},{5,7},{6,4},{7,5},{8,10},{9,11},{10,... | collective-permute-start | bytes 2359304 | tf_op jit(solution)/shard_map/ppermute | solution.py:69
  98.6 26.1 %collective-permute-start.22 = (bf16[512,1536]{1,0:T(8,128)(2,1)}, bf16[512,1536]{1,0:T(8,128)(2,1)S(1)}, u32[]{:S(2)}, u32[]{:S(2)}) collective-permute-start(bf16[512,1536]{1,0:T(8,128)(2,1)} %collective-permute-done.21), channel_id=1, source_target_pairs={{0,1},{1,0},{2,3},{3,2},{4,5},{5,4},{6,7},{7,6},{8,9},{9,8},{10,11... | collective-permute-start | bytes 4718600 | tf_op jit(solution)/shard_map/ppermute | solution.py:69
  103.3 19.2 %collective-permute-start.2 = (bf16[256,1536]{1,0:T(8,128)(2,1)S(1)}, bf16[256,1536]{1,0:T(8,128)(2,1)S(1)}, u32[]{:S(2)}, u32[]{:S(2)}) collective-permute-start(bf16[256,1536]{1,0:T(8,128)(2,1)S(1)} %get-tuple-element.81), channel_id=1, source_target_pairs={{0,2},{1,3},{2,0},{3,1},{4,6},{5,7},{6,4},{7,5},{8,10},{9,11},{10,... | collective-permute-start | bytes 2359304 | tf_op jit(solution)/shard_map/ppermute | solution.py:69
  104.6 18.9 %collective-permute-start.4 = (bf16[256,1536]{1,0:T(8,128)(2,1)S(1)}, bf16[256,1536]{1,0:T(8,128)(2,1)S(1)}, u32[]{:S(2)}, u32[]{:S(2)}) collective-permute-start(bf16[256,1536]{1,0:T(8,128)(2,1)S(1)} %get-tuple-element.81), channel_id=1, source_target_pairs={{0,4},{4,0},{8,12},{12,8},{16,20},{20,16},{24,28},{28,24},{1,5},{5... | collective-permute-start | bytes 2359304 | tf_op jit(solution)/shard_map/ppermute | solution.py:72
  108.0 41.7 %collective-permute-start.10 = (bf16[576,1536]{1,0:T(8,128)(2,1)}, bf16[576,1536]{1,0:T(8,128)(2,1)S(1)}, u32[]{:S(2)}, u32[]{:S(2)}) collective-permute-start(bf16[576,1536]{1,0:T(8,128)(2,1)} %collective-permute-done.8), channel_id=1, source_target_pairs={{0,8},{4,12},{8,16},{12,20},{16,24},{20,28},{1,9},{5,13},{9,17},{1... | collective-permute-start | bytes 5308424 | tf_op jit(solution)/shard_map/ppermute | solution.py:77
  112.1 41.7 %collective-permute-start.11 = (bf16[576,1536]{1,0:T(8,128)(2,1)}, bf16[576,1536]{1,0:T(8,128)(2,1)S(1)}, u32[]{:S(2)}, u32[]{:S(2)}) collective-permute-start(bf16[576,1536]{1,0:T(8,128)(2,1)} %collective-permute-done.9), channel_id=1, source_target_pairs={{8,0},{12,4},{16,8},{20,12},{24,16},{28,20},{9,1},{13,5},{17,9},{2... | collective-permute-start | bytes 5308424 | tf_op jit(solution)/shard_map/ppermute | solution.py:77
  122.6 35.4 %collective-permute-start.3 = (bf16[512,1536]{1,0:T(8,128)(2,1)S(1)}, bf16[512,1536]{1,0:T(8,128)(2,1)S(1)}, u32[]{:S(2)}, u32[]{:S(2)}) collective-permute-start(bf16[512,1536]{1,0:T(8,128)(2,1)S(1)} %pad_maximum_fusion.12), channel_id=1, source_target_pairs={{0,1},{1,0},{2,3},{3,2},{4,5},{5,4},{6,7},{7,6},{8,9},{9,8},{10,11... | collective-permute-start | bytes 4718600 | tf_op jit(solution)/shard_map/ppermute | solution.py:69
  123.5 31.5 %collective-permute-start.5 = (bf16[256,1536]{1,0:T(8,128)(2,1)S(1)}, bf16[256,1536]{1,0:T(8,128)(2,1)S(1)}, u32[]{:S(2)}, u32[]{:S(2)}) collective-permute-start(bf16[256,1536]{1,0:T(8,128)(2,1)S(1)} %collective-permute-done.4), channel_id=1, source_target_pairs={{0,2},{1,3},{2,0},{3,1},{4,6},{5,7},{6,4},{7,5},{8,10},{9,11},{10,... | collective-permute-start | bytes 2359304 | tf_op jit(solution)/shard_map/ppermute | solution.py:69
  149.7 40.4 %collective-permute-start.12 = (bf16[576,1536]{1,0:T(8,128)(2,1)S(1)}, bf16[576,1536]{1,0:T(8,128)(2,1)S(1)}, u32[]{:S(2)}, u32[]{:S(2)}) collective-permute-start(bf16[576,1536]{1,0:T(8,128)(2,1)S(1)} %collective-permute-done.10), channel_id=1, source_target_pairs={{0,8},{4,12},{8,16},{12,20},{16,24},{20,28},{1,9},{5,13},{9,17},{1... | collective-permute-start | bytes 5308424 | tf_op jit(solution)/shard_map/ppermute | solution.py:77
  153.8 40.4 %collective-permute-start.13 = (bf16[576,1536]{1,0:T(8,128)(2,1)S(1)}, bf16[576,1536]{1,0:T(8,128)(2,1)}, u32[]{:S(2)}, u32[]{:S(2)}) collective-permute-start(bf16[576,1536]{1,0:T(8,128)(2,1)S(1)} %collective-permute-done.11), channel_id=1, source_target_pairs={{8,0},{12,4},{16,8},{20,12},{24,16},{28,20},{9,1},{13,5},{17,9},{2... | collective-permute-start | bytes 5308424 | tf_op jit(solution)/shard_map/ppermute | solution.py:77
  156.3 41.1 %collective-permute-start.6 = (bf16[512,1536]{1,0:T(8,128)(2,1)}, bf16[512,1536]{1,0:T(8,128)(2,1)}, u32[]{:S(2)}, u32[]{:S(2)}) collective-permute-start(bf16[512,1536]{1,0:T(8,128)(2,1)} %pad_maximum_fusion.13), channel_id=1, source_target_pairs={{0,1},{1,0},{2,3},{3,2},{4,5},{5,4},{6,7},{7,6},{8,9},{9,8},{10,11... | collective-permute-start | bytes 4718600 | tf_op jit(solution)/shard_map/ppermute | solution.py:69
  197.4 78.1 %copy-start.18 = (bf16[576,1536]{1,0:T(8,128)(2,1)}, bf16[576,1536]{1,0:T(8,128)(2,1)S(1)}, u32[]{:S(2)}) copy-start(bf16[576,1536]{1,0:T(8,128)(2,1)S(1)} %get-tuple-element.120) | copy-start | bytes 5308420
  205.8 52.7 %copy-start.100 = (f32[1,2048]{1,0:T(1,128)}, f32[1,2048]{1,0:T(1,128)S(1)}, u32[]{:S(2)}) copy-start(f32[1,2048]{1,0:T(1,128)S(1)} %get-tuple-element.164) | copy-start | bytes 24580
  221.0 224.3 %collective-permute-start.39 = (bf16[576,1536]{1,0:T(8,128)(2,1)}, bf16[576,1536]{1,0:T(8,128)(2,1)}, u32[]{:S(2)}, u32[]{:S(2)}) collective-permute-start(bf16[576,1536]{1,0:T(8,128)(2,1)} %fusion.10), channel_id=1, source_target_pairs={{0,8},{4,12},{1,9},{5,13},{2,10},{6,14},{3,11},{7,15}} | collective-permute-start | bytes 5308424 | tf_op jit(solution)/shard_map/ppermute | solution.py:77
  224.9 220.4 %collective-permute-start.42 = (bf16[576,1536]{1,0:T(8,128)(2,1)}, bf16[576,1536]{1,0:T(8,128)(2,1)}, u32[]{:S(2)}, u32[]{:S(2)}) collective-permute-start(bf16[576,1536]{1,0:T(8,128)(2,1)} %fusion.10), channel_id=1, source_target_pairs={{24,16},{28,20},{25,17},{29,21},{26,18},{30,22},{27,19},{31,23}} | collective-permute-start | bytes 5308424 | tf_op jit(solution)/shard_map/ppermute | solution.py:77
  266.4 107.1 %collective-permute-start.28 = (f32[16,256]{1,0:T(8,128)}, f32[16,256]{1,0:T(8,128)}, u32[]{:S(2)}, u32[]{:S(2)}) collective-permute-start(f32[16,256]{1,0:T(8,128)} %pad_maximum_fusion.47), channel_id=1, source_target_pairs={{0,1},{1,0},{2,3},{3,2},{4,5},{5,4},{6,7},{7,6},{8,9},{9,8},{10,11... | collective-permute-start | bytes 49160 | tf_op jit(solution)/shard_map/ppermute | solution.py:69
  306.9 57.3 %collective-permute-start.25 = (bf16[512,1536]{1,0:T(8,128)(2,1)}, bf16[512,1536]{1,0:T(8,128)(2,1)}, u32[]{:S(2)}, u32[]{:S(2)}) collective-permute-start(bf16[512,1536]{1,0:T(8,128)(2,1)} %pad_maximum_fusion.23), channel_id=1, source_target_pairs={{0,1},{1,0},{2,3},{3,2},{4,5},{5,4},{6,7},{7,6},{8,9},{9,8},{10,11... | collective-permute-start | bytes 4718600 | tf_op jit(solution)/shard_map/ppermute | solution.py:69
  308.1 56.1 %collective-permute-start.23 = (bf16[512,1536]{1,0:T(8,128)(2,1)}, bf16[512,1536]{1,0:T(8,128)(2,1)}, u32[]{:S(2)}, u32[]{:S(2)}) collective-permute-start(bf16[512,1536]{1,0:T(8,128)(2,1)} %pad_maximum_fusion.22), channel_id=1, source_target_pairs={{0,1},{1,0},{2,3},{3,2},{4,5},{5,4},{6,7},{7,6},{8,9},{9,8},{10,11... | collective-permute-start | bytes 4718600 | tf_op jit(solution)/shard_map/ppermute | solution.py:69
  368.0 20.3 %collective-permute-start.26 = (bf16[256,1536]{1,0:T(8,128)(2,1)S(1)}, bf16[256,1536]{1,0:T(8,128)(2,1)S(1)}, u32[]{:S(2)}, u32[]{:S(2)}) collective-permute-start(bf16[256,1536]{1,0:T(8,128)(2,1)S(1)} %get-tuple-element.85), channel_id=1, source_target_pairs={{0,2},{1,3},{2,0},{3,1},{4,6},{5,7},{6,4},{7,5},{8,10},{9,11},{10,... | collective-permute-start | bytes 2359304 | tf_op jit(solution)/shard_map/ppermute | solution.py:69
  374.1 13.2 %collective-permute-start.29 = (f32[8,256]{1,0:T(8,128)S(1)}, f32[8,256]{1,0:T(8,128)S(1)}, u32[]{:S(2)}, u32[]{:S(2)}) collective-permute-start(f32[8,256]{1,0:T(8,128)S(1)} %slice_add_fusion.8), channel_id=1, source_target_pairs={{0,2},{1,3},{2,0},{3,1},{4,6},{5,7},{6,4},{7,5},{8,10},{9,11},{10,... | collective-permute-start | bytes 24584 | tf_op jit(solution)/shard_map/ppermute | solution.py:69
  388.0 24.9 %collective-permute-start.24 = (bf16[256,1536]{1,0:T(8,128)(2,1)}, bf16[256,1536]{1,0:T(8,128)(2,1)}, u32[]{:S(2)}, u32[]{:S(2)}) collective-permute-start(bf16[256,1536]{1,0:T(8,128)(2,1)} %get-tuple-element.84), channel_id=1, source_target_pairs={{0,2},{1,3},{2,0},{3,1},{4,6},{5,7},{6,4},{7,5},{8,10},{9,11},{10,... | collective-permute-start | bytes 2359304 | tf_op jit(solution)/shard_map/ppermute | solution.py:69
  391.1 21.9 %collective-permute-start.27 = (bf16[256,1536]{1,0:T(8,128)(2,1)}, bf16[256,1536]{1,0:T(8,128)(2,1)}, u32[]{:S(2)}, u32[]{:S(2)}) collective-permute-start(bf16[256,1536]{1,0:T(8,128)(2,1)} %fusion.37), channel_id=1, source_target_pairs={{0,4},{4,0},{8,12},{12,8},{16,20},{20,16},{24,28},{28,24},{1,5},{5... | collective-permute-start | bytes 2359304 | tf_op jit(solution)/shard_map/ppermute | solution.py:72
  391.3 18.1 %collective-permute-start.30 = (f32[4,256]{1,0:T(4,128)S(1)}, f32[4,256]{1,0:T(4,128)S(1)}, u32[]{:S(2)}, u32[]{:S(2)}) collective-permute-start(f32[4,256]{1,0:T(4,128)S(1)} %get-tuple-element.177), channel_id=1, source_target_pairs={{0,4},{4,0},{8,12},{12,8},{16,20},{20,16},{24,28},{28,24},{1,5},{5... | collective-permute-start | bytes 12296 | tf_op jit(solution)/shard_map/ppermute | solution.py:72
  409.4 13.8 %collective-permute-start.16 = (bf16[512,1536]{1,0:T(8,128)(2,1)}, bf16[512,1536]{1,0:T(8,128)(2,1)}, u32[]{:S(2)}, u32[]{:S(2)}) collective-permute-start(bf16[512,1536]{1,0:T(8,128)(2,1)} %pad_maximum_fusion.15), channel_id=1, source_target_pairs={{0,1},{1,0},{2,3},{3,2},{4,5},{5,4},{6,7},{7,6},{8,9},{9,8},{10,11... | collective-permute-start | bytes 4718600 | tf_op jit(solution)/shard_map/ppermute | solution.py:69
  412.9 10.4 %collective-permute-start.14 = (bf16[512,1536]{1,0:T(8,128)(2,1)}, bf16[512,1536]{1,0:T(8,128)(2,1)S(1)}, u32[]{:S(2)}, u32[]{:S(2)}) collective-permute-start(bf16[512,1536]{1,0:T(8,128)(2,1)} %pad_maximum_fusion.14), channel_id=1, source_target_pairs={{0,1},{1,0},{2,3},{3,2},{4,5},{5,4},{6,7},{7,6},{8,9},{9,8},{10,11... | collective-permute-start | bytes 4718600 | tf_op jit(solution)/shard_map/ppermute | solution.py:69
  417.8 18.7 %collective-permute-start.31 = (bf16[256,1536]{1,0:T(8,128)(2,1)S(1)}, bf16[256,1536]{1,0:T(8,128)(2,1)S(1)}, u32[]{:S(2)}, u32[]{:S(2)}) collective-permute-start(bf16[256,1536]{1,0:T(8,128)(2,1)S(1)} %fusion.179), channel_id=1, source_target_pairs={{0,2},{1,3},{2,0},{3,1},{4,6},{5,7},{6,4},{7,5},{8,10},{9,11},{10,... | collective-permute-start | bytes 2359304 | tf_op jit(solution)/shard_map/ppermute | solution.py:69
  427.8 26.0 %collective-permute-start.17 = (bf16[256,1536]{1,0:T(8,128)(2,1)S(1)}, bf16[256,1536]{1,0:T(8,128)(2,1)S(1)}, u32[]{:S(2)}, u32[]{:S(2)}) collective-permute-start(bf16[256,1536]{1,0:T(8,128)(2,1)S(1)} %get-tuple-element.87), channel_id=1, source_target_pairs={{0,2},{1,3},{2,0},{3,1},{4,6},{5,7},{6,4},{7,5},{8,10},{9,11},{10,... | collective-permute-start | bytes 2359304 | tf_op jit(solution)/shard_map/ppermute | solution.py:69
  436.7 20.2 %collective-permute-start.32 = (bf16[512,1536]{1,0:T(8,128)(2,1)S(1)}, bf16[512,1536]{1,0:T(8,128)(2,1)S(1)}, u32[]{:S(2)}, u32[]{:S(2)}) collective-permute-start(bf16[512,1536]{1,0:T(8,128)(2,1)S(1)} %pad_maximum_fusion.24), channel_id=1, source_target_pairs={{0,1},{1,0},{2,3},{3,2},{4,5},{5,4},{6,7},{7,6},{8,9},{9,8},{10,11... | collective-permute-start | bytes 4718600 | tf_op jit(solution)/shard_map/ppermute | solution.py:69
  444.0 93.9 %collective-permute-start.15 = (bf16[256,1536]{1,0:T(8,128)(2,1)}, bf16[256,1536]{1,0:T(8,128)(2,1)}, u32[]{:S(2)}, u32[]{:S(2)}) collective-permute-start(bf16[256,1536]{1,0:T(8,128)(2,1)} %get-tuple-element.86), channel_id=1, source_target_pairs={{0,2},{1,3},{2,0},{3,1},{4,6},{5,7},{6,4},{7,5},{8,10},{9,11},{10,... | collective-permute-start | bytes 2359304 | tf_op jit(solution)/shard_map/ppermute | solution.py:69
  449.4 51.5 %collective-permute-start.40 = (bf16[576,1536]{1,0:T(8,128)(2,1)}, bf16[576,1536]{1,0:T(8,128)(2,1)}, u32[]{:S(2)}, u32[]{:S(2)}) collective-permute-start(bf16[576,1536]{1,0:T(8,128)(2,1)} %get-tuple-element.88), channel_id=1, source_target_pairs={{0,8},{4,12},{8,16},{12,20},{1,9},{5,13},{9,17},{13,21},{2,10},{6,... | collective-permute-start | bytes 5308424 | tf_op jit(solution)/shard_map/ppermute | solution.py:77
  451.9 50.8 %collective-permute-start.43 = (bf16[576,1536]{1,0:T(8,128)(2,1)}, bf16[576,1536]{1,0:T(8,128)(2,1)}, u32[]{:S(2)}, u32[]{:S(2)}) collective-permute-start(bf16[576,1536]{1,0:T(8,128)(2,1)} %get-tuple-element.89), channel_id=1, source_target_pairs={{16,8},{20,12},{24,16},{28,20},{17,9},{21,13},{25,17},{29,21},{18,... | collective-permute-start | bytes 5308424 | tf_op jit(solution)/shard_map/ppermute | solution.py:77
  456.6 81.4 %collective-permute-start.18 = (bf16[256,1536]{1,0:T(8,128)(2,1)}, bf16[256,1536]{1,0:T(8,128)(2,1)}, u32[]{:S(2)}, u32[]{:S(2)}) collective-permute-start(bf16[256,1536]{1,0:T(8,128)(2,1)} %fusion.44), channel_id=1, source_target_pairs={{0,4},{4,0},{8,12},{12,8},{16,20},{20,16},{24,28},{28,24},{1,5},{5... | collective-permute-start | bytes 2359304 | tf_op jit(solution)/shard_map/ppermute | solution.py:72
  496.4 15.9 %collective-permute-start.33 = (bf16[512,1536]{1,0:T(8,128)(2,1)S(1)}, bf16[512,1536]{1,0:T(8,128)(2,1)S(1)}, u32[]{:S(2)}, u32[]{:S(2)}) collective-permute-start(bf16[512,1536]{1,0:T(8,128)(2,1)S(1)} %pad_maximum_fusion.25), channel_id=1, source_target_pairs={{0,1},{1,0},{2,3},{3,2},{4,5},{5,4},{6,7},{7,6},{8,9},{9,8},{10,11... | collective-permute-start | bytes 4718600 | tf_op jit(solution)/shard_map/ppermute | solution.py:69
  501.0 14.6 %collective-permute-start.37 = (bf16[1536,256]{0,1:T(8,128)(2,1)S(1)}, bf16[1536,256]{0,1:T(8,128)(2,1)S(1)}, u32[]{:S(2)}, u32[]{:S(2)}) collective-permute-start(bf16[1536,256]{0,1:T(8,128)(2,1)S(1)} %slice.765), channel_id=1, source_target_pairs={{0,1},{1,0},{2,3},{3,2},{4,5},{5,4},{6,7},{7,6},{8,9},{9,8},{10,11... | collective-permute-start | bytes 2359304 | tf_op jit(solution)/shard_map/ppermute | solution.py:69
  506.9 56.4 %collective-permute-start.41 = (bf16[576,1536]{1,0:T(8,128)(2,1)}, bf16[576,1536]{1,0:T(8,128)(2,1)}, u32[]{:S(2)}, u32[]{:S(2)}) collective-permute-start(bf16[576,1536]{1,0:T(8,128)(2,1)} %get-tuple-element.117), channel_id=1, source_target_pairs={{0,8},{4,12},{8,16},{12,20},{16,24},{20,28},{1,9},{5,13},{9,17},{1... | collective-permute-start | bytes 5308424 | tf_op jit(solution)/shard_map/ppermute | solution.py:77
  512.3 75.0 %collective-permute-start.44 = (bf16[576,1536]{1,0:T(8,128)(2,1)}, bf16[576,1536]{1,0:T(8,128)(2,1)}, u32[]{:S(2)}, u32[]{:S(2)}) collective-permute-start(bf16[576,1536]{1,0:T(8,128)(2,1)} %get-tuple-element.118), channel_id=1, source_target_pairs={{8,0},{12,4},{16,8},{20,12},{24,16},{28,20},{9,1},{13,5},{17,9},{2... | collective-permute-start | bytes 5308424 | tf_op jit(solution)/shard_map/ppermute | solution.py:77
  515.6 18.2 %collective-permute-start.34 = (bf16[256,1536]{1,0:T(8,128)(2,1)}, bf16[256,1536]{1,0:T(8,128)(2,1)}, u32[]{:S(2)}, u32[]{:S(2)}) collective-permute-start(bf16[256,1536]{1,0:T(8,128)(2,1)} %add_convert_fusion.5), channel_id=1, source_target_pairs={{0,2},{1,3},{2,0},{3,1},{4,6},{5,7},{6,4},{7,5},{8,10},{9,11},{10,... | collective-permute-start | bytes 2359304 | tf_op jit(solution)/shard_map/ppermute | solution.py:69
  542.4 100.2 %collective-permute-start.35 = (bf16[256,1536]{1,0:T(8,128)(2,1)}, bf16[256,1536]{1,0:T(8,128)(2,1)S(1)}, u32[]{:S(2)}, u32[]{:S(2)}) collective-permute-start(bf16[256,1536]{1,0:T(8,128)(2,1)} %get-tuple-element.141), channel_id=1, source_target_pairs={{0,2},{1,3},{2,0},{3,1},{4,6},{5,7},{6,4},{7,5},{8,10},{9,11},{10,... | collective-permute-start | bytes 2359304 | tf_op jit(solution)/shard_map/ppermute | solution.py:69
  590.2 90.6 %collective-permute-start.19 = (bf16[256,1536]{1,0:T(8,128)(2,1)}, bf16[256,1536]{1,0:T(8,128)(2,1)S(1)}, u32[]{:S(2)}, u32[]{:S(2)}) collective-permute-start(bf16[256,1536]{1,0:T(8,128)(2,1)} %get-tuple-element.142), channel_id=1, source_target_pairs={{0,2},{1,3},{2,0},{3,1},{4,6},{5,7},{6,4},{7,5},{8,10},{9,11},{10,... | collective-permute-start | bytes 2359304 | tf_op jit(solution)/shard_map/ppermute | solution.py:69
  645.2 60.4 %collective-permute-start.36 = (bf16[512,1536]{1,0:T(8,128)(2,1)}, bf16[512,1536]{1,0:T(8,128)(2,1)}, u32[]{:S(2)}, u32[]{:S(2)}) collective-permute-start(bf16[512,1536]{1,0:T(8,128)(2,1)} %pad_maximum_fusion.26), channel_id=1, source_target_pairs={{0,1},{1,0},{2,3},{3,2},{4,5},{5,4},{6,7},{7,6},{8,9},{9,8},{10,11... | collective-permute-start | bytes 4718600 | tf_op jit(solution)/shard_map/ppermute | solution.py:69
  679.6 18.7 %collective-permute-start.38 = (bf16[1536,256]{0,1:T(8,128)(2,1)}, bf16[1536,256]{0,1:T(8,128)(2,1)}, u32[]{:S(2)}, u32[]{:S(2)}) collective-permute-start(bf16[1536,256]{0,1:T(8,128)(2,1)} %slice.512), channel_id=1, source_target_pairs={{0,2},{1,3},{2,0},{3,1},{4,6},{5,7},{6,4},{7,5},{8,10},{9,11},{10,... | collective-permute-start | bytes 2359304 | tf_op jit(solution)/shard_map/ppermute | solution.py:69
  683.5 25.3 %collective-permute-start.20 = (bf16[512,1536]{1,0:T(8,128)(2,1)}, bf16[512,1536]{1,0:T(8,128)(2,1)}, u32[]{:S(2)}, u32[]{:S(2)}) collective-permute-start(bf16[512,1536]{1,0:T(8,128)(2,1)} %pad_maximum_fusion.16), channel_id=1, source_target_pairs={{0,1},{1,0},{2,3},{3,2},{4,5},{5,4},{6,7},{7,6},{8,9},{9,8},{10,11... | collective-permute-start | bytes 4718600 | tf_op jit(solution)/shard_map/ppermute | solution.py:69
  (139 other events, 1288.3 us)
Sparse Core Ops, SparseCore 0:
  518.6 158.8 all-reduce.3

commit v2 on v1

v2 whole, which is shorter than its diff:
```python
import functools

import jax
import jax.numpy as jnp
from jax import lax
from jax.experimental import pallas as pl
from jax.experimental.pallas import tpu as pltpu
from jax.sharding import PartitionSpec as P

HEADS = 12
KV = 2
HD = 128
EPSILON = 1e-06
ROPE_BASE = 10000.0
NEGATIVE = -1e30
F32 = jnp.float32
BF16 = jnp.bfloat16


def dot(left, right, left_dim, right_dim):
    return lax.dot_general(
        left, right, (((left_dim,), (right_dim,)), ((), ())), preferred_element_type=F32
    )


def rms_norm(values, gain):
    inverse = lax.rsqrt(jnp.mean(values * values, axis=-1, keepdims=True) + EPSILON)
    normed = values * inverse
    return normed * gain, normed, inverse


def norm_backward(upstream, normed, inverse, gain):
    scaled = upstream * gain
    through = inverse * (scaled - normed * jnp.mean(scaled * normed, axis=-1, keepdims=True))
    return through, jnp.sum(upstream * normed, axis=0)


def rotary_tables(length, head_size):
    half_size = head_size // 2
    positions = jnp.arange(length, dtype=F32)[:, None]
    frequency = ROPE_BASE ** (-jnp.arange(half_size, dtype=F32) * 2.0 / head_size)
    angles = positions * frequency[None, :]
    return jnp.cos(angles), jnp.sin(angles)


def rotate(values, cos_table, sin_table):
    half = values.shape[-1] // 2
    a, b = values[..., :half], values[..., half:]
    return jnp.concatenate([a * cos_table - b * sin_table, b * cos_table + a * sin_table], axis=-1)


def unrotate(values, cos_table, sin_table):
    half = values.shape[-1] // 2
    a, b = values[..., :half], values[..., half:]
    return jnp.concatenate([a * cos_table + b * sin_table, b * cos_table - a * sin_table], axis=-1)


def causal(scores):
    rows = lax.broadcasted_iota(jnp.int32, scores.shape[-2:], 0)
    cols = lax.broadcasted_iota(jnp.int32, scores.shape[-2:], 1)
    return jnp.where(cols <= rows, scores, NEGATIVE)


class Links:
    def __init__(self, experts, tensors):
        self.experts, self.tensors = experts, tensors
        self.line = experts // 2
        self.tensor = lax.axis_index("tensor")
        expert = lax.axis_index("expert")
        self.place, self.side = expert // 2, expert % 2

    def over_tensor(self, values, bit):
        return lax.ppermute(values, "tensor", [(i, i ^ bit) for i in range(self.tensors)])

    def over_expert(self, values, bit):
        return lax.ppermute(values, "expert", [(i, i ^ bit) for i in range(self.experts)])

    def over_pair(self, values):
        return self.over_expert(values, 1)

    def along(self, values, step, reach=1):
        places = [p for p in range(self.line) if 0 <= p + step * reach < self.line]
        pairs = [(2 * p + s, 2 * (p + step) + s) for p in places for s in range(2)]
        return lax.ppermute(values, "expert", pairs)

    def relative(self, values):
        rows = values.shape[0] // 4
        return jnp.concatenate(
            [
                lax.dynamic_slice_in_dim(values, (self.tensor ^ r) * rows, rows, 0)
                for r in (0, 2, 1, 3)
            ],
            0,
        )

    def absolute(self, values):
        rows = values.shape[0] // 4
        place = jnp.asarray([0, 2, 1, 3], jnp.int32)
        return jnp.concatenate(
            [
                lax.dynamic_slice_in_dim(values, place[self.tensor ^ q] * rows, rows, 0)
                for q in range(4)
            ],
            0,
        )

    def gather(self, quarter):
        both = jnp.concatenate([quarter, self.over_tensor(quarter, 2)], 0)
        return jnp.concatenate([both, self.over_tensor(both, 1)], 0)


def nearest_first(line):
    tables = []
    for place in range(line):
        offsets = [p - place for p in range(line) if p != place]
        tables.append(sorted(offsets, key=lambda o: (abs(o), -o)))
    return tables


def pick(place, options):
    chosen = options[0][0]
    for values, places in options[1:]:
        wanted = place == places[0]
        for p in places[1:]:
            wanted = jnp.logical_or(wanted, place == p)
        chosen = jnp.where(wanted, values, chosen)
    return chosen


def expert_kernel(count, hidden, split, prior, *refs):
    names, tokens, grads, gates = refs[:4]
    weights, refs = refs[4 : 4 + count], refs[4 + count :]
    if prior:
        before, refs = refs[0], refs[1:]
    outs, (gated_out, grad_pre_out, rows_out) = refs[: 2 if split else 1], refs[2 if split else 1 :]
    tile, grad_tile = tokens[...], grads[...]
    total = before[...].astype(F32) if prior else None
    for slot in range(count):
        weight = weights[slot]
        pre = dot(weight[: 2 * hidden, :], tile, 1, 1)
        back = dot(weight[2 * hidden :, :], grad_tile, 1, 1)
        gate = gates[pl.ds(names[slot], 1), :]
        gate_pre, up_pre = pre[:hidden], pre[hidden:]
        sigmoid = jax.nn.sigmoid(gate_pre)
        activated = gate_pre * sigmoid
        hid = (activated * up_pre).astype(BF16).astype(F32)
        rows_out[slot : slot + 1, :] = jnp.sum(hid * back, axis=0, keepdims=True)
        gated_out[slot * hidden : (slot + 1) * hidden, :] = (hid * gate).astype(BF16)
        grad_hidden = back * gate
        grad_pre = jnp.concatenate(
            [
                (grad_hidden * up_pre * (sigmoid * (1.0 + gate_pre * (1.0 - sigmoid)))).astype(BF16),
                (grad_hidden * activated).astype(BF16),
            ],
            0,
        )
        grad_pre_out[2 * slot * hidden : 2 * (slot + 1) * hidden, :] = grad_pre
        part = dot(grad_pre, weight[: 2 * hidden, :], 0, 0)
        total = part if total is None else total + part
    if split:
        for step in range(2):

            @pl.when(pl.program_id(0) == step)
            def _(step=step):
                outs[step][...] = total.astype(BF16)
    else:
        outs[0][...] = total.astype(BF16)


def expert_pass(tokens, grads, gates, names, weights, before=None, split=False):
    count, length, width = len(weights), tokens.shape[0], tokens.shape[1]
    hidden = weights[0].shape[0] // 3
    tile = length // 2
    token_spec = pl.BlockSpec((tile, width), lambda i, *_: (i, 0))
    half_spec = pl.BlockSpec((tile, width), lambda i, *_: (0, 0))

    def column_spec(rows):
        return pl.BlockSpec((rows, tile), lambda i, *_: (0, i))

    weight_spec = pl.BlockSpec((3 * hidden, width), lambda i, *_: (0, 0))
    token_shape = jax.ShapeDtypeStruct((length, width), BF16)
    half_shape = jax.ShapeDtypeStruct((tile, width), BF16)
    columns = [(count * hidden, BF16), (2 * count * hidden, BF16), (count, F32)]
    return pl.pallas_call(
        functools.partial(expert_kernel, count, hidden, split, before is not None),
        grid_spec=pltpu.PrefetchScalarGridSpec(
            num_scalar_prefetch=1,
            grid=(2,),
            in_specs=[token_spec, token_spec, column_spec(gates.shape[0])]
            + [weight_spec] * count
            + [token_spec] * (before is not None),
            out_specs=([half_spec] * 2 if split else [token_spec]) + [column_spec(r) for r, _ in columns],
        ),
        out_shape=([half_shape] * 2 if split else [token_shape])
        + [jax.ShapeDtypeStruct((r, length), t) for r, t in columns],
        compiler_params=pltpu.CompilerParams(vmem_limit_bytes=48 * 2**20),
        cost_estimate=pl.CostEstimate(
            flops=2 * count * length * width * hidden * 5,
            bytes_accessed=(4 * length + 3 * hidden * count) * width * 2,
            transcendentals=0,
        ),
    )(names, tokens, grads, gates, *weights, *([before] if before is not None else []))


def weight_grad_kernel(grad_pre_own, grad_pre_pair, gated_own, gated_pair, own, pair, grad_own, grad_pair, out):
    rows = grad_pre_own.shape[0]
    out[:rows, :] = (
        dot(grad_pre_own[...], own[...], 1, 0) + dot(grad_pre_pair[...], pair[...], 1, 0)
    ).astype(out.dtype)
    out[rows:, :] = (
        dot(gated_own[...], grad_own[...], 1, 0) + dot(gated_pair[...], grad_pair[...], 1, 0)
    ).astype(out.dtype)


def weight_grad(slot, hidden, grad_pre, gated, tokens, grads, kept_as):
    length, width = tokens[0].shape
    tile = width // 3
    pre_spec = pl.BlockSpec((2 * hidden, length), lambda i: (slot, 0))
    gated_spec = pl.BlockSpec((hidden, length), lambda i: (slot, 0))
    token_spec = pl.BlockSpec((length, tile), lambda i: (0, i))
    return pl.pallas_call(
        weight_grad_kernel,
        grid=(3,),
        in_specs=[pre_spec] * 2 + [gated_spec] * 2 + [token_spec] * 4,
        out_specs=pl.BlockSpec((3 * hidden, tile), lambda i: (0, i)),
        out_shape=jax.ShapeDtypeStruct((3 * hidden, width), kept_as),
        compiler_params=pltpu.CompilerParams(vmem_limit_bytes=32 * 2**20),
        cost_estimate=pl.CostEstimate(
            flops=2 * 2 * length * width * hidden * 3,
            bytes_accessed=(4 * length + 6 * hidden) * width * 2,
            transcendentals=0,
        ),
    )(*grad_pre, *gated, *tokens, *grads)


MESH = pl.DeviceIdType.MESH


class Copies:
    def __init__(self, tensors, send, recv):
        self.send, self.recv, self.started = send, recv, []
        expert, tensor = lax.axis_index("expert"), lax.axis_index("tensor")
        self.core = (expert, tensor + 1 - 2 * (tensor % 2))
        self.far = (expert, (tensor + tensors // 2) % tensors)
        self.mate = (expert + 1 - 2 * (expert % 2), tensor)

    def across(self, bit):
        expert, tensor = lax.axis_index("expert"), lax.axis_index("tensor")
        return (expert + bit - 2 * bit * (expert // bit % 2), tensor)

    def greet(self, partners):
        barrier = pltpu.get_barrier_semaphore()
        for partner in partners:
            pl.semaphore_signal(barrier, inc=1, device_id=partner, device_id_type=MESH)
        pl.semaphore_wait(barrier, len(partners))

    def start(self, source, target, device):
        place = len(self.started)
        copy = pltpu.make_async_remote_copy(
            src_ref=source,
            dst_ref=target,
            send_sem=self.send.at[place],
            recv_sem=self.recv.at[place],
            device_id=device,
            device_id_type=MESH,
        )
        copy.start()
        self.started.append(copy)
        return copy

    def finish(self):
        for copy in self.started:
            copy.wait_send()


def sum_quarter(copies, part, sent, got, crossing, crossed):
    rows = crossing.shape[0]
    sent[rows:, :] = part(3).astype(BF16)
    last = copies.start(sent.at[pl.ds(rows, rows)], got.at[pl.ds(rows, rows)], copies.core)
    sent[:rows, :] = part(2).astype(BF16)
    first = copies.start(sent.at[pl.ds(0, rows)], got.at[pl.ds(0, rows)], copies.core)
    other = part(1)
    last.wait_recv()
    crossing[...] = (other + got[rows:, :].astype(F32)).astype(BF16)
    far = copies.start(crossing, crossed, copies.far)
    mine = part(0)
    first.wait_recv()
    mine = mine + got[:rows, :].astype(F32)
    far.wait_recv()
    return mine + crossed[...].astype(F32)


def gather_quarters(copies, whole, rows, fill=None):
    far = copies.start(whole.at[pl.ds(0, rows)], whole.at[pl.ds(rows, rows)], copies.far)
    first = copies.start(whole.at[pl.ds(0, rows)], whole.at[pl.ds(2 * rows, rows)], copies.core)
    if fill is not None:
        fill()
    far.wait_recv()
    last = copies.start(whole.at[pl.ds(rows, rows)], whole.at[pl.ds(3 * rows, rows)], copies.core)
    first.wait_recv()
    last.wait_recv()


def attend_out_kernel(
    tensors, context, weight, stream, gain, own, pair, after, sent, got, crossing, crossed, send, recv
):
    copies = Copies(tensors, send, recv)
    copies.greet([copies.core, copies.far, copies.mate])
    rows = stream.shape[0]

    def part(place):
        return dot(context[place * rows : (place + 1) * rows, :], weight[...], 1, 0)

    total = stream[...].astype(F32) + sum_quarter(copies, part, sent, got, crossing, crossed)
    after[...] = total
    own[:rows, :] = rms_norm(total, gain[...])[0].astype(BF16)
    mate = copies.start(own.at[pl.ds(0, rows)], pair.at[pl.ds(0, rows)], copies.mate)
    gather_quarters(copies, own, rows)
    mate.wait_recv()
    gather_quarters(copies, pair, rows)
    copies.finish()


def vmem():
    return pl.BlockSpec(memory_space=pltpu.VMEM)


def attend_out(tensors, context, weight, stream, gain):
    rows, width = stream.shape
    return pl.pallas_call(
        functools.partial(attend_out_kernel, tensors),
        out_shape=[
            jax.ShapeDtypeStruct((4 * rows, width), BF16),
            jax.ShapeDtypeStruct((4 * rows, width), BF16),
            jax.ShapeDtypeStruct((rows, width), F32),
        ],
        in_specs=[vmem()] * 4,
        out_specs=[vmem()] * 3,
        scratch_shapes=[
            pltpu.VMEM((2 * rows, width), BF16),
            pltpu.VMEM((2 * rows, width), BF16),
            pltpu.VMEM((rows, width), BF16),
            pltpu.VMEM((rows, width), BF16),
            pltpu.SemaphoreType.DMA((10,)),
            pltpu.SemaphoreType.DMA((10,)),
        ],
        compiler_params=pltpu.CompilerParams(
            collective_id=1, has_side_effects=True, vmem_limit_bytes=40 * 2**20
        ),
        cost_estimate=pl.CostEstimate(flops=6 * 10**10, bytes_accessed=10**7, transcendentals=0),
    )(context, weight, stream, gain)


def tokens_back_kernel(
    tensors,
    kept_pair,
    sent_pair,
    kept_own,
    sent_own,
    rows_kept,
    rows_sent,
    names,
    probs,
    named,
    router,
    after,
    gain,
    grad,
    whole,
    grad_after,
    grad_router,
    grad_second,
    got_pair,
    got_own,
    crossing_pair,
    crossed_pair,
    crossing_own,
    crossed_own,
    mate_out,
    mate_in,
    rows_got,
    rows_crossing,
    rows_crossed,
    rows_mine,
    rows_mate,
    send,
    recv,
):
    copies = Copies(tensors, send, recv)
    copies.greet([copies.core, copies.far, copies.mate])
    rows = grad.shape[0]
    low, high = pl.ds(0, rows), pl.ds(rows, rows)
    pair_last = copies.start(sent_pair.at[high], got_pair.at[high], copies.core)
    pair_first = copies.start(sent_pair.at[low], got_pair.at[low], copies.core)
    rows_core = copies.start(rows_sent, rows_got, copies.core)
    own_last = copies.start(sent_own.at[high], got_own.at[high], copies.core)
    own_first = copies.start(sent_own.at[low], got_own.at[low], copies.core)
    pair_last.wait_recv()
    crossing_pair[...] = (kept_pair[rows:, :].astype(F32) + got_pair[rows:, :].astype(F32)).astype(BF16)
    pair_far = copies.start(crossing_pair, crossed_pair, copies.far)
    rows_core.wait_recv()
    rows_crossing[...] = rows_kept[:, rows:] + rows_got[:, rows:]
    rows_far = copies.start(rows_crossing, rows_crossed, copies.far)
    pair_first.wait_recv()
    mine_pair = kept_pair[:rows, :].astype(F32) + got_pair[:rows, :].astype(F32)
    own_last.wait_recv()
    crossing_own[...] = (kept_own[rows:, :].astype(F32) + got_own[rows:, :].astype(F32)).astype(BF16)
    own_first.wait_recv()
    grad_tokens = kept_own[:rows, :].astype(F32) + got_own[:rows, :].astype(F32)
    pair_far.wait_recv()
    own_far = copies.start(crossing_own, crossed_own, copies.far)
    mate_out[...] = (mine_pair + crossed_pair[...].astype(F32)).astype(BF16)
    mate = copies.start(mate_out, mate_in, copies.mate)
    rows_far.wait_recv()
    rows_mine[...] = rows_kept[:, :rows] + rows_got[:, :rows] + rows_crossed[...]
    rows_over = copies.start(rows_mine, rows_mate, copies.mate)
    rows_over.wait_recv()
    line = rows_mine.shape[0] // 2
    slots = jnp.concatenate([rows_mine[:line, :], rows_mate[line:, :]], 0)
    dprobs = jnp.zeros(probs.shape, F32)
    for slot in range(2 * line):
        dprobs = dprobs + names[:, slot : slot + 1] * slots[slot : slot + 1, :]
    dprobs = dprobs * named[...]
    dlogits = (
        probs[...] * (dprobs - jnp.sum(probs[...] * dprobs, axis=0, keepdims=True))
    ).astype(BF16)
    second_out, normed, inverse = rms_norm(after[...], gain[...])
    grad_router[...] = dot(dlogits, second_out.astype(BF16), 1, 0)
    grad_tokens = grad_tokens + dot(dlogits, router[...], 0, 0)
    own_far.wait_recv()
    grad_tokens = grad_tokens + crossed_own[...].astype(F32)
    mate.wait_recv()
    grad_tokens = grad_tokens + mate_in[...].astype(F32)
    through, second = norm_backward(grad_tokens, normed, inverse, gain[...])
    grad_second[...] = second[None]
    total = grad[...].astype(F32) + through
    grad_after[...] = total
    whole[:rows, :] = total.astype(BF16)
    gather_quarters(copies, whole, rows)
    copies.finish()


def tokens_back(tensors, experts, *operands):
    rows, width = operands[-1].shape
    half = pltpu.VMEM((2 * rows, width), BF16)
    quarter = pltpu.VMEM((rows, width), BF16)
    small = pltpu.VMEM((experts, rows), F32)
    return pl.pallas_call(
        functools.partial(tokens_back_kernel, tensors),
        out_shape=[
            jax.ShapeDtypeStruct((4 * rows, width), BF16),
            jax.ShapeDtypeStruct((rows, width), F32),
            jax.ShapeDtypeStruct((experts, width), F32),
            jax.ShapeDtypeStruct((1, width), F32),
        ],
        in_specs=[vmem()] * len(operands),
        out_specs=[vmem()] * 4,
        scratch_shapes=[half, half]
        + [quarter] * 6
        + [pltpu.VMEM((experts, 2 * rows), F32), small, small, small, small]
        + [pltpu.SemaphoreType.DMA((16,)), pltpu.SemaphoreType.DMA((16,))],
        compiler_params=pltpu.CompilerParams(
            collective_id=2, has_side_effects=True, vmem_limit_bytes=48 * 2**20
        ),
        cost_estimate=pl.CostEstimate(flops=6 * 10**10, bytes_accessed=10**7, transcendentals=0),
    )(*operands)


def inputs_back_kernel(
    tensors,
    experts,
    grads,
    weight,
    stream,
    gain,
    grad_after,
    early,
    whole,
    sums,
    sent,
    got,
    crossing,
    crossed,
    running,
    arrived,
    send,
    recv,
):
    copies = Copies(tensors, send, recv)
    bits = [1 << k for k in range(experts.bit_length() - 1)]
    copies.greet([copies.core, copies.far] + [copies.across(bit) for bit in bits])
    rows = stream.shape[0]

    def part(place):
        return dot(grads[place * rows : (place + 1) * rows, :], weight[...], 1, 1)

    grad_in = sum_quarter(copies, part, sent, got, crossing, crossed)
    _, normed, inverse = rms_norm(stream[...].astype(F32), gain[...])
    through, first = norm_backward(grad_in, normed, inverse, gain[...])
    whole[:rows, :] = (grad_after[...] + through).astype(BF16)

    def fill():
        running[0] = early[...]
        running[0, experts + 1 : experts + 2, :] = first[None]
        steps = [copies.core] + [copies.across(bit) for bit in bits] + [copies.far]
        for step, device in enumerate(steps):
            copy = copies.start(running.at[step], arrived.at[step], device)
            copy.wait_recv()
            if step + 1 < len(steps):
                running[step + 1] = running[step] + arrived[step]
            else:
                sums[...] = running[step] + arrived[step]

    gather_quarters(copies, whole, rows, fill)
    copies.finish()


def inputs_back(tensors, experts, *operands):
    rows, width = operands[2].shape
    early = operands[-1].shape
    steps = 1 + experts.bit_length()
    return pl.pallas_call(
        functools.partial(inputs_back_kernel, tensors, experts),
        out_shape=[
            jax.ShapeDtypeStruct((4 * rows, width), BF16),
            jax.ShapeDtypeStruct(early, F32),
        ],
        in_specs=[vmem()] * len(operands),
        out_specs=[vmem()] * 2,
        scratch_shapes=[
            pltpu.VMEM((2 * rows, width), BF16),
            pltpu.VMEM((2 * rows, width), BF16),
            pltpu.VMEM((rows, width), BF16),
            pltpu.VMEM((rows, width), BF16),
            pltpu.VMEM((steps,) + early, F32),
            pltpu.VMEM((steps,) + early, F32),
            pltpu.SemaphoreType.DMA((6 + steps,)),
            pltpu.SemaphoreType.DMA((6 + steps,)),
        ],
        compiler_params=pltpu.CompilerParams(
            collective_id=3, has_side_effects=True, vmem_limit_bytes=48 * 2**20
        ),
        cost_estimate=pl.CostEstimate(flops=5 * 10**10, bytes_accessed=10**7, transcendentals=0),
    )(*operands)


def shards(
    experts,
    tensors,
    inputs,
    routes,
    cotangent,
    first_gain,
    second_gain,
    w_query,
    w_key,
    w_value,
    w_output,
    w_router,
    w_gate,
    w_up,
    w_down,
):
    links = Links(experts, tensors)
    line, place, side = links.line, links.place, links.side
    length, width = inputs.shape
    heads = w_query.shape[1] // HD
    hidden = w_gate.shape[2]
    group = HEADS // KV
    kv_head = links.tensor * heads // group
    scale = HD ** (-0.5)
    order = nearest_first(line)

    own_weights = jnp.concatenate([w_gate[0].T, w_up[0].T, w_down[0]], 0)
    short = line <= 4
    if short:
        arrived = {0: own_weights}
        for step in range(1, line):
            arrived[-step] = links.along(arrived[1 - step] if step > 1 else own_weights, 1)
            arrived[step] = links.along(arrived[step - 1] if step > 1 else own_weights, -1)
        weights = [own_weights]
        for slot in range(line - 1):
            takers = {}
            for p in range(line):
                takers.setdefault(order[p][slot], []).append(p)
            weights.append(pick(place, [(arrived[o], ps) for o, ps in takers.items()]))
    else:
        sides = [[2 * p + s for p in range(line)] for s in range(2)]
        weights = lax.all_gather(own_weights, "expert", axis_index_groups=sides)

    grad_rel = links.relative(cotangent)
    rows, half = length // 4, length // 2
    grad_half = links.over_pair(grad_rel[:half])
    grad_pair = jnp.concatenate([grad_half, links.over_tensor(grad_half, 1)], 0)
    routes_own = links.relative(routes).T
    routes_pair = links.over_pair(routes_own)

    cos_table, sin_table = rotary_tables(length, HD)
    residual = inputs.astype(F32)
    first_out, _, _ = rms_norm(residual, first_gain)
    attn_in = first_out.astype(BF16)
    key_weight = lax.dynamic_slice_in_dim(w_key, kv_head * HD, HD, 1)
    value_weight = lax.dynamic_slice_in_dim(w_value, kv_head * HD, HD, 1)
    query_rot = rotate(
        dot(attn_in, w_query, 1, 0).reshape(length, heads, HD), cos_table[:, None], sin_table[:, None]
    ).astype(BF16)
    key_rot = rotate(dot(attn_in, key_weight, 1, 0), cos_table, sin_table).astype(BF16)
    value_low = dot(attn_in, value_weight, 1, 0).astype(BF16)
    probs, contexts = [], []
    for head in range(heads):
        scores = causal(dot(query_rot[:, head], key_rot, 1, 1) * scale)
        peak = jnp.max(scores, axis=-1, keepdims=True)
        exponent = jnp.exp(scores - peak)
        prob = exponent / jnp.sum(exponent, axis=-1, keepdims=True)
        probs.append(prob)
        contexts.append(dot(prob.astype(BF16), value_low, 1, 0))
    context = jnp.concatenate(contexts, 1).astype(BF16)
    context_rel = links.relative(context)
    def own_quarter(values):
        return lax.dynamic_slice_in_dim(values, links.tensor * rows, rows, 0)

    stream = own_quarter(inputs)
    if short:
        early = [arrived[o] for o in (-1, 1) if o in arrived]
        context_rel, *early = lax.optimization_barrier([context_rel] + early)
    tokens_own, tokens_pair, after = attend_out(
        tensors, context_rel, w_output, stream, second_gain[None]
    )
    names = jnp.arange(experts, dtype=jnp.int32)[:, None, None]

    def gates_of(tokens, tokens_routes):
        logits = dot(router_rows, tokens, 1, 1)
        logit_exp = jnp.exp(logits - jnp.max(logits, axis=0, keepdims=True))
        probs = logit_exp / jnp.sum(logit_exp, axis=0, keepdims=True)
        named = jnp.any(tokens_routes[None] == names, axis=1).astype(F32)
        return probs, named, probs * named

    router_rows = w_router.T
    router_probs, named, gates_own = gates_of(tokens_own, routes_own)
    _, _, gates_pair = gates_of(tokens_pair, routes_pair)

    both_tokens, both_grads = (tokens_own, tokens_pair), (grad_rel, grad_pair)
    if short:
        offsets = jnp.asarray([[0] + order[p] for p in range(line)], jnp.int32)[place]
        slot_names = (place + offsets) * 2 + side
        last = line - 1
        first_own = expert_pass(tokens_own, grad_rel, gates_own, slot_names[:last], weights[:last])
        first_pair = expert_pass(tokens_pair, grad_pair, gates_pair, slot_names[:last], weights[:last])
        kept_pair, sent_pair, *last_pair = expert_pass(
            tokens_pair, grad_pair, gates_pair, slot_names[last:], weights[last:], first_pair[0], True
        )
        kept_own, sent_own, *last_own = expert_pass(
            tokens_own, grad_rel, gates_own, slot_names[last:], weights[last:], first_own[0], True
        )
        gate_own = jnp.concatenate([first_own[3], last_own[2]], 0)
        gate_pair = jnp.concatenate([first_pair[3], last_pair[2]], 0)
        gated_own = jnp.concatenate([first_own[1], last_own[0]], 0)
        gated_pair = jnp.concatenate([first_pair[1], last_pair[0]], 0)
        all_down = jnp.concatenate([w[2 * hidden :] for w in weights], 0)
    else:
        zeros = jnp.zeros((length, width), BF16)

        def step(totals, weight_at):
            weight, position = weight_at
            name = (position * 2 + side)[None]
            down = weight[2 * hidden :]
            own = expert_pass(tokens_own, grad_rel, gates_own, name, [weight], totals[0])
            pair = expert_pass(tokens_pair, grad_pair, gates_pair, name, [weight], totals[1])
            grads = weight_grad(
                0, hidden, (own[2], pair[2]), (own[1], pair[1]), both_tokens, both_grads, BF16
            )
            moe_own = totals[2] + dot(own[1], down, 0, 0)
            moe_pair = totals[3] + dot(pair[1], down, 0, 0)
            return (own[0], pair[0], moe_own, moe_pair), (own[3][0], pair[3][0], grads)

        (sum_own, sum_pair, moe_own, moe_pair), (gate_own, gate_pair, weight_grads) = lax.scan(
            step,
            (zeros, zeros, zeros.astype(F32), zeros.astype(F32)),
            (weights, jnp.arange(line, dtype=jnp.int32)),
        )
        kept_own, sent_own, kept_pair, sent_pair = sum_own[:half], sum_own[half:], sum_pair[:half], sum_pair[half:]

    slot_of = jnp.asarray(
        [
            [q if not short else 0 if q == p else 1 + order[p].index(q - p) for q in range(line)]
            for p in range(line)
        ],
        jnp.int32,
    )[place]
    numbers = jnp.arange(experts, dtype=jnp.int32)
    slot_at = slot_of[numbers // 2] + jnp.where(numbers % 2 == side, 0, line)
    slot_names_hot = (slot_at[:, None] == numbers[None, :]).astype(F32)
    gate_sums = jnp.concatenate([gate_own, gate_pair], 0)
    grad_after_low, grad_after, grad_router, grad_second = tokens_back(
        tensors,
        experts,
        kept_pair,
        sent_pair,
        kept_own,
        sent_own,
        gate_sums[:, :half],
        gate_sums[:, half:],
        slot_names_hot,
        router_probs[:, :rows],
        named[:, :rows],
        router_rows,
        after,
        second_gain[None],
        own_quarter(cotangent),
    )

    if short:
        moe_own = dot(gated_own, all_down, 0, 0).astype(BF16)
        moe_pair = dot(gated_pair, all_down, 0, 0).astype(BF16)
    moe = jnp.stack([moe_own, moe_pair])
    got = links.over_tensor(moe[:, half:].astype(BF16), 1).astype(F32)
    crossing = (moe[:, rows:half].astype(F32) + got[:, rows:]).astype(BF16)
    moe = moe[:, :rows].astype(F32) + got[:, :rows] + links.over_tensor(crossing, 2).astype(F32)
    moe = moe[0] + links.over_pair(moe[1].astype(BF16)).astype(F32)
    layer_out = links.absolute(links.gather((after + moe).astype(BF16)))

    def sum_rows(values):
        return lax.psum(values, "expert")

    def flow(step):
        got = None
        for reach in range(line - 1, 0, -1):
            takers = {}
            for p in range(line):
                if 0 <= p + step * reach < line:
                    takers.setdefault(1 + order[p].index(step * reach), []).append(p)
            total = pick(place, [(weight_grads[s], ps) for s, ps in takers.items()])
            if got is not None:
                total = total.astype(F32) + got.astype(F32)
            got = links.along(total.astype(BF16), step, reach)
        return got.astype(F32)

    if short:
        weight_grads = {}
        for slot in range(line - 1, -1, -1):
            if slot == last:
                columns, own, pair = 0, last_own, last_pair
            else:
                columns, own, pair = slot, first_own[1:], first_pair[1:]
            weight_grads[slot] = weight_grad(
                columns,
                hidden,
                (own[1], pair[1]),
                (own[0], pair[0]),
                both_tokens,
                both_grads,
                F32 if slot == 0 else BF16,
            )
        expert_grads = weight_grads[0]
        if line > 1:
            expert_grads = expert_grads + flow(1) + flow(-1)
    else:
        expert_grads = lax.psum_scatter(
            weight_grads, "expert", scatter_dimension=0, axis_index_groups=sides
        ).astype(F32)

    grad_output = dot(context_rel, grad_after_low, 0, 0).astype(BF16)
    grad_output = sum_rows(grad_output).astype(F32)
    grad_context = links.absolute(dot(grad_after_low, w_output, 1, 1).astype(BF16))
    grad_heads = grad_context.reshape(length, heads, HD)
    query_grads = []
    key_grad = jnp.zeros((length, HD), F32)
    value_grad = jnp.zeros((length, HD), F32)
    for head in range(heads):
        dprob = dot(grad_heads[:, head], value_low, 1, 1)
        delta = jnp.sum(probs[head] * dprob, axis=-1, keepdims=True)
        dscore = (probs[head] * (dprob - delta)).astype(BF16)
        query_grads.append(dot(dscore, key_rot, 1, 0) * scale)
        key_grad = key_grad + dot(dscore, query_rot[:, head], 0, 0) * scale
        value_grad = value_grad + dot(probs[head].astype(BF16), grad_heads[:, head], 0, 0)
    query_grad = jnp.concatenate(
        [unrotate(g, cos_table, sin_table).astype(BF16) for g in query_grads], 1
    )
    key_grad = unrotate(key_grad, cos_table, sin_table).astype(BF16)
    value_grad = value_grad.astype(BF16)
    attn_weights = jnp.concatenate([w_query, key_weight, value_weight], 1)
    attn_grads = jnp.concatenate([query_grad, key_grad, value_grad], 1)
    grads_rel = links.relative(attn_grads)
    early = jnp.zeros((-(-(experts + 2) // 8) * 8, width), F32)
    early = early.at[:experts].set(grad_router).at[experts : experts + 1].set(grad_second)
    grad_inputs, sums = inputs_back(
        tensors, experts, grads_rel, attn_weights, stream, first_gain[None], grad_after, early
    )
    grad_inputs = links.absolute(grad_inputs)
    grad_router, grad_second, grad_first = sums[:experts].T, sums[experts], sums[experts + 1]
    query_width = heads * HD
    attn_weight_grads = dot(attn_grads, attn_in, 0, 0)
    lead = links.tensor % 2
    kv_kept = lax.dynamic_slice_in_dim(attn_weight_grads, query_width + lead * HD, HD, 0)
    kv_sent = lax.dynamic_slice_in_dim(attn_weight_grads, query_width + (1 - lead) * HD, HD, 0)
    kv_kept = kv_kept + links.over_tensor(kv_sent.astype(BF16), 1).astype(F32)
    summed = sum_rows(
        jnp.concatenate([attn_weight_grads[:query_width].astype(BF16), kv_kept.astype(BF16)], 0)
    )
    grad_query = summed[:query_width].T.astype(F32)
    kv_mine = summed[query_width:]
    kv_theirs = links.over_tensor(kv_mine, 2)
    first_head = kv_head == 0
    kv_both = jnp.concatenate(
        [jnp.where(first_head, kv_mine, kv_theirs), jnp.where(first_head, kv_theirs, kv_mine)], 0
    )
    kv_other = links.over_tensor(kv_both, 1)
    grad_key = jnp.where(lead == 0, kv_both, kv_other).T.astype(F32)
    grad_value = jnp.where(lead == 0, kv_other, kv_both).T.astype(F32)

    return (
        layer_out,
        grad_inputs,
        grad_first,
        grad_second,
        grad_query,
        grad_key,
        grad_value,
        grad_output,
        grad_router,
        expert_grads[:hidden].T[None],
        expert_grads[hidden : 2 * hidden].T[None],
        expert_grads[2 * hidden :][None],
    )


def solution(mesh):
    experts, tensors = mesh.shape["expert"], mesh.shape["tensor"]
    in_specs = (
        P("expert", None),
        P("expert", None),
        P("expert", None),
        P(),
        P(),
        P(None, "tensor"),
        P(),
        P(),
        P("tensor", None),
        P(),
        P("expert", None, "tensor"),
        P("expert", None, "tensor"),
        P("expert", "tensor", None),
    )
    out_specs = (
        P("expert", None),
        P("expert", None),
        P(),
        P(),
        P(None, "tensor"),
        P(),
        P(),
        P("tensor", None),
        P(),
        P("expert", None, "tensor"),
        P("expert", None, "tensor"),
        P("expert", "tensor", None),
    )

    def run(*arrays):
        return shards(experts, tensors, *arrays)

    return jax.shard_map(run, mesh=mesh, in_specs=in_specs, out_specs=out_specs, check_vma=False)
```

time: 730 us -> 682 us (0.934)
  Pallas kernels: 13.4 us -> 276 us
  matrix products: 212 us -> 56.7 us
  waiting for transfers between devices: 206 us -> 128 us
  blocking collectives: 49.2 us -> 0 us
  other arithmetic: 98.5 us -> 78.1 us
  starting transfers between devices: 69.6 us -> 50.2 us
  local copies, waits for them, and re-layouts: 48 us -> 67 us
  between operations: 26.4 us -> 18.5 us
    pallas_call x0 -> x11, Pallas kernels: none -> 263 us  [the longest x1 68.3 us: tokens_back(): pl.pallas_call(functools.partial(tokens_back_kernel, tensors), out_shape=...]
    dot_general x56 -> x25, matrix products: 212 us -> 56.7 us  [dot(): lax.dot_general(left, right, (((left_dim,), (right_dim,)), ((), ())), pre...]
    ppermute x12, waiting for transfers between devices: 101 us -> 18.8 us  [along(): return lax.ppermute(values, 'expert', pairs)]
    psum x1, waiting for transfers between devices: 30.8 us -> 93.3 us  [sum_rows(): return lax.psum(values, 'expert')]
    psum x1 -> x0, blocking collectives: 49.2 us -> none  [shards(): lax.psum((grad_first, grad_second, grad_router), ('expert', 'tensor'))]
    ppermute x27 -> x8, waiting for transfers between devices: 49.5 us -> 8.27 us  [over_tensor(): lax.ppermute(values, 'tensor', [(i, i ^ bit) for i in range(self.tensors)])]
    ppermute x27 -> x8, starting transfers between devices: 32.5 us -> 9.77 us  [over_tensor(): lax.ppermute(values, 'tensor', [(i, i ^ bit) for i in range(self.tensors)])]
    ppermute x6 -> x3, waiting for transfers between devices: 25.2 us -> 7.48 us  [over_expert(): lax.ppermute(values, 'expert', [(i, i ^ bit) for i in range(self.experts)])]
  transfers between devices with their start and end apart: 46 -> 24, of which waited for: 14 -> 4; matrix products, arithmetic and copies ran while one was open for 44% -> 23% of each run, Pallas kernels for 2% -> 32%
where the time goes in v2:
time: 682 us; the launch traced here: 675 us
  Pallas kernels  276 us (40%)
  waiting for transfers between devices  128 us (19%)
  other arithmetic  78.1 us (11%)
  local copies, waits for them, and re-layouts  67 us (10%)
  matrix products  56.7 us (8%)
  starting transfers between devices  50.2 us (7%)
  between operations  18.5 us (3%)
    psum x1, waiting for transfers between devices, sum_rows(): return lax.psum(values, 'expert')  93.3 us
    pallas_call x1, Pallas kernels, tokens_back(): pl.pallas_call(functools.partial(tokens_back_kernel, tensors), out_shape=...  68.3 us
    pallas_call x1, Pallas kernels, attend_out(): pl.pallas_call(functools.partial(attend_out_kernel, tensors), out_shape=[...  68.3 us
    dot_general x25, matrix products, dot(): lax.dot_general(left, right, (((left_dim,), (right_dim,)), ((), ())), pre...  56.7 us
    pallas_call x4, Pallas kernels, expert_pass(): pl.pallas_call(functools.partial(expert_kernel, count, hidden, split, bef...  53.8 us
    pallas_call x1, Pallas kernels, inputs_back(): pl.pallas_call(functools.partial(inputs_back_kernel, tensors, experts), o...  49.8 us
    unnamed x250, local copies, waits for them, and re-layouts  40.8 us
    ppermute x12, starting transfers between devices, along(): return lax.ppermute(values, 'expert', pairs)  37.6 us
  transfers between devices with their start and end apart: 24, of which 4 were waited for; matrix products, arithmetic and copies ran while one was open for 23% of the time, Pallas kernels for 32%

profile of v2, /device:TPU:1, one launch (start us, length us, event | category | flops | bytes accessed | tf_op | source)
XLA Modules:
  0.0 674.6 jit_solution(10885280760582244151)
XLA Ops:
  10.1 5.9 collective-permute-start
  17.4 3.6 constant_dynamic-slice_fusion.24
  27.8 3.1 fusion.77
  30.9 3.2 fusion.41
  37.2 3.8 fusion.79
  41.6 2.9 fusion.88
  44.4 2.9 fusion.90
  47.4 3.0 fusion.89
  50.4 3.8 fusion.75
  54.1 4.5 online-softmax
  59.7 4.5 online-softmax.2
  65.2 4.5 online-softmax.1
  73.1 3.8 fusion.4
  78.6 5.5 collective-permute-start.2
  99.2 18.8 %collective-permute-done.3 = bf16[576,1536]{1,0:T(8,128)(2,1)} collective-permute-done((bf16[576,1536]{1,0:T(8,128)(2,1)}, bf16[576,1536]{1,0:T(8,128)(2,1)}, u32[]{:S(2)}, u32[]{:S(2)}) %collective-permute-start.3) | collective-permute-done | bytes 1769504 | tf_op jit(solution)/shard_map/ppermute | solution.py:84
  119.3 4.2 collective-permute-start.4
  126.0 68.3 %shard_map.265 = (bf16[1024,1536]{1,0:T(8,128)(2,1)S(1)}, bf16[1024,1536]{1,0:T(8,128)(2,1)S(1)}, f32[256,1536]{1,0:T(8,128)S(1)}) custom-call(bf16[1024,384]{1,0:T(8,128)(2,1)S(1)} %copy-done.43, bf16[384,1536]{1,0:T(8,128)(2,1)S(1)} %copy-done.57, bf16[256,1536]{1,0:T(8,128)(2,1)S(1)} %copy-done.41, f32[1,1536]{1,0:T(1,128)S(1)} %broadcast_in_dim.19.gain), custom_call_target="tpu_custom_call" | custom-call | flops 60000002048 | bytes 10000000 | tf_op jit(solution)/shard_map/pallas_call | solution.py:330
  197.6 4.9 select_select_fusion.1
  205.4 18.1 %shard_map.268 = (bf16[1024,1536]{1,0:T(8,128)(2,1)}, bf16[576,1024]{1,0:T(8,128)(2,1)S(1)}, bf16[1152,1024]{1,0:T(8,128)(2,1)}, f32[3,1024]{1,0:T(4,128)S(1)}) custom-call(s32[3]{0:T(128)S(1)} %slice_bitcast_fusion.14.refs_0_, bf16[1024,1536]{1,0:T(8,128)(2,1)} %copy-done.3, bf16[1024,1536]{1,0:T(8,128)(2,1)} %copy-done.10, ...), custom_call_target="tpu_custom_call" | custom-call | flops 9059696640 | bytes 17891328 | tf_op jit(solution)/shard_map/pallas_call | solution.py:184
  224.6 8.1 %shard_map.269 = (bf16[512,1536]{1,0:T(8,128)(2,1)S(1)}, bf16[512,1536]{1,0:T(8,128)(2,1)S(1)}, bf16[192,1024]{1,0:T(8,128)(2,1)S(1)}, bf16[384,1024]{1,0:T(8,128)(2,1)S(1)}, f32[1,1024]{1,0:T(1,128)S(1)}) custom-call(s32[1]{0:T(128)} %bitcast.12.refs_0_, bf16[1024,1536]{1,0:T(8,128)(2,1)} %copy-done.3, bf16[1024,1536]{1,0:T(8,128)(2,1)} %copy-done.10, ...), custom_call_target="tpu_custom_call" | custom-call | flops 3019898880 | bytes 14352384 | tf_op jit(solution)/shard_map/pallas_call | solution.py:184
  232.8 18.6 %shard_map.266 = (bf16[1024,1536]{1,0:T(8,128)(2,1)}, bf16[576,1024]{1,0:T(8,128)(2,1)S(1)}, bf16[1152,1024]{1,0:T(8,128)(2,1)}, f32[3,1024]{1,0:T(4,128)S(1)}) custom-call(s32[3]{0:T(128)S(1)} %slice_bitcast_fusion.14.refs_0_, bf16[1024,1536]{1,0:T(8,128)(2,1)} %copy-done, bf16[1024,1536]{1,0:T(8,128)(2,1)} %pad_maximum_fusion.refs_2_.grad_own, ...), custom_call_target="tpu_custom_call" | custom-call | flops 9059696640 | bytes 17891328 | tf_op jit(solution)/shard_map/pallas_call | solution.py:184
  253.9 9.0 %shard_map.267 = (bf16[512,1536]{1,0:T(8,128)(2,1)S(1)}, bf16[512,1536]{1,0:T(8,128)(2,1)S(1)}, bf16[192,1024]{1,0:T(8,128)(2,1)S(1)}, bf16[384,1024]{1,0:T(8,128)(2,1)S(1)}, f32[1,1024]{1,0:T(1,128)S(1)}) custom-call(s32[1]{0:T(128)} %bitcast.12.refs_0_, bf16[1024,1536]{1,0:T(8,128)(2,1)} %copy-done, bf16[1024,1536]{1,0:T(8,128)(2,1)} %pad_maximum_fusion.refs_2_.grad_own, ...), custom_call_target="tpu_custom_call" | custom-call | flops 3019898880 | bytes 14352384 | tf_op jit(solution)/shard_map/pallas_call | solution.py:184
  268.8 6.0 shard_map.274
  276.7 4.4 collective-permute-start.17
  282.5 68.3 %shard_map.270 = (bf16[1024,1536]{1,0:T(8,128)(2,1)}, f32[256,1536]{1,0:T(8,128)S(1)}, f32[8,1536]{1,0:T(8,128)S(1)}, f32[1,1536]{1,0:T(1,128)S(1)}) custom-call(bf16[512,1536]{1,0:T(8,128)(2,1)S(1)} %copy-done.52, bf16[512,1536]{1,0:T(8,128)(2,1)S(1)} %copy-done.54, bf16[512,1536]{1,0:T(8,128)(2,1)} %copy-done.55, bf16[512,1536]{1,0:T(8,128)(2,1)} %copy-done.56, ...), custom_call_target="tpu_custom_call" | custom-call | flops 60000002048 | bytes 10000000 | tf_op jit(solution)/shard_map/pallas_call | solution.py:448
  350.9 4.3 convolution_convert_fusion.3
  355.8 4.3 fusion.14
  372.8 3.0 fusion.10
  375.8 4.8 fusion.9
  400.7 49.8 %shard_map.271 = (bf16[1024,1536]{1,0:T(8,128)(2,1)}, f32[16,1536]{1,0:T(8,128)S(1)}) custom-call(bf16[1024,640]{1,0:T(8,128)(2,1)S(1)} %pad_maximum_fusion.11.grads, bf16[1536,640]{1,0:T(8,128)(2,1)S(1)} %copy-done.34, bf16[256,1536]{1,0:T(8,128)(2,1)S(1)} %copy-done.42, f32[1,1536]{1,0:T(1,128)S(1)} %broadcast_in_dim.20.gain, f32[256,1536]{1,0:T(8,128)S(1)} %copy-done.60, ...), custom_call_target="tpu_custom_call" | custom-call | flops 49999998976 | bytes 10000000 | tf_op jit(solution)/shard_map/pallas_call | solution.py:522
  450.6 4.4 fusion.73
  459.8 5.3 shard_map.275
  465.1 5.1 shard_map.273
  478.0 3.7 convert_element_type.164
  489.4 6.2 shard_map.272
  495.6 5.6 add_convert_fusion.3
  501.2 5.4 collective-permute-start.18
  509.7 93.3 %all-reduce.4.cloned.1.call-done = (bf16[512,1536]{1,0:T(8,128)(2,1)}, bf16[384,1536]{1,0:T(8,128)(2,1)}) async-done(((bf16[512,1536]{1,0:T(8,128)(2,1)}, bf16[384,1536]{1,0:T(8,128)(2,1)}), (bf16[512,1536]{1,0:T(8,128)(2,1)}, bf16[384,1536]{1,0:T(8,128)(2,1)})) %all-reduce.4.cloned.1.call-update) | async-done | bytes 2752528 | tf_op jit(solution)/shard_map/psum | solution.py:723
  605.3 3.1 fusion.13
  609.9 4.8 add_convert_fusion.2
  614.7 3.2 collective-permute-start.19
  619.3 7.5 %collective-permute-done.11 = bf16[256,1536]{1,0:T(8,128)(2,1)S(1)} collective-permute-done((bf16[256,1536]{1,0:T(8,128)(2,1)S(1)}, bf16[256,1536]{1,0:T(8,128)(2,1)S(1)}, u32[]{:S(2)}, u32[]{:S(2)}) %collective-permute-start.11) | collective-permute-done | bytes 786464 | tf_op jit(solution)/shard_map/ppermute | solution.py:76
  633.2 3.0 convert_element_type.187
  636.2 8.3 %collective-permute-done.12 = bf16[256,1536]{1,0:T(8,128)(2,1)} collective-permute-done((bf16[256,1536]{1,0:T(8,128)(2,1)S(1)}, bf16[256,1536]{1,0:T(8,128)(2,1)}, u32[]{:S(2)}, u32[]{:S(2)}) %collective-permute-start.12) | collective-permute-done | bytes 786464 | tf_op jit(solution)/shard_map/ppermute | solution.py:73
  646.8 2.8 collective-permute-start.13
  649.7 3.3 convert_bitcast_fusion.1
  652.9 3.2 copy.142
  656.1 3.0 copy.141
  (382 shorter events, 135.4 us)
Async XLA Ops:
  7.2 595.8 %all-reduce.4.cloned.1.call-start = ((), (), s32[]{:S(2)}) async-start(), calls=%async_computation | async-start | bytes 5505024 | tf_op jit(solution)/shard_map/psum | solution.py:723
  8.8 12.2 %copy-start.35 = (bf16[576,1536]{1,0:T(8,128)(2,1)}, bf16[576,1536]{1,0:T(8,128)(2,1)S(1)}, u32[]{:S(2)}) copy-start(bf16[576,1536]{1,0:T(8,128)(2,1)S(1)} %pad_maximum_fusion.6.refs_4_) | copy-start | bytes 5308420
  8.8 68.2 %collective-permute-start.1 = (bf16[576,1536]{1,0:T(8,128)(2,1)S(1)}, bf16[576,1536]{1,0:T(8,128)(2,1)}, u32[]{:S(2)}, u32[]{:S(2)}) collective-permute-start(bf16[576,1536]{1,0:T(8,128)(2,1)S(1)} %pad_maximum_fusion.6.refs_4_), channel_id=1, source_target_pairs={{8,0},{12,4},{16,8},{20,12},{24,16},{28,20},{9,1},{13,5},{17,9},{2... | collective-permute-start | bytes 5308424 | tf_op jit(solution)/shard_map/ppermute | solution.py:84
  10.1 68.5 %collective-permute-start = (bf16[576,1536]{1,0:T(8,128)(2,1)S(1)}, bf16[576,1536]{1,0:T(8,128)(2,1)}, u32[]{:S(2)}, u32[]{:S(2)}) collective-permute-start(bf16[576,1536]{1,0:T(8,128)(2,1)S(1)} %pad_maximum_fusion.6.refs_4_), channel_id=1, source_target_pairs={{0,8},{4,12},{8,16},{12,20},{16,24},{20,28},{1,9},{5,13},{9,17},{1... | collective-permute-start | bytes 5308424 | tf_op jit(solution)/shard_map/ppermute | solution.py:84
  16.0 79.6 %collective-permute-start.8 = (s32[4,1024]{1,0:T(4,128)S(1)}, s32[4,1024]{1,0:T(4,128)S(1)}, u32[]{:S(2)}, u32[]{:S(2)}) collective-permute-start(s32[4,1024]{1,0:T(4,128)S(1)} %add_bitcast_fusion), channel_id=1, source_target_pairs={{0,4},{4,0},{8,12},{12,8},{16,20},{20,16},{24,28},{28,24},{1,5},{5... | collective-permute-start | bytes 49160 | tf_op jit(solution)/shard_map/ppermute | solution.py:76
  23.1 72.4 %collective-permute-start.6 = (bf16[512,1536]{1,0:T(8,128)(2,1)}, bf16[512,1536]{1,0:T(8,128)(2,1)}, u32[]{:S(2)}, u32[]{:S(2)}) collective-permute-start(bf16[512,1536]{1,0:T(8,128)(2,1)} %pad_maximum_fusion.8), channel_id=1, source_target_pairs={{0,4},{4,0},{8,12},{12,8},{16,20},{20,16},{24,28},{28,24},{1,5},{5... | collective-permute-start | bytes 4718600 | tf_op jit(solution)/shard_map/ppermute | solution.py:76
  25.8 24.5 %copy-start.104 = (f32[1024]{0:T(1024)}, f32[1024]{0:T(1024)S(1)}, u32[]{:S(2)}) copy-start(f32[1024]{0:T(1024)S(1)} %add_rsqrt_fusion) | copy-start | bytes 12292
  44.4 28.6 %copy-start.107 = (f32[1024]{0:T(1024)}, f32[1024]{0:T(1024)S(1)}, u32[]{:S(2)}) copy-start(f32[1024]{0:T(1024)S(1)} %get-tuple-element.220) | copy-start | bytes 12292
  47.4 38.2 %copy-start.111 = (f32[1024]{0:T(1024)}, f32[1024]{0:T(1024)S(1)}, u32[]{:S(2)}) copy-start(f32[1024]{0:T(1024)S(1)} %get-tuple-element.228) | copy-start | bytes 12292
  50.3 36.9 %copy-start.109 = (f32[1024]{0:T(1024)}, f32[1024]{0:T(1024)S(1)}, u32[]{:S(2)}) copy-start(f32[1024]{0:T(1024)S(1)} %get-tuple-element.224) | copy-start | bytes 12292
  77.0 41.1 %collective-permute-start.3 = (bf16[576,1536]{1,0:T(8,128)(2,1)}, bf16[576,1536]{1,0:T(8,128)(2,1)}, u32[]{:S(2)}, u32[]{:S(2)}) collective-permute-start(bf16[576,1536]{1,0:T(8,128)(2,1)} %collective-permute-done.1), channel_id=1, source_target_pairs={{8,0},{12,4},{16,8},{20,12},{24,16},{28,20},{9,1},{13,5},{17,9},{2... | collective-permute-start | bytes 5308424 | tf_op jit(solution)/shard_map/ppermute | solution.py:84
  78.6 40.8 %collective-permute-start.2 = (bf16[576,1536]{1,0:T(8,128)(2,1)}, bf16[576,1536]{1,0:T(8,128)(2,1)}, u32[]{:S(2)}, u32[]{:S(2)}) collective-permute-start(bf16[576,1536]{1,0:T(8,128)(2,1)} %collective-permute-done), channel_id=1, source_target_pairs={{0,8},{4,12},{8,16},{12,20},{16,24},{20,28},{1,9},{5,13},{9,17},{1... | collective-permute-start | bytes 5308424 | tf_op jit(solution)/shard_map/ppermute | solution.py:84
  95.5 28.0 %copy-start.43 = (bf16[1024,384]{1,0:T(8,128)(2,1)S(1)}, bf16[1024,384]{1,0:T(8,128)(2,1)}, u32[]{:S(2)}) copy-start(bf16[1024,384]{1,0:T(8,128)(2,1)} %pad_maximum_fusion.13.context) | copy-start | bytes 2359300
  95.6 101.9 %collective-permute-start.7 = (bf16[512,1536]{1,0:T(8,128)(2,1)}, bf16[512,1536]{1,0:T(8,128)(2,1)S(1)}, u32[]{:S(2)}, u32[]{:S(2)}) collective-permute-start(bf16[512,1536]{1,0:T(8,128)(2,1)} %collective-permute-done.6), channel_id=1, source_target_pairs={{0,1},{1,0},{2,3},{3,2},{4,5},{5,4},{6,7},{7,6},{8,9},{9,8},{10,11... | collective-permute-start | bytes 4718600 | tf_op jit(solution)/shard_map/ppermute | solution.py:73
  118.0 79.6 %collective-permute-start.5 = (bf16[576,1536]{1,0:T(8,128)(2,1)}, bf16[576,1536]{1,0:T(8,128)(2,1)S(1)}, u32[]{:S(2)}, u32[]{:S(2)}) collective-permute-start(bf16[576,1536]{1,0:T(8,128)(2,1)} %collective-permute-done.3), channel_id=1, source_target_pairs={{8,0},{12,4},{16,8},{20,12},{24,16},{28,20},{9,1},{13,5},{17,9},{2... | collective-permute-start | bytes 5308424 | tf_op jit(solution)/shard_map/ppermute | solution.py:84
  119.3 78.3 %collective-permute-start.4 = (bf16[576,1536]{1,0:T(8,128)(2,1)}, bf16[576,1536]{1,0:T(8,128)(2,1)S(1)}, u32[]{:S(2)}, u32[]{:S(2)}) collective-permute-start(bf16[576,1536]{1,0:T(8,128)(2,1)} %collective-permute-done.2), channel_id=1, source_target_pairs={{0,8},{4,12},{8,16},{12,20},{16,24},{20,28},{1,9},{5,13},{9,17},{1... | collective-permute-start | bytes 5308424 | tf_op jit(solution)/shard_map/ppermute | solution.py:84
  126.0 68.3 %copy-start.50 = (bf16[1536,8]{0,1:T(8,128)(2,1)S(1)}, bf16[1536,8]{0,1:T(8,128)(2,1)}, u32[]{:S(2)}) copy-start(bf16[1536,8]{0,1:T(8,128)(2,1)} %param.31) | copy-start | bytes 73732
  202.6 22.0 %copy-start.18 = (bf16[576,1536]{1,0:T(8,128)(2,1)}, bf16[576,1536]{1,0:T(8,128)(2,1)S(1)}, u32[]{:S(2)}) copy-start(bf16[576,1536]{1,0:T(8,128)(2,1)S(1)} %get-tuple-element.152.refs_4_) | copy-start | bytes 5308420
  232.7 18.7 %copy-start.39 = (bf16[384,1024]{1,0:T(8,128)(2,1)}, bf16[384,1024]{1,0:T(8,128)(2,1)S(1)}, u32[]{:S(2)}) copy-start(bf16[384,1024]{1,0:T(8,128)(2,1)S(1)} %get-tuple-element.91.grad_pre_pair) | copy-start | bytes 2359300
  232.7 18.6 %copy-start.45 = (bf16[192,1024]{1,0:T(8,128)(2,1)}, bf16[192,1024]{1,0:T(8,128)(2,1)S(1)}, u32[]{:S(2)}) copy-start(bf16[192,1024]{1,0:T(8,128)(2,1)S(1)} %get-tuple-element.73.gated_pair) | copy-start | bytes 1179652
  232.8 18.6 %copy-start.51 = (bf16[512,1536]{1,0:T(8,128)(2,1)}, bf16[512,1536]{1,0:T(8,128)(2,1)S(1)}, u32[]{:S(2)}) copy-start(bf16[512,1536]{1,0:T(8,128)(2,1)S(1)} %get-tuple-element.74.kept_pair) | copy-start | bytes 4718596
  232.8 18.6 %copy-start.53 = (bf16[512,1536]{1,0:T(8,128)(2,1)}, bf16[512,1536]{1,0:T(8,128)(2,1)S(1)}, u32[]{:S(2)}) copy-start(bf16[512,1536]{1,0:T(8,128)(2,1)S(1)} %get-tuple-element.75.sent_pair) | copy-start | bytes 4718596
  268.8 12.3 %copy-start.54 = (bf16[512,1536]{1,0:T(8,128)(2,1)S(1)}, bf16[512,1536]{1,0:T(8,128)(2,1)}, u32[]{:S(2)}) copy-start(bf16[512,1536]{1,0:T(8,128)(2,1)} %copy-done.53) | copy-start | bytes 4718596
  274.8 220.8 %collective-permute-start.20 = (bf16[576,1536]{1,0:T(8,128)(2,1)}, bf16[576,1536]{1,0:T(8,128)(2,1)}, u32[]{:S(2)}, u32[]{:S(2)}) collective-permute-start(bf16[576,1536]{1,0:T(8,128)(2,1)} %shard_map.274), channel_id=1, source_target_pairs={{24,16},{28,20},{25,17},{29,21},{26,18},{30,22},{27,19},{31,23}} | collective-permute-start | bytes 5308424 | tf_op jit(solution)/shard_map/ppermute | solution.py:84
  276.7 218.9 %collective-permute-start.17 = (bf16[576,1536]{1,0:T(8,128)(2,1)}, bf16[576,1536]{1,0:T(8,128)(2,1)}, u32[]{:S(2)}, u32[]{:S(2)}) collective-permute-start(bf16[576,1536]{1,0:T(8,128)(2,1)} %shard_map.274), channel_id=1, source_target_pairs={{0,8},{4,12},{1,9},{5,13},{2,10},{6,14},{3,11},{7,15}} | collective-permute-start | bytes 5308424 | tf_op jit(solution)/shard_map/ppermute | solution.py:84
  282.5 68.3 %copy-start.58 = (bf16[384,1536]{1,0:T(8,128)(2,1)S(1)}, bf16[384,1536]{1,0:T(8,128)(2,1)}, u32[]{:S(2)}) copy-start(bf16[384,1536]{1,0:T(8,128)(2,1)} %weight.1) | copy-start | bytes 3538948
  382.6 95.3 %collective-permute-start.9 = (bf16[2,512,1536]{2,1,0:T(8,128)(2,1)}, bf16[2,512,1536]{2,1,0:T(8,128)(2,1)}, u32[]{:S(2)}, u32[]{:S(2)}) collective-permute-start(bf16[2,512,1536]{2,1,0:T(8,128)(2,1)} %fusion.11), channel_id=1, source_target_pairs={{0,1},{1,0},{2,3},{3,2},{4,5},{5,4},{6,7},{7,6},{8,9},{9,8},{10,11... | collective-permute-start | bytes 9437192 | tf_op jit(solution)/shard_map/ppermute | solution.py:73
  400.6 49.9 %copy-start.73 = (bf16[1024,640]{1,0:T(8,128)(2,1)S(1)}, bf16[1024,640]{1,0:T(8,128)(2,1)}, u32[]{:S(2)}) copy-start(bf16[1024,640]{1,0:T(8,128)(2,1)} %concatenate.103) | copy-start | bytes 3932164
  400.6 49.9 %copy-start.103 = (f32[1536]{0:T(1024)S(1)}, f32[1536]{0:T(1024)}, u32[]{:S(2)}) copy-start(f32[1536]{0:T(1024)} %param.25) | copy-start | bytes 18436
  400.6 49.9 %copy-start.105 = (f32[1024]{0:T(1024)S(1)}, f32[1024]{0:T(1024)}, u32[]{:S(2)}) copy-start(f32[1024]{0:T(1024)} %copy-done.104) | copy-start | bytes 12292
  400.6 54.7 %copy-start.12 = (bf16[1024,1536]{1,0:T(8,128)(2,1)S(1)}, bf16[1024,1536]{1,0:T(8,128)(2,1)}, u32[]{:S(2)}) copy-start(bf16[1024,1536]{1,0:T(8,128)(2,1)} %copy-done.10) | copy-start | bytes 9437188
  400.6 54.7 %copy-start.14 = (bf16[1152,1024]{1,0:T(8,128)(2,1)S(1)}, bf16[1152,1024]{1,0:T(8,128)(2,1)}, u32[]{:S(2)}) copy-start(bf16[1152,1024]{1,0:T(8,128)(2,1)} %get-tuple-element.89.grad_pre_pair) | copy-start | bytes 7077892
  455.2 17.5 %collective-permute-start.14 = (bf16[128,1536]{1,0:T(8,128)(2,1)S(1)}, bf16[128,1536]{1,0:T(8,128)(2,1)S(1)}, u32[]{:S(2)}, u32[]{:S(2)}) collective-permute-start(bf16[128,1536]{1,0:T(8,128)(2,1)S(1)} %dynamic-slice_convert_fusion), channel_id=1, source_target_pairs={{0,1},{1,0},{2,3},{3,2},{4,5},{5,4},{6,7},{7,6},{8,9},{9,8},{10,11... | collective-permute-start | bytes 1179656 | tf_op jit(solution)/shard_map/ppermute | solution.py:73
  481.9 13.7 %copy-start.71 = (f32[2,512,1536]{2,1,0:T(8,128)}, f32[2,512,1536]{2,1,0:T(8,128)S(1)}, u32[]{:S(2)}) copy-start(f32[2,512,1536]{2,1,0:T(8,128)S(1)} %convert_element_type.164) | copy-start | bytes 18874372
  483.5 121.8 %collective-permute-start.10 = (bf16[2,256,1536]{2,1,0:T(8,128)(2,1)}, bf16[2,256,1536]{2,1,0:T(8,128)(2,1)}, u32[]{:S(2)}, u32[]{:S(2)}) collective-permute-start(bf16[2,256,1536]{2,1,0:T(8,128)(2,1)} %fusion.12), channel_id=1, source_target_pairs={{0,2},{1,3},{2,0},{3,1},{4,6},{5,7},{6,4},{7,5},{8,10},{9,11},{10,... | collective-permute-start | bytes 4718600 | tf_op jit(solution)/shard_map/ppermute | solution.py:73
  495.6 109.8 %copy-start.68 = (bf16[1,1024,1536]{2,1,0:T(8,128)(2,1)S(1)}, bf16[1,1024,1536]{2,1,0:T(8,128)(2,1)}, u32[]{:S(2)}) copy-start(bf16[1,1024,1536]{2,1,0:T(8,128)(2,1)} %copy-done.66) | copy-start | bytes 9437188
  501.2 108.7 %collective-permute-start.18 = (bf16[576,1536]{1,0:T(8,128)(2,1)}, bf16[576,1536]{1,0:T(8,128)(2,1)}, u32[]{:S(2)}, u32[]{:S(2)}) collective-permute-start(bf16[576,1536]{1,0:T(8,128)(2,1)} %get-tuple-element.149), channel_id=1, source_target_pairs={{0,8},{4,12},{8,16},{12,20},{1,9},{5,13},{9,17},{13,21},{2,10},{6,... | collective-permute-start | bytes 5308424 | tf_op jit(solution)/shard_map/ppermute | solution.py:84
  506.6 103.3 %collective-permute-start.21 = (bf16[576,1536]{1,0:T(8,128)(2,1)}, bf16[576,1536]{1,0:T(8,128)(2,1)}, u32[]{:S(2)}, u32[]{:S(2)}) collective-permute-start(bf16[576,1536]{1,0:T(8,128)(2,1)} %get-tuple-element.150), channel_id=1, source_target_pairs={{16,8},{20,12},{24,16},{28,20},{17,9},{21,13},{25,17},{29,21},{18,... | collective-permute-start | bytes 5308424 | tf_op jit(solution)/shard_map/ppermute | solution.py:84
  604.1 15.1 %collective-permute-start.15 = (bf16[128,1536]{1,0:T(8,128)(2,1)S(1)}, bf16[128,1536]{1,0:T(8,128)(2,1)S(1)}, u32[]{:S(2)}, u32[]{:S(2)}) collective-permute-start(bf16[128,1536]{1,0:T(8,128)(2,1)S(1)} %slice.264), channel_id=1, source_target_pairs={{0,2},{1,3},{2,0},{3,1},{4,6},{5,7},{6,4},{7,5},{8,10},{9,11},{10,... | collective-permute-start | bytes 1179656 | tf_op jit(solution)/shard_map/ppermute | solution.py:73
  608.6 18.2 %copy-start.38 = (f32[256,1536]{1,0:T(8,128)S(1)}, f32[256,1536]{1,0:T(8,128)}, u32[]{:S(2)}) copy-start(f32[256,1536]{1,0:T(8,128)} %copy-done.37) | copy-start | bytes 4718596
  608.6 18.1 %collective-permute-start.11 = (bf16[256,1536]{1,0:T(8,128)(2,1)S(1)}, bf16[256,1536]{1,0:T(8,128)(2,1)S(1)}, u32[]{:S(2)}, u32[]{:S(2)}) collective-permute-start(bf16[256,1536]{1,0:T(8,128)(2,1)S(1)} %fusion.39), channel_id=1, source_target_pairs={{0,4},{4,0},{8,12},{12,8},{16,20},{20,16},{24,28},{28,24},{1,5},{5... | collective-permute-start | bytes 2359304 | tf_op jit(solution)/shard_map/ppermute | solution.py:76
  614.7 44.4 %collective-permute-start.19 = (bf16[576,1536]{1,0:T(8,128)(2,1)}, bf16[576,1536]{1,0:T(8,128)(2,1)}, u32[]{:S(2)}, u32[]{:S(2)}) collective-permute-start(bf16[576,1536]{1,0:T(8,128)(2,1)} %get-tuple-element.169), channel_id=1, source_target_pairs={{0,8},{4,12},{8,16},{12,20},{16,24},{20,28},{1,9},{5,13},{9,17},{1... | collective-permute-start | bytes 5308424 | tf_op jit(solution)/shard_map/ppermute | solution.py:84
  617.9 41.2 %collective-permute-start.22 = (bf16[576,1536]{1,0:T(8,128)(2,1)}, bf16[576,1536]{1,0:T(8,128)(2,1)}, u32[]{:S(2)}, u32[]{:S(2)}) collective-permute-start(bf16[576,1536]{1,0:T(8,128)(2,1)} %get-tuple-element.170), channel_id=1, source_target_pairs={{8,0},{12,4},{16,8},{20,12},{24,16},{28,20},{9,1},{13,5},{17,9},{2... | collective-permute-start | bytes 5308424 | tf_op jit(solution)/shard_map/ppermute | solution.py:84
  627.1 17.3 %copy-start.76 = (bf16[256,1536]{1,0:T(8,128)(2,1)}, bf16[256,1536]{1,0:T(8,128)(2,1)S(1)}, u32[]{:S(2)}) copy-start(bf16[256,1536]{1,0:T(8,128)(2,1)S(1)} %fusion.22) | copy-start | bytes 2359300
  627.1 17.3 %collective-permute-start.12 = (bf16[256,1536]{1,0:T(8,128)(2,1)S(1)}, bf16[256,1536]{1,0:T(8,128)(2,1)}, u32[]{:S(2)}, u32[]{:S(2)}) collective-permute-start(bf16[256,1536]{1,0:T(8,128)(2,1)S(1)} %fusion.22), channel_id=1, source_target_pairs={{0,2},{1,3},{2,0},{3,1},{4,6},{5,7},{6,4},{7,5},{8,10},{9,11},{10,... | collective-permute-start | bytes 2359304 | tf_op jit(solution)/shard_map/ppermute | solution.py:73
  628.4 21.2 %collective-permute-start.16 = (bf16[256,1536]{1,0:T(8,128)(2,1)}, bf16[256,1536]{1,0:T(8,128)(2,1)}, u32[]{:S(2)}, u32[]{:S(2)}) collective-permute-start(bf16[256,1536]{1,0:T(8,128)(2,1)} %pad_maximum_fusion.15), channel_id=1, source_target_pairs={{0,1},{1,0},{2,3},{3,2},{4,5},{5,4},{6,7},{7,6},{8,9},{9,8},{10,11... | collective-permute-start | bytes 2359304 | tf_op jit(solution)/shard_map/ppermute | solution.py:73
  633.2 16.5 %copy-start.86 = (bf16[128,1536]{1,0:T(8,128)(2,1)S(1)}, bf16[128,1536]{1,0:T(8,128)(2,1)}, u32[]{:S(2)}) copy-start(bf16[128,1536]{1,0:T(8,128)(2,1)} %copy-done.85) | copy-start | bytes 1179652
  646.8 16.9 %collective-permute-start.13 = (bf16[512,1536]{1,0:T(8,128)(2,1)}, bf16[512,1536]{1,0:T(8,128)(2,1)}, u32[]{:S(2)}, u32[]{:S(2)}) collective-permute-start(bf16[512,1536]{1,0:T(8,128)(2,1)} %pad_maximum_fusion.9), channel_id=1, source_target_pairs={{0,1},{1,0},{2,3},{3,2},{4,5},{5,4},{6,7},{7,6},{8,9},{9,8},{10,11... | collective-permute-start | bytes 4718600 | tf_op jit(solution)/shard_map/ppermute | solution.py:73
  (99 other events, 422.0 us)
Sparse Core Ops, SparseCore 0:
  474.2 128.7 all-reduce.3

commit v3 on v2

--- a/solution.py
+++ b/solution.py
@@ -2,6 +2,7 @@
 
 import jax
 import jax.numpy as jnp
+import numpy as np
 from jax import lax
 from jax.experimental import pallas as pl
 from jax.experimental.pallas import tpu as pltpu
@@ -35,30 +36,16 @@
     return through, jnp.sum(upstream * normed, axis=0)
 
 
-def rotary_tables(length, head_size):
-    half_size = head_size // 2
-    positions = jnp.arange(length, dtype=F32)[:, None]
-    frequency = ROPE_BASE ** (-jnp.arange(half_size, dtype=F32) * 2.0 / head_size)
-    angles = positions * frequency[None, :]
-    return jnp.cos(angles), jnp.sin(angles)
-
-
-def rotate(values, cos_table, sin_table):
-    half = values.shape[-1] // 2
-    a, b = values[..., :half], values[..., half:]
-    return jnp.concatenate([a * cos_table - b * sin_table, b * cos_table + a * sin_table], axis=-1)
-
-
-def unrotate(values, cos_table, sin_table):
-    half = values.shape[-1] // 2
-    a, b = values[..., :half], values[..., half:]
-    return jnp.concatenate([a * cos_table + b * sin_table, b * cos_table - a * sin_table], axis=-1)
-
-
-def causal(scores):
-    rows = lax.broadcasted_iota(jnp.int32, scores.shape[-2:], 0)
-    cols = lax.broadcasted_iota(jnp.int32, scores.shape[-2:], 1)
-    return jnp.where(cols <= rows, scores, NEGATIVE)
+def rotary_tables(length):
+    frequency = np.float32(ROPE_BASE) ** (-np.arange(HD // 2, dtype=np.float32) * np.float32(2.0 / HD))
+    angles = np.arange(length, dtype=np.float32)[:, None] * frequency.astype(np.float32)[None]
+    cos, sin = np.cos(angles), np.sin(angles)
+    return np.concatenate([cos, cos], 1), np.concatenate([-sin, sin], 1)
+
+
+def turned(values, cos, sin, back=False):
+    other = pltpu.roll(values, HD // 2, 1) * sin
+    return values * cos - other if back else values * cos + other
 
 
 class Links:
@@ -77,11 +64,6 @@
 
     def over_pair(self, values):
         return self.over_expert(values, 1)
-
-    def along(self, values, step, reach=1):
-        places = [p for p in range(self.line) if 0 <= p + step * reach < self.line]
-        pairs = [(2 * p + s, 2 * (p + step) + s) for p in places for s in range(2)]
-        return lax.ppermute(values, "expert", pairs)
 
     def relative(self, values):
         rows = values.shape[0] // 4
@@ -115,16 +97,6 @@
         offsets = [p - place for p in range(line) if p != place]
         tables.append(sorted(offsets, key=lambda o: (abs(o), -o)))
     return tables
-
-
-def pick(place, options):
-    chosen = options[0][0]
-    for values, places in options[1:]:
-        wanted = place == places[0]
-        for p in places[1:]:
-            wanted = jnp.logical_or(wanted, place == p)
-        chosen = jnp.where(wanted, values, chosen)
-    return chosen
 
 
 def expert_kernel(count, hidden, split, prior, *refs):
@@ -248,11 +220,23 @@
         expert, tensor = lax.axis_index("expert"), lax.axis_index("tensor")
         return (expert + bit - 2 * bit * (expert // bit % 2), tensor)
 
-    def greet(self, partners):
+    def greet(self, partners, line=0):
         barrier = pltpu.get_barrier_semaphore()
         for partner in partners:
             pl.semaphore_signal(barrier, inc=1, device_id=partner, device_id_type=MESH)
-        pl.semaphore_wait(barrier, len(partners))
+        count = len(partners)
+        if line:
+            expert, tensor = lax.axis_index("expert"), lax.axis_index("tensor")
+            position = expert // 2
+            for step, there in ((2, position < line - 1), (-2, position > 0)):
+
+                @pl.when(there)
+                def _(step=step):
+                    device = (expert + step, tensor)
+                    pl.semaphore_signal(barrier, inc=1, device_id=device, device_id_type=MESH)
+
+            count = count + 1 - (position + 1) // line + (position + line - 1) // line
+        pl.semaphore_wait(barrier, count)
 
     def start(self, source, target, device):
         place = len(self.started)
@@ -268,12 +252,41 @@
         self.started.append(copy)
         return copy
 
+    def along(self, source, target, step, sends, receives):
+        device = (lax.axis_index("expert") + 2 * step, lax.axis_index("tensor"))
+        return self.over_when(source, target, device, sends, receives)
+
+    def over_when(self, source, target, device, sends, receives=None):
+        place = len(self.started)
+        copy = pltpu.make_async_remote_copy(
+            src_ref=source,
+            dst_ref=target,
+            send_sem=self.send.at[place],
+            recv_sem=self.recv.at[place],
+            device_id=device,
+            device_id_type=MESH,
+        )
+        pl.when(sends)(lambda: copy.start())
+        self.started.append(When(copy, sends, sends if receives is None else receives))
+        return self.started[-1]
+
     def finish(self):
         for copy in self.started:
             copy.wait_send()
 
 
-def sum_quarter(copies, part, sent, got, crossing, crossed):
+class When:
+    def __init__(self, copy, sends, receives):
+        self.copy, self.sends, self.receives = copy, sends, receives
+
+    def wait_send(self):
+        pl.when(self.sends)(lambda: self.copy.wait_send())
+
+    def wait_recv(self):
+        pl.when(self.receives)(lambda: self.copy.wait_recv())
+
+
+def sum_quarter(copies, part, sent, got, crossing, crossed, beside=None):
     rows = crossing.shape[0]
     sent[rows:, :] = part(3).astype(BF16)
     last = copies.start(sent.at[pl.ds(rows, rows)], got.at[pl.ds(rows, rows)], copies.core)
@@ -283,6 +296,8 @@
     last.wait_recv()
     crossing[...] = (other + got[rows:, :].astype(F32)).astype(BF16)
     far = copies.start(crossing, crossed, copies.far)
+    if beside is not None:
+        beside()
     mine = part(0)
     first.wait_recv()
     mine = mine + got[:rows, :].astype(F32)
@@ -301,11 +316,172 @@
     last.wait_recv()
 
 
-def attend_out_kernel(
-    tensors, context, weight, stream, gain, own, pair, after, sent, got, crossing, crossed, send, recv
-):
+def quarter_at(place):
+    tensor = lax.axis_index("tensor")
+    return (tensor % 2 + place // 2) % 2 + 2 * ((tensor // 2 + place % 2) % 2)
+
+
+def place_of(quarter):
+    tensor = lax.axis_index("tensor")
+    return 2 * ((tensor % 2 + quarter % 2) % 2) + (tensor // 2 + quarter // 2) % 2
+
+
+def masked_scores(query, keys, start, scale):
+    scores = dot(query, keys, 1, 1) * scale
+    rows = lax.broadcasted_iota(jnp.int32, scores.shape, 0) + start
+    cols = lax.broadcasted_iota(jnp.int32, scores.shape, 1)
+    return jnp.where(cols <= rows, scores, NEGATIVE)
+
+
+def attend_kernel(tensors, line, heads, *refs):
+    refs = list(refs)
+    stream, gain, weight, cos, sin, grad, routes = [refs.pop(0) for _ in range(7)]
+    own_weights = refs.pop(0) if line else None
+    attn_in, query, key, value, context, logsum = [refs.pop(0) for _ in range(6)]
+    grad_rel, grad_pair, routes_pair = [refs.pop(0) for _ in range(3)]
+    arrived = refs.pop(0) if line else None
+    send, recv = refs
     copies = Copies(tensors, send, recv)
-    copies.greet([copies.core, copies.far, copies.mate])
+    expert = lax.axis_index("expert")
+    position = expert // 2
+    copies.greet([copies.core, copies.mate], line)
+    length = stream.shape[0]
+    rows = length // 4
+    if line:
+        up = copies.along(
+            own_weights, arrived.at[1 - (position + 2) // line], 1, position < line - 1, position > 0
+        )
+        down = copies.along(own_weights, arrived.at[0], -1, position > 0, position < line - 1)
+    mates = []
+    for place in range(4):
+        at = pl.ds(place * rows, rows)
+        grad_rel[at, :] = grad[pl.ds(pl.multiple_of(quarter_at(place) * rows, rows), rows), :]
+        if place < 2:
+            mates.append(copies.start(grad_rel.at[at], grad_pair.at[at], copies.mate))
+    routes_copy = copies.start(routes, routes_pair, copies.mate)
+    for tile in range(4):
+        at = slice(tile * rows, (tile + 1) * rows)
+        normed = rms_norm(stream[at, :].astype(F32), gain[...])[0].astype(BF16)
+        attn_in[at, :] = normed
+        proj = dot(normed, weight[...], 1, 0)
+        for head in range(heads + 1):
+            part = proj[:, head * HD : (head + 1) * HD]
+            part = turned(part, cos[at, :], sin[at, :]).astype(BF16)
+            if head < heads:
+                query[at, head * HD : (head + 1) * HD] = part
+            else:
+                key[at, :] = part
+        value[at, :] = proj[:, (heads + 1) * HD :].astype(BF16)
+    for tile in range(4):
+        at, seen = slice(tile * rows, (tile + 1) * rows), (tile + 1) * rows
+        to = pl.ds(pl.multiple_of(place_of(tile) * rows, rows), rows)
+        for head in range(heads):
+            columns = slice(head * HD, (head + 1) * HD)
+            scores = masked_scores(query[at, columns], key[:seen, :], tile * rows, HD**-0.5)
+            peak = jnp.max(scores, axis=-1, keepdims=True)
+            exponent = jnp.exp(scores - peak)
+            total = jnp.sum(exponent, axis=-1, keepdims=True)
+            prob = (exponent / total).astype(BF16)
+            context[to, columns] = dot(prob, value[:seen, :], 1, 0).astype(BF16)
+            logsum[at, head : head + 1] = peak + jnp.log(total)
+    cores = []
+    for place in range(2):
+        mates[place].wait_recv()
+        source = grad_pair.at[pl.ds(place * rows, rows)]
+        cores.append(copies.start(source, grad_pair.at[pl.ds((2 + place) * rows, rows)], copies.core))
+    routes_copy.wait_recv()
+    for copy in cores + ([up, down] if line else []):
+        copy.wait_recv()
+    copies.finish()
+
+
+def anywhere():
+    return pl.BlockSpec(memory_space=pl.ANY)
+
+
+def attend(tensors, line, stream, gain, weight, cos, sin, grad, routes, own_weights):
+    length, width = stream.shape
+    heads = weight.shape[1] // HD - 2
+    shape = jax.ShapeDtypeStruct
+    return pl.pallas_call(
+        functools.partial(attend_kernel, tensors, line, heads),
+        out_shape=[
+            shape((length, width), BF16),
+            shape((length, heads * HD), BF16),
+            shape((length, HD), BF16),
+            shape((length, HD), BF16),
+            shape((length, heads * HD), BF16),
+            shape((length, HD), F32),
+            shape((length, width), BF16),
+            shape((length, width), BF16),
+            shape(routes.shape, routes.dtype),
+        ]
+        + ([shape((2,) + own_weights.shape, BF16)] if line else []),
+        in_specs=[vmem()] * 7 + [anywhere()] * bool(line),
+        out_specs=[vmem()] * 9 + [anywhere()] * bool(line),
+        scratch_shapes=[
+            pltpu.SemaphoreType.DMA((8,)),
+            pltpu.SemaphoreType.DMA((8,)),
+        ],
+        compiler_params=pltpu.CompilerParams(
+            collective_id=4, has_side_effects=True, vmem_limit_bytes=48 * 2**20
+        ),
+        cost_estimate=pl.CostEstimate(flops=4 * 10**10, bytes_accessed=10**7, transcendentals=0),
+    )(stream, gain, weight, cos, sin, grad, routes, *([own_weights] if line else []))
+
+
+def attend_back(heads, grad, weight, query, key, value, logsum, cos, sin, grads, grads_rel, key_grad, value_grad):
+    length = query.shape[0]
+    rows = length // 4
+    scale = HD**-0.5
+    for tile in range(3, -1, -1):
+        at, seen = slice(tile * rows, (tile + 1) * rows), (tile + 1) * rows
+        to = pl.ds(pl.multiple_of(place_of(tile) * rows, rows), rows)
+        grad_context = dot(grad[to, :], weight[...], 1, 1).astype(BF16)
+        for head in range(heads):
+            columns = slice(head * HD, (head + 1) * HD)
+            head_query = query[at, columns]
+            scores = masked_scores(head_query, key[:seen, :], tile * rows, scale)
+            prob = jnp.exp(scores - logsum[at, head : head + 1])
+            head_grad = grad_context[:, columns]
+            dprob = dot(head_grad, value[:seen, :], 1, 1)
+            delta = jnp.sum(prob * dprob, axis=-1, keepdims=True)
+            dscore = (prob * (dprob - delta)).astype(BF16)
+            dquery = dot(dscore, key[:seen, :], 1, 0) * scale
+            dquery = turned(dquery, cos[at, :], sin[at, :], True).astype(BF16)
+            grads[at, columns] = dquery
+            grads_rel[to, columns] = dquery
+            dkey = dot(dscore, head_query, 0, 0)
+            dvalue = dot(prob.astype(BF16), head_grad, 0, 0)
+            if tile == 3 and head == 0:
+                key_grad[...] = dkey
+                value_grad[...] = dvalue
+            else:
+                key_grad[:seen, :] += dkey
+                value_grad[:seen, :] += dvalue
+    for tile in range(4):
+        at = slice(tile * rows, (tile + 1) * rows)
+        to = pl.ds(pl.multiple_of(place_of(tile) * rows, rows), rows)
+        dkey = turned(key_grad[at, :] * scale, cos[at, :], sin[at, :], True).astype(BF16)
+        both = jnp.concatenate([dkey, value_grad[at, :].astype(BF16)], 1)
+        grads[at, heads * HD :] = both
+        grads_rel[to, heads * HD :] = both
+
+
+def attend_out_kernel(tensors, line, *refs):
+    refs = list(refs)
+    context, weight, stream, gain = [refs.pop(0) for _ in range(4)]
+    arrived = refs.pop(0) if line else None
+    own, pair, after = [refs.pop(0) for _ in range(3)]
+    second = refs.pop(0) if line else None
+    sent, got, crossing, crossed, send, recv = refs
+    copies = Copies(tensors, send, recv)
+    position = lax.axis_index("expert") // 2
+    copies.greet([copies.core, copies.far, copies.mate], line)
+    if line:
+        inner = (position > 0) & (position < line - 1)
+        up = copies.along(arrived.at[1], second, 1, inner, position >= line // 2)
+        down = copies.along(arrived.at[0], second, -1, inner, position < line // 2)
     rows = stream.shape[0]
 
     def part(place):
@@ -318,6 +494,9 @@
     gather_quarters(copies, own, rows)
     mate.wait_recv()
     gather_quarters(copies, pair, rows)
+    if line:
+        up.wait_recv()
+        down.wait_recv()
     copies.finish()
 
 
@@ -325,76 +504,90 @@
     return pl.BlockSpec(memory_space=pltpu.VMEM)
 
 
-def attend_out(tensors, context, weight, stream, gain):
+def attend_out(tensors, line, context, weight, stream, gain, arrived):
     rows, width = stream.shape
     return pl.pallas_call(
-        functools.partial(attend_out_kernel, tensors),
+        functools.partial(attend_out_kernel, tensors, line),
         out_shape=[
             jax.ShapeDtypeStruct((4 * rows, width), BF16),
             jax.ShapeDtypeStruct((4 * rows, width), BF16),
             jax.ShapeDtypeStruct((rows, width), F32),
-        ],
-        in_specs=[vmem()] * 4,
-        out_specs=[vmem()] * 3,
+        ]
+        + ([jax.ShapeDtypeStruct(arrived.shape[1:], BF16)] if line else []),
+        in_specs=[vmem()] * 4 + [anywhere()] * bool(line),
+        out_specs=[vmem()] * 3 + [anywhere()] * bool(line),
         scratch_shapes=[
             pltpu.VMEM((2 * rows, width), BF16),
             pltpu.VMEM((2 * rows, width), BF16),
             pltpu.VMEM((rows, width), BF16),
             pltpu.VMEM((rows, width), BF16),
-            pltpu.SemaphoreType.DMA((10,)),
-            pltpu.SemaphoreType.DMA((10,)),
+            pltpu.SemaphoreType.DMA((12,)),
+            pltpu.SemaphoreType.DMA((12,)),
         ],
         compiler_params=pltpu.CompilerParams(
             collective_id=1, has_side_effects=True, vmem_limit_bytes=40 * 2**20
         ),
         cost_estimate=pl.CostEstimate(flops=6 * 10**10, bytes_accessed=10**7, transcendentals=0),
-    )(context, weight, stream, gain)
-
-
-def tokens_back_kernel(
-    tensors,
-    kept_pair,
-    sent_pair,
-    kept_own,
-    sent_own,
-    rows_kept,
-    rows_sent,
-    names,
-    probs,
-    named,
-    router,
-    after,
-    gain,
-    grad,
-    whole,
-    grad_after,
-    grad_router,
-    grad_second,
-    got_pair,
-    got_own,
-    crossing_pair,
-    crossed_pair,
-    crossing_own,
-    crossed_own,
-    mate_out,
-    mate_in,
-    rows_got,
-    rows_crossing,
-    rows_crossed,
-    rows_mine,
-    rows_mate,
-    send,
-    recv,
-):
+    )(context, weight, stream, gain, *([arrived] if line else []))
+
+
+def tokens_back_kernel(tensors, line, hidden, heads, *refs):
+    refs = list(refs)
+    kept_pair, kept_own, rows_kept, rows_sent = [refs.pop(0) for _ in range(4)]
+    names, probs, named, router, after, gain, grad = [refs.pop(0) for _ in range(7)]
+    attention = [refs.pop(0) for _ in range(7)]
+    sent_pair, sent_own, moe_own, moe_pair = [refs.pop(0) for _ in range(4)]
+    factors = [refs.pop(0) for _ in range(12 if line else 0)]
+    whole, grad_after, grad_router, grad_second = [refs.pop(0) for _ in range(4)]
+    attention += [refs.pop(0) for _ in range(2)]
+    moe_out, mate_moe = refs.pop(0), refs.pop(0)
+    moe_got = refs.pop(0)
+    weight_grads = [refs.pop(0) for _ in range(line)]
+    going, turning = (refs.pop(0), refs.pop(0)) if line else (None, None)
+    attention += [refs.pop(0) for _ in range(2)]
+    moe_crossing, moe_crossed, block, local = [refs.pop(0) for _ in range(4)]
+    if line:
+        first_in, first_out, up_in, down_in = [refs.pop(0) for _ in range(4)]
+    got_pair, got_own, crossing_pair, crossed_pair, crossing_own, crossed_own = [refs.pop(0) for _ in range(6)]
+    mate_out, mate_in, rows_got, rows_crossing, rows_crossed, rows_mine, rows_mate, send, recv = refs
     copies = Copies(tensors, send, recv)
-    copies.greet([copies.core, copies.far, copies.mate])
+    position = lax.axis_index("expert") // 2
+    copies.greet([copies.core, copies.far, copies.mate], line)
     rows = grad.shape[0]
+
+    def weight_grad(slot):
+        if not line:
+            return
+        last = slot == line - 1
+        column = 0 if last else slot
+        pre_own, pre_pair, gated_own, gated_pair = factors[4:8] if last else factors[:4]
+        length, width = factors[8].shape
+        tile = width // 6
+        pre_spec = pl.BlockSpec((2 * hidden, length), lambda i: (column, 0))
+        gated_spec = pl.BlockSpec((hidden, length), lambda i: (column, 0))
+        token_spec = pl.BlockSpec((length, tile), lambda i: (0, i))
+        pltpu.emit_pipeline(
+            weight_grad_kernel,
+            grid=(6,),
+            in_specs=[pre_spec] * 2 + [gated_spec] * 2 + [token_spec] * 4,
+            out_specs=[pl.BlockSpec((3 * hidden, tile), lambda i: (0, i))],
+        )(pre_own, pre_pair, gated_own, gated_pair, *factors[8:], weight_grads[slot])
+
     low, high = pl.ds(0, rows), pl.ds(rows, rows)
     pair_last = copies.start(sent_pair.at[high], got_pair.at[high], copies.core)
     pair_first = copies.start(sent_pair.at[low], got_pair.at[low], copies.core)
     rows_core = copies.start(rows_sent, rows_got, copies.core)
     own_last = copies.start(sent_own.at[high], got_own.at[high], copies.core)
     own_first = copies.start(sent_own.at[low], got_own.at[low], copies.core)
+    moe_core = [
+        copies.start(source.at[pl.ds(2 * rows, 2 * rows)], moe_got.at[side], copies.core)
+        for side, source in enumerate((moe_own, moe_pair))
+    ]
+    if line:
+        weight_grad(line - 1)
+        up = copies.along(weight_grads[-1], first_in, 1, position == 0, position == 1)
+        down = copies.along(weight_grads[-1], first_in, -1, position == line - 1, position == line - 2)
+        inner = (position > 0) & (position < line - 1)
     pair_last.wait_recv()
     crossing_pair[...] = (kept_pair[rows:, :].astype(F32) + got_pair[rows:, :].astype(F32)).astype(BF16)
     pair_far = copies.start(crossing_pair, crossed_pair, copies.far)
@@ -407,6 +600,8 @@
     crossing_own[...] = (kept_own[rows:, :].astype(F32) + got_own[rows:, :].astype(F32)).astype(BF16)
     own_first.wait_recv()
     grad_tokens = kept_own[:rows, :].astype(F32) + got_own[:rows, :].astype(F32)
+    for slot in range(line - 2, 0, -1):
+        weight_grad(slot)
     pair_far.wait_recv()
     own_far = copies.start(crossing_own, crossed_own, copies.far)
     mate_out[...] = (mine_pair + crossed_pair[...].astype(F32)).astype(BF16)
@@ -414,11 +609,12 @@
     rows_far.wait_recv()
     rows_mine[...] = rows_kept[:, :rows] + rows_got[:, :rows] + rows_crossed[...]
     rows_over = copies.start(rows_mine, rows_mate, copies.mate)
+    weight_grad(0)
     rows_over.wait_recv()
-    line = rows_mine.shape[0] // 2
-    slots = jnp.concatenate([rows_mine[:line, :], rows_mate[line:, :]], 0)
+    count = rows_mine.shape[0] // 2
+    slots = jnp.concatenate([rows_mine[:count, :], rows_mate[count:, :]], 0)
     dprobs = jnp.zeros(probs.shape, F32)
-    for slot in range(2 * line):
+    for slot in range(2 * count):
         dprobs = dprobs + names[:, slot : slot + 1] * slots[slot : slot + 1, :]
     dprobs = dprobs * named[...]
     dlogits = (
@@ -436,70 +632,240 @@
     total = grad[...].astype(F32) + through
     grad_after[...] = total
     whole[:rows, :] = total.astype(BF16)
-    gather_quarters(copies, whole, rows)
+    second = []
+
+    def move(source, target, place):
+        copy = pltpu.make_async_copy(source, target, local.at[place])
+        copy.start()
+        copy.wait()
+
+    def moe_part(side, at):
+        move((moe_own, moe_pair)[side].at[at], block.at[0], 0)
+        move(moe_got.at[side, at], block.at[1], 0)
+        return block[0].astype(F32) + block[1].astype(F32)
+
+    def second_round():
+        up.wait_recv()
+        down.wait_recv()
+
+        @pl.when(inner)
+        def _():
+            move(weight_grads[line - 1], first_out, 0)
+            first_out[...] = (first_out[...].astype(F32) + first_in[...].astype(F32)).astype(BF16)
+
+        @pl.when(jnp.logical_not(inner))
+        def _():
+            move(weight_grads[line - 2], first_out, 0)
+
+        second.append(copies.along(first_out, up_in, 1, position < line // 2, inner))
+        second.append(copies.along(first_out, down_in, -1, position >= line // 2, inner))
+
+    gather_quarters(copies, whole, rows, second_round if line else None)
+    moe_far = []
+    for side in range(2):
+        moe_core[side].wait_recv()
+        moe_crossing[side] = moe_part(side, pl.ds(rows, rows)).astype(BF16)
+        moe_far.append(copies.start(moe_crossing.at[side], moe_crossed.at[side], copies.far))
+    attend_back(heads, whole, *attention)
+    for side, target in enumerate((moe_out, mate_moe)):
+        moe_far[side].wait_recv()
+        total = moe_part(side, pl.ds(0, rows)) + moe_crossed[side].astype(F32)
+        target[...] = (after[...] + total).astype(target.dtype) if side == 0 else total.astype(target.dtype)
+    if line:
+        move(weight_grads[1], going, 0)
+        move(weight_grads[2], turning, 0)
+        for copy in second:
+            copy.wait_recv()
+
+        @pl.when(inner)
+        def _():
+            going[...] = (going[...].astype(F32) + up_in[...].astype(F32)).astype(BF16)
+            turning[...] = (turning[...].astype(F32) + down_in[...].astype(F32)).astype(BF16)
+
     copies.finish()
 
 
-def tokens_back(tensors, experts, *operands):
-    rows, width = operands[-1].shape
+def tokens_back(tensors, experts, line, hidden, *operands):
+    rows, width = operands[10].shape
+    heads = operands[11].shape[0] // HD
     half = pltpu.VMEM((2 * rows, width), BF16)
     quarter = pltpu.VMEM((rows, width), BF16)
+    two_quarters = pltpu.VMEM((2, rows, width), BF16)
     small = pltpu.VMEM((experts, rows), F32)
+    shape = jax.ShapeDtypeStruct
+    shard = shape((3 * hidden, width), BF16)
+    outs = [
+        shape((4 * rows, width), BF16),
+        shape((rows, width), F32),
+        shape((experts, width), F32),
+        shape((1, width), F32),
+        shape((4 * rows, (heads + 2) * HD), BF16),
+        shape((4 * rows, (heads + 2) * HD), BF16),
+        shape((rows, width), F32),
+        shape((rows, width), BF16),
+        shape((2, 2 * rows, width), BF16),
+    ]
+    grads = [shape(shard.shape, F32)] + [shard] * (line - 1) if line else []
+    moving = [pltpu.VMEM(shard.shape, BF16)] * 4 if line else []
     return pl.pallas_call(
-        functools.partial(tokens_back_kernel, tensors),
-        out_shape=[
-            jax.ShapeDtypeStruct((4 * rows, width), BF16),
-            jax.ShapeDtypeStruct((rows, width), F32),
-            jax.ShapeDtypeStruct((experts, width), F32),
-            jax.ShapeDtypeStruct((1, width), F32),
-        ],
-        in_specs=[vmem()] * len(operands),
-        out_specs=[vmem()] * 4,
-        scratch_shapes=[half, half]
+        functools.partial(tokens_back_kernel, tensors, line, hidden, heads),
+        out_shape=outs + grads + [shard] * (2 if line else 0),
+        in_specs=[vmem()] * 18 + [anywhere()] * (len(operands) - 18),
+        out_specs=[vmem()] * 8 + [anywhere()] * (1 + line) + [vmem()] * (2 if line else 0),
+        scratch_shapes=[pltpu.VMEM((4 * rows, HD), F32)] * 2
+        + [two_quarters] * 3
+        + [pltpu.SemaphoreType.DMA((1,))]
+        + moving
+        + [half, half]
         + [quarter] * 6
         + [pltpu.VMEM((experts, 2 * rows), F32), small, small, small, small]
-        + [pltpu.SemaphoreType.DMA((16,)), pltpu.SemaphoreType.DMA((16,))],
+        + [pltpu.SemaphoreType.DMA((24,)), pltpu.SemaphoreType.DMA((24,))],
         compiler_params=pltpu.CompilerParams(
-            collective_id=2, has_side_effects=True, vmem_limit_bytes=48 * 2**20
+            collective_id=2, has_side_effects=True, vmem_limit_bytes=60 * 2**20
         ),
-        cost_estimate=pl.CostEstimate(flops=6 * 10**10, bytes_accessed=10**7, transcendentals=0),
+        cost_estimate=pl.CostEstimate(flops=10**11, bytes_accessed=10**7, transcendentals=0),
     )(*operands)
 
 
-def inputs_back_kernel(
-    tensors,
-    experts,
-    grads,
-    weight,
-    stream,
-    gain,
-    grad_after,
-    early,
-    whole,
-    sums,
-    sent,
-    got,
-    crossing,
-    crossed,
-    running,
-    arrived,
-    send,
-    recv,
-):
+def line_sum(copies, line, partial, whole, got, running, up_in, down_in):
+    position, side = lax.axis_index("expert") // 2, lax.axis_index("expert") % 2
+    count = partial.shape[0] // 2
+    chunk = count // line
+    order = [3 * (1 - position // 2), 2 - position // 2, position + 1 - 2 * (position % 2), position]
+    over = []
+
+    def rows_at(half, place):
+        return pl.ds(pl.multiple_of(half * count + place * chunk, 16), chunk)
+
+    def send_pair():
+        for place in order:
+            over.append(
+                copies.start(partial.at[rows_at(1 - side, place)], got.at[rows_at(0, place)], copies.mate)
+            )
+
+    def part(place):
+        mine = partial[rows_at(side, place), :].astype(F32)
+        return mine + got[rows_at(0, place), :].astype(F32)
+
+    flows = {1: {}, -1: {}}
+
+    def reach_step(reach):
+        over[line - 1 - reach].wait_recv()
+        for way, (step, landed) in enumerate(((1, up_in), (-1, down_in))):
+            target = position + step * reach
+            sends = (target >= 0) & (target < line)
+            origin = position - step
+            receives = (origin >= 0) & (origin < line) & (origin + step * reach >= 0) & (origin + step * reach < line)
+            slot = 3 * way + reach - 1
+            if reach < line - 1:
+                flows[step][reach + 1].wait_recv()
+
+            @pl.when(sends)
+            def _(slot=slot, target=target, landed=landed, step=step):
+                running[slot] = part(target).astype(BF16)
+                if reach < line - 1:
+
+                    @pl.when((position - step >= 0) & (position - step < line))
+                    def _():
+                        total = part(target) + landed[reach].astype(F32)
+                        running[slot] = total.astype(BF16)
+
+            flows[step][reach] = copies.along(running.at[slot], landed.at[reach - 1], step, sends, receives)
+
+    spread = []
+
+    def settle():
+        over[line - 1].wait_recv()
+        flows[1][1].wait_recv()
+        flows[-1][1].wait_recv()
+        total = part(position)
+        total = total + jnp.where(position > 0, up_in[0].astype(F32), 0.0)
+        total = total + jnp.where(position < line - 1, down_in[0].astype(F32), 0.0)
+        here = rows_at(side, position)
+        whole[here, :] = total.astype(BF16)
+        spread.append(copies.start(whole.at[here], whole.at[here], copies.mate))
+
+    mates = []
+
+    def spread_step(hop):
+        for step in (1, -1):
+            place = position - step * (hop - 1)
+            sends = (place >= 0) & (place < line) & (position + step >= 0) & (position + step < line)
+            origin = position - step * hop
+            receives = (origin >= 0) & (origin < line)
+            at = rows_at(side, jnp.clip(place, 0, line - 1))
+            spread.append(copies.along(whole.at[at], whole.at[at], step, sends, receives))
+
+    def spread_mate(hop):
+        for step, copy in ((1, spread[2 * hop - 1]), (-1, spread[2 * hop])):
+            copy.wait_recv()
+            origin = position - step * hop
+            there = (origin >= 0) & (origin < line)
+            at = rows_at(side, jnp.clip(origin, 0, line - 1))
+            mates.append(copies.over_when(whole.at[at], whole.at[at], copies.mate, there))
+
+    def end():
+        spread[0].wait_recv()
+        for copy in mates:
+            copy.wait_recv()
+
+    return send_pair, reach_step, settle, spread_step, spread_mate, end
+
+
+def inputs_back_kernel(tensors, experts, line, *refs):
+    refs = list(refs)
+    grads_rel, weight, stream, gain, grad_after, early = [refs.pop(0) for _ in range(6)]
+    attn_in, grads, context, grad_low, layer_part, mate_out = [refs.pop(0) for _ in range(6)]
+    going, turning = (refs.pop(0), refs.pop(0)) if line else (None, None)
+    whole, layer, sums, summed, kv_out = [refs.pop(0) for _ in range(5)]
+    final = refs.pop(0) if line else None
+    partial, kv_sent, kv_got, mate_in = [refs.pop(0) for _ in range(4)]
+    buffers = [refs.pop(0) for _ in range(4)] if line else []
+    sent, got, crossing, crossed, running, arrived, send, recv = refs
     copies = Copies(tensors, send, recv)
     bits = [1 << k for k in range(experts.bit_length() - 1)]
-    copies.greet([copies.core, copies.far] + [copies.across(bit) for bit in bits])
+    position = lax.axis_index("expert") // 2
+    copies.greet([copies.core, copies.far] + [copies.across(bit) for bit in bits], line)
     rows = stream.shape[0]
+    lines = []
+    if line:
+        end, inner = position == line - 1, (position > 0) & (position < line - 1)
+        lines = [
+            copies.along(going, final.at[0], 1, position < line - 1, position > 0),
+            copies.along(going, final.at[1], -1, end, position == line - 2),
+            copies.along(turning, final.at[1], -1, inner, position < line - 2),
+        ]
+    mate = copies.start(mate_out, mate_in, copies.mate)
 
     def part(place):
-        return dot(grads[place * rows : (place + 1) * rows, :], weight[...], 1, 1)
-
-    grad_in = sum_quarter(copies, part, sent, got, crossing, crossed)
+        return dot(grads_rel[place * rows : (place + 1) * rows, :], weight[...], 1, 1)
+
+    if line:
+        send_pair, reach_step, settle, spread_step, spread_mate, finish_sum = line_sum(
+            copies, line, partial, summed, *buffers
+        )
+
+    def projections():
+        lead = lax.axis_index("tensor") % 2
+        query_width = context.shape[1]
+        kept_at = pl.ds(pl.multiple_of(query_width + lead * HD, HD), HD)
+        sent_at = pl.ds(pl.multiple_of(query_width + (1 - lead) * HD, HD), HD)
+        kv_sent[...] = dot(grads[:, sent_at], attn_in[...], 0, 0).astype(BF16)
+        kv = copies.start(kv_sent, kv_got, copies.core)
+        partial[:query_width, :] = dot(grads[:, :query_width], attn_in[...], 0, 0).astype(BF16)
+        partial[query_width + HD :, :] = dot(context[...], grad_low[...], 0, 0).astype(BF16)
+        kept = dot(grads[:, kept_at], attn_in[...], 0, 0)
+        kv.wait_recv()
+        partial[query_width : query_width + HD, :] = (kept + kv_got[...].astype(F32)).astype(BF16)
+        if line:
+            send_pair()
+
+    grad_in = sum_quarter(copies, part, sent, got, crossing, crossed, projections)
     _, normed, inverse = rms_norm(stream[...].astype(F32), gain[...])
     through, first = norm_backward(grad_in, normed, inverse, gain[...])
     whole[:rows, :] = (grad_after[...] + through).astype(BF16)
 
-    def fill():
+    def small_sums():
         running[0] = early[...]
         running[0, experts + 1 : experts + 2, :] = first[None]
         steps = [copies.core] + [copies.across(bit) for bit in bits] + [copies.far]
@@ -511,36 +877,94 @@
             else:
                 sums[...] = running[step] + arrived[step]
 
-    gather_quarters(copies, whole, rows, fill)
+    def beside_inputs():
+        mate.wait_recv()
+        layer[:rows, :] = (layer_part[...] + mate_in[...].astype(F32)).astype(BF16)
+        if line:
+            for reach in range(line - 1, 0, -1):
+                reach_step(reach)
+
+    def beside_layer():
+        if line:
+            settle()
+            spread_step(1)
+        small_sums()
+        if line:
+            for hop in range(1, line):
+                spread_mate(hop)
+                if hop < line - 1:
+                    spread_step(hop + 1)
+            finish_sum()
+            query_width = context.shape[1]
+            mine = summed.at[pl.ds(query_width, HD)]
+            far = copies.start(mine, kv_out.at[0], copies.far)
+            first_kv = copies.start(mine, kv_out.at[1], copies.core)
+            far.wait_recv()
+            last_kv = copies.start(kv_out.at[0], kv_out.at[2], copies.core)
+            first_kv.wait_recv()
+            last_kv.wait_recv()
+
+    gather_quarters(copies, whole, rows, beside_inputs)
+    gather_quarters(copies, layer, rows, beside_layer)
+    if not line:
+        summed[...] = partial[...]
+        kv_out[...] = jnp.zeros(kv_out.shape, BF16)
+    for copy in lines:
+        copy.wait_recv()
     copies.finish()
 
 
-def inputs_back(tensors, experts, *operands):
+def inputs_back(tensors, experts, line, *operands):
     rows, width = operands[2].shape
-    early = operands[-1].shape
+    early = operands[5].shape
     steps = 1 + experts.bit_length()
+    shape = jax.ShapeDtypeStruct
+    query_width = operands[8].shape[1]
+    projected = 2 * query_width + HD
+    quarter = pltpu.VMEM((rows, width), BF16)
+    half = pltpu.VMEM((2 * rows, width), BF16)
+    buffers = []
+    if line:
+        chunk = projected // 2 // line
+        buffers = [
+            pltpu.VMEM((projected // 2, width), BF16),
+            pltpu.VMEM((6, chunk, width), BF16),
+            pltpu.VMEM((3, chunk, width), BF16),
+            pltpu.VMEM((3, chunk, width), BF16),
+        ]
     return pl.pallas_call(
-        functools.partial(inputs_back_kernel, tensors, experts),
+        functools.partial(inputs_back_kernel, tensors, experts, line),
         out_shape=[
-            jax.ShapeDtypeStruct((4 * rows, width), BF16),
-            jax.ShapeDtypeStruct(early, F32),
-        ],
-        in_specs=[vmem()] * len(operands),
-        out_specs=[vmem()] * 2,
+            shape((4 * rows, width), BF16),
+            shape((4 * rows, width), BF16),
+            shape(early, F32),
+            shape((projected, width), BF16),
+            shape((3, HD, width), BF16),
+        ]
+        + ([shape((2,) + operands[12].shape, BF16)] if line else []),
+        in_specs=[vmem()] * 12 + [anywhere()] * (len(operands) - 12),
+        out_specs=[vmem()] * 5 + [anywhere()] * bool(line),
         scratch_shapes=[
-            pltpu.VMEM((2 * rows, width), BF16),
-            pltpu.VMEM((2 * rows, width), BF16),
-            pltpu.VMEM((rows, width), BF16),
-            pltpu.VMEM((rows, width), BF16),
+            pltpu.VMEM((projected, width), BF16),
+            pltpu.VMEM((HD, width), BF16),
+            pltpu.VMEM((HD, width), BF16),
+            quarter,
+        ]
+        + buffers
+        + [
+            half,
+            half,
+            quarter,
+            quarter,
             pltpu.VMEM((steps,) + early, F32),
             pltpu.VMEM((steps,) + early, F32),
-            pltpu.SemaphoreType.DMA((6 + steps,)),
-            pltpu.SemaphoreType.DMA((6 + steps,)),
+            pltpu.SemaphoreType.DMA((50 + steps,)),
+            pltpu.SemaphoreType.DMA((50 + steps,)),
         ],
         compiler_params=pltpu.CompilerParams(
-            collective_id=3, has_side_effects=True, vmem_limit_bytes=48 * 2**20
+            collective_id=3, has_side_effects=True, vmem_limit_bytes=60 * 2**20
         ),
-        cost_estimate=pl.CostEstimate(flops=5 * 10**10, bytes_accessed=10**7, transcendentals=0),
+        cost_estimate=pl.CostEstimate(flops=10**11, bytes_accessed=10**7, transcendentals=0),
     )(*operands)
 
 
@@ -572,60 +996,39 @@
     order = nearest_first(line)
 
     own_weights = jnp.concatenate([w_gate[0].T, w_up[0].T, w_down[0]], 0)
-    short = line <= 4
-    if short:
-        arrived = {0: own_weights}
-        for step in range(1, line):
-            arrived[-step] = links.along(arrived[1 - step] if step > 1 else own_weights, 1)
-            arrived[step] = links.along(arrived[step - 1] if step > 1 else own_weights, -1)
-        weights = [own_weights]
-        for slot in range(line - 1):
-            takers = {}
-            for p in range(line):
-                takers.setdefault(order[p][slot], []).append(p)
-            weights.append(pick(place, [(arrived[o], ps) for o, ps in takers.items()]))
-    else:
+    short = line if line == 4 else 0
+    if not short:
         sides = [[2 * p + s for p in range(line)] for s in range(2)]
         weights = lax.all_gather(own_weights, "expert", axis_index_groups=sides)
 
-    grad_rel = links.relative(cotangent)
     rows, half = length // 4, length // 2
-    grad_half = links.over_pair(grad_rel[:half])
-    grad_pair = jnp.concatenate([grad_half, links.over_tensor(grad_half, 1)], 0)
-    routes_own = links.relative(routes).T
-    routes_pair = links.over_pair(routes_own)
-
-    cos_table, sin_table = rotary_tables(length, HD)
-    residual = inputs.astype(F32)
-    first_out, _, _ = rms_norm(residual, first_gain)
-    attn_in = first_out.astype(BF16)
+    cos, sin = rotary_tables(length)
     key_weight = lax.dynamic_slice_in_dim(w_key, kv_head * HD, HD, 1)
     value_weight = lax.dynamic_slice_in_dim(w_value, kv_head * HD, HD, 1)
-    query_rot = rotate(
-        dot(attn_in, w_query, 1, 0).reshape(length, heads, HD), cos_table[:, None], sin_table[:, None]
-    ).astype(BF16)
-    key_rot = rotate(dot(attn_in, key_weight, 1, 0), cos_table, sin_table).astype(BF16)
-    value_low = dot(attn_in, value_weight, 1, 0).astype(BF16)
-    probs, contexts = [], []
-    for head in range(heads):
-        scores = causal(dot(query_rot[:, head], key_rot, 1, 1) * scale)
-        peak = jnp.max(scores, axis=-1, keepdims=True)
-        exponent = jnp.exp(scores - peak)
-        prob = exponent / jnp.sum(exponent, axis=-1, keepdims=True)
-        probs.append(prob)
-        contexts.append(dot(prob.astype(BF16), value_low, 1, 0))
-    context = jnp.concatenate(contexts, 1).astype(BF16)
-    context_rel = links.relative(context)
+    attn_weights = jnp.concatenate([w_query, key_weight, value_weight], 1)
+    routes_own = links.relative(routes).T
+    routes_own = jnp.concatenate([routes_own, routes_own], 0)
+    attn_in, query, key, value, context_rel, logsum, grad_rel, grad_pair, routes_pair, *arrived = attend(
+        tensors, short, inputs, first_gain[None], attn_weights, cos, sin, cotangent, routes_own, own_weights
+    )
+
     def own_quarter(values):
         return lax.dynamic_slice_in_dim(values, links.tensor * rows, rows, 0)
 
     stream = own_quarter(inputs)
+    tokens_own, tokens_pair, after, *second = attend_out(
+        tensors, short, context_rel, w_output, stream, second_gain[None], *(arrived or [None])
+    )
     if short:
-        early = [arrived[o] for o in (-1, 1) if o in arrived]
-        context_rel, *early = lax.optimization_barrier([context_rel] + early)
-    tokens_own, tokens_pair, after = attend_out(
-        tensors, context_rel, w_output, stream, second_gain[None]
-    )
+        arrived, second = arrived[0], second[0]
+        inner = jnp.logical_and(place > 0, place < line - 1)
+        third = lax.ppermute(second, "expert", [(2 + s, s) for s in range(2)] + [(4 + s, 6 + s) for s in range(2)])
+        weights = [
+            own_weights,
+            arrived[0],
+            jnp.where(inner, arrived[1], second),
+            jnp.where(inner, second, third),
+        ]
     names = jnp.arange(experts, dtype=jnp.int32)[:, None, None]
 
     def gates_of(tokens, tokens_routes):
@@ -636,8 +1039,8 @@
         return probs, named, probs * named
 
     router_rows = w_router.T
-    router_probs, named, gates_own = gates_of(tokens_own, routes_own)
-    _, _, gates_pair = gates_of(tokens_pair, routes_pair)
+    router_probs, named, gates_own = gates_of(tokens_own, routes_own[:4])
+    _, _, gates_pair = gates_of(tokens_pair, routes_pair[:4])
 
     both_tokens, both_grads = (tokens_own, tokens_pair), (grad_rel, grad_pair)
     if short:
@@ -691,13 +1094,33 @@
     slot_at = slot_of[numbers // 2] + jnp.where(numbers % 2 == side, 0, line)
     slot_names_hot = (slot_at[:, None] == numbers[None, :]).astype(F32)
     gate_sums = jnp.concatenate([gate_own, gate_pair], 0)
-    grad_after_low, grad_after, grad_router, grad_second = tokens_back(
+    factors = []
+    if short:
+        factors = [first_own[2], first_pair[2], first_own[1], first_pair[1]]
+        factors += [last_own[1], last_pair[1], last_own[0], last_pair[0], *both_tokens, *both_grads]
+    if short:
+        moe_own = dot(gated_own, all_down, 0, 0).astype(BF16)
+        moe_pair = dot(gated_pair, all_down, 0, 0).astype(BF16)
+    else:
+        moe_own, moe_pair = moe_own.astype(BF16), moe_pair.astype(BF16)
+    (
+        grad_after_low,
+        grad_after,
+        grad_router,
+        grad_second,
+        attn_grads,
+        grads_rel,
+        layer_part,
+        mate_moe,
+        _,
+        *weight_sums,
+    ) = tokens_back(
         tensors,
         experts,
+        short,
+        hidden,
         kept_pair,
-        sent_pair,
         kept_own,
-        sent_own,
         gate_sums[:, :half],
         gate_sums[:, half:],
         slot_names_hot,
@@ -707,107 +1130,69 @@
         after,
         second_gain[None],
         own_quarter(cotangent),
+        w_output,
+        query,
+        key,
+        value,
+        logsum,
+        cos,
+        sin,
+        sent_pair,
+        sent_own,
+        moe_own,
+        moe_pair,
+        *factors,
     )
 
+    line_sums = []
     if short:
-        moe_own = dot(gated_own, all_down, 0, 0).astype(BF16)
-        moe_pair = dot(gated_pair, all_down, 0, 0).astype(BF16)
-    moe = jnp.stack([moe_own, moe_pair])
-    got = links.over_tensor(moe[:, half:].astype(BF16), 1).astype(F32)
-    crossing = (moe[:, rows:half].astype(F32) + got[:, rows:]).astype(BF16)
-    moe = moe[:, :rows].astype(F32) + got[:, :rows] + links.over_tensor(crossing, 2).astype(F32)
-    moe = moe[0] + links.over_pair(moe[1].astype(BF16)).astype(F32)
-    layer_out = links.absolute(links.gather((after + moe).astype(BF16)))
-
-    def sum_rows(values):
-        return lax.psum(values, "expert")
-
-    def flow(step):
-        got = None
-        for reach in range(line - 1, 0, -1):
-            takers = {}
-            for p in range(line):
-                if 0 <= p + step * reach < line:
-                    takers.setdefault(1 + order[p].index(step * reach), []).append(p)
-            total = pick(place, [(weight_grads[s], ps) for s, ps in takers.items()])
-            if got is not None:
-                total = total.astype(F32) + got.astype(F32)
-            got = links.along(total.astype(BF16), step, reach)
-        return got.astype(F32)
-
-    if short:
-        weight_grads = {}
-        for slot in range(line - 1, -1, -1):
-            if slot == last:
-                columns, own, pair = 0, last_own, last_pair
-            else:
-                columns, own, pair = slot, first_own[1:], first_pair[1:]
-            weight_grads[slot] = weight_grad(
-                columns,
-                hidden,
-                (own[1], pair[1]),
-                (own[0], pair[0]),
-                both_tokens,
-                both_grads,
-                F32 if slot == 0 else BF16,
-            )
-        expert_grads = weight_grads[0]
-        if line > 1:
-            expert_grads = expert_grads + flow(1) + flow(-1)
+        own_sum, line_sums = weight_sums[0], weight_sums[-2:]
     else:
         expert_grads = lax.psum_scatter(
             weight_grads, "expert", scatter_dimension=0, axis_index_groups=sides
         ).astype(F32)
 
-    grad_output = dot(context_rel, grad_after_low, 0, 0).astype(BF16)
-    grad_output = sum_rows(grad_output).astype(F32)
-    grad_context = links.absolute(dot(grad_after_low, w_output, 1, 1).astype(BF16))
-    grad_heads = grad_context.reshape(length, heads, HD)
-    query_grads = []
-    key_grad = jnp.zeros((length, HD), F32)
-    value_grad = jnp.zeros((length, HD), F32)
-    for head in range(heads):
-        dprob = dot(grad_heads[:, head], value_low, 1, 1)
-        delta = jnp.sum(probs[head] * dprob, axis=-1, keepdims=True)
-        dscore = (probs[head] * (dprob - delta)).astype(BF16)
-        query_grads.append(dot(dscore, key_rot, 1, 0) * scale)
-        key_grad = key_grad + dot(dscore, query_rot[:, head], 0, 0) * scale
-        value_grad = value_grad + dot(probs[head].astype(BF16), grad_heads[:, head], 0, 0)
-    query_grad = jnp.concatenate(
-        [unrotate(g, cos_table, sin_table).astype(BF16) for g in query_grads], 1
-    )
-    key_grad = unrotate(key_grad, cos_table, sin_table).astype(BF16)
-    value_grad = value_grad.astype(BF16)
-    attn_weights = jnp.concatenate([w_query, key_weight, value_weight], 1)
-    attn_grads = jnp.concatenate([query_grad, key_grad, value_grad], 1)
-    grads_rel = links.relative(attn_grads)
     early = jnp.zeros((-(-(experts + 2) // 8) * 8, width), F32)
     early = early.at[:experts].set(grad_router).at[experts : experts + 1].set(grad_second)
-    grad_inputs, sums = inputs_back(
-        tensors, experts, grads_rel, attn_weights, stream, first_gain[None], grad_after, early
+    grad_inputs, layer_out, sums, summed, kv_rest, *got = inputs_back(
+        tensors,
+        experts,
+        short,
+        grads_rel,
+        attn_weights,
+        stream,
+        first_gain[None],
+        grad_after,
+        early,
+        attn_in,
+        attn_grads,
+        context_rel,
+        grad_after_low,
+        layer_part,
+        mate_moe,
+        *line_sums,
     )
-    grad_inputs = links.absolute(grad_inputs)
+    query_width = heads * HD
+    if short:
+        got = got[0].astype(F32)
+        expert_grads = own_sum + jnp.where(place > 0, got[0], 0.0) + jnp.where(place < line - 1, got[1], 0.0)
+        kv_mine, (kv_far, kv_core, kv_across) = summed[query_width : query_width + HD], kv_rest
+    else:
+        summed = lax.psum(summed, "expert")
+        kv_mine = summed[query_width : query_width + HD]
+        kv_far = links.over_tensor(kv_mine, 2)
+        kv_core, kv_across = links.over_tensor(kv_mine, 1), links.over_tensor(kv_far, 1)
+    grad_query = summed[:query_width].T.astype(F32)
+    grad_output = summed[query_width + HD :].astype(F32)
+    lead, low_head = links.tensor % 2 == 0, kv_head == 0
+    keys = jnp.where(lead, kv_mine, kv_core), jnp.where(lead, kv_far, kv_across)
+    values = jnp.where(lead, kv_core, kv_mine), jnp.where(lead, kv_across, kv_far)
+    grad_key, grad_value = [
+        jnp.concatenate([jnp.where(low_head, near, far), jnp.where(low_head, far, near)], 0).T.astype(F32)
+        for near, far in (keys, values)
+    ]
+    grad_inputs, layer_out = links.absolute(grad_inputs), links.absolute(layer_out)
     grad_router, grad_second, grad_first = sums[:experts].T, sums[experts], sums[experts + 1]
-    query_width = heads * HD
-    attn_weight_grads = dot(attn_grads, attn_in, 0, 0)
-    lead = links.tensor % 2
-    kv_kept = lax.dynamic_slice_in_dim(attn_weight_grads, query_width + lead * HD, HD, 0)
-    kv_sent = lax.dynamic_slice_in_dim(attn_weight_grads, query_width + (1 - lead) * HD, HD, 0)
-    kv_kept = kv_kept + links.over_tensor(kv_sent.astype(BF16), 1).astype(F32)
-    summed = sum_rows(
-        jnp.concatenate([attn_weight_grads[:query_width].astype(BF16), kv_kept.astype(BF16)], 0)
-    )
-    grad_query = summed[:query_width].T.astype(F32)
-    kv_mine = summed[query_width:]
-    kv_theirs = links.over_tensor(kv_mine, 2)
-    first_head = kv_head == 0
-    kv_both = jnp.concatenate(
-        [jnp.where(first_head, kv_mine, kv_theirs), jnp.where(first_head, kv_theirs, kv_mine)], 0
-    )
-    kv_other = links.over_tensor(kv_both, 1)
-    grad_key = jnp.where(lead == 0, kv_both, kv_other).T.astype(F32)
-    grad_value = jnp.where(lead == 0, kv_other, kv_both).T.astype(F32)
-
     return (
         layer_out,
         grad_inputs,

time: 682 us -> 542 us (0.79)
  Pallas kernels: 276 us -> 431 us
  waiting for transfers between devices: 128 us -> 26.4 us
  other arithmetic: 78.1 us -> 18.7 us
  starting transfers between devices: 50.2 us -> 1.45 us
  matrix products: 56.7 us -> 11.9 us
  local copies, waits for them, and re-layouts: 67 us -> 37.7 us
  between operations: 18.5 us -> 4.13 us
    pallas_call x7 -> x4, Pallas kernels: 209 us -> 379 us  [the longest x1 134 us: inputs_back(): pl.pallas_call(functools.partial(inputs_back_kernel, tensors, experts, li...]
    psum x1 -> x0, waiting for transfers between devices: 93.3 us -> none  [sum_rows(): return lax.psum(values, 'expert')]
    ppermute x23 -> x1, starting transfers between devices: 50.2 us -> 1.45 us  [shards(): lax.ppermute(second, 'expert', [(2 + s, s) for s in range(2)] + [(4 + s,...]
    dot_general x25 -> x4, matrix products: 56.7 us -> 11.9 us  [dot(): lax.dot_general(left, right, (((left_dim,), (right_dim,)), ((), ())), pre...]
    unnamed x250 -> x87, local copies, waits for them, and re-layouts: 40.8 us -> 17.4 us
    convert_element_type x12 -> x4, other arithmetic: 26.6 us -> 7.81 us  [the longest x1 3.12 us: shards(): got = got[0].astype(F32)]
    unnamed x3 -> x0, Pallas kernels: 13.4 us -> none
    concatenate x10 -> x1, other arithmetic: 11.9 us -> 0.01 us  [shards(): routes_own = jnp.concatenate([routes_own, routes_own], 0)]
  transfers between devices with their start and end apart: 24 -> 1, of which waited for: 4 -> 1; matrix products, arithmetic and copies ran while one was open for 23% -> 2% of each run, Pallas kernels for 32% -> 0%
where the time goes in v3:
time: 542 us; the launch traced here: 532 us
  Pallas kernels  431 us (80%)
  local copies, waits for them, and re-layouts  37.7 us (7%)
  waiting for transfers between devices  26.4 us (5%)
  other arithmetic  18.7 us (3%)
  matrix products  11.9 us (2%)
    pallas_call x1, Pallas kernels, inputs_back(): pl.pallas_call(functools.partial(inputs_back_kernel, tensors, experts, li...  134 us
    pallas_call x1, Pallas kernels, tokens_back(): pl.pallas_call(functools.partial(tokens_back_kernel, tensors, line, hidde...  129 us
    pallas_call x1, Pallas kernels, attend_out(): pl.pallas_call(functools.partial(attend_out_kernel, tensors, line), out_s...  66.5 us
    pallas_call x4, Pallas kernels, expert_pass(): pl.pallas_call(functools.partial(expert_kernel, count, hidden, split, bef...  52.4 us
    pallas_call x1, Pallas kernels, attend(): pl.pallas_call(functools.partial(attend_kernel, tensors, line, heads), ou...  49.4 us
    ppermute x1, waiting for transfers between devices, shards(): lax.ppermute(second, 'expert', [(2 + s, s) for s in range(2)] + [(4 + s,...  26.4 us
    unnamed x87, local copies, waits for them, and re-layouts  17.4 us
    dot_general x4, matrix products, dot(): lax.dot_general(left, right, (((left_dim,), (right_dim,)), ((), ())), pre...  11.9 us
  transfers between devices with their start and end apart: 1, of which 1 were waited for; matrix products, arithmetic and copies ran while one was open for 2% of the time, Pallas kernels for 0%

profile of v3, /device:TPU:1, one launch (start us, length us, event | category | flops | bytes accessed | tf_op | source)
XLA Modules:
  0.0 531.6 jit_solution(17849020516481761521)
XLA Ops:
  0.7 0.9 constant_dynamic-slice_fusion.14
  1.6 0.7 broadcast_in_dim.18.refs_1_.refs_3_
  2.3 0.7 broadcast_in_dim.19.refs_3_.refs_9_
  3.0 2.4 constant_dynamic-slice_fusion.8
  5.6 1.5 pad_maximum_fusion.3.refs_2_.refs_1_
  8.2 49.4 %shard_map.274 = (bf16[1024,1536]{1,0:T(8,128)(2,1)}, bf16[1024,384]{1,0:T(8,128)(2,1)S(1)}, bf16[1024,128]{1,0:T(8,128)(2,1)S(1)}, bf16[1024,128]{1,0:T(8,128)(...) custom-call(bf16[1024,1536]{1,0:T(8,128)(2,1)} %refs_0_.1, ...), custom_call_target="tpu_custom_call" | custom-call | flops 40000000000 | bytes 10000000 | tf_op jit(solution)/shard_map/pallas_call | solution.py:406
  57.6 0.8 copy-done.23
  58.5 66.5 %shard_map.275 = (bf16[1024,1536]{1,0:T(8,128)(2,1)S(1)}, bf16[1024,1536]{1,0:T(8,128)(2,1)S(1)}, f32[256,1536]{1,0:T(8,128)S(1)}, bf16[576,1536]{1,0:T(8,128)(2,1)}) custom-call(bf16[1024,384]{1,0:T(8,128)(2,1)S(1)} %get-tuple-element.85.refs_0_.refs_8_, bf16[384,1536]{1,0:T(8,128)(2,1)S(1)} %copy-done.11, ...), custom_call_target="tpu_custom_call" | custom-call | flops 60000002048 | bytes 10000000 | tf_op jit(solution)/shard_map/pallas_call | solution.py:509
  125.0 1.7 copy-done.1
  126.7 1.2 copy-done.22
  127.9 1.5 collective-permute-start
  129.4 0.7 fusion.19
  130.1 2.8 fusion.25
  133.0 0.9 fusion.26
  133.9 0.7 fusion.20
  139.8 0.7 fusion.14.refs_4_
  141.0 1.1 slice_bitcast_fusion.4
  142.1 1.6 slice_bitcast_fusion.refs_5_
  143.8 26.4 %collective-permute-done = bf16[576,1536]{1,0:T(8,128)(2,1)} collective-permute-done((bf16[576,1536]{1,0:T(8,128)(2,1)}, bf16[576,1536]{1,0:T(8,128)(2,1)}, u32[]{:S(2)}, u32[]{:S(2)}) %collective-permute-start) | collective-permute-done | bytes 1769504 | tf_op jit(solution)/shard_map/ppermute | solution.py:1025
  170.1 2.3 bitcast_select_fusion
  172.5 1.1 copy-done.29
  173.7 17.7 %shard_map.276 = (bf16[1024,1536]{1,0:T(8,128)(2,1)}, bf16[576,1024]{1,0:T(8,128)(2,1)S(1)}, bf16[1152,1024]{1,0:T(8,128)(2,1)}, f32[3,1024]{1,0:T(4,128)S(1)}) custom-call(s32[3]{0:T(128)S(1)} %slice_bitcast_fusion.6.refs_0_, bf16[1024,1536]{1,0:T(8,128)(2,1)} %copy-done.1, bf16[1024,1536]{1,0:T(8,128)(2,1)} %get-tuple-element.88.refs_2_.refs_33_, ...), custom_call_target="tpu_custom_call" | custom-call | flops 9059696640 | bytes 17891328 | tf_op jit(solution)/shard_map/pallas_call | solution.py:156
  191.4 8.1 %shard_map.277 = (bf16[512,1536]{1,0:T(8,128)(2,1)S(1)}, bf16[512,1536]{1,0:T(8,128)(2,1)S(1)}, bf16[192,1024]{1,0:T(8,128)(2,1)S(1)}, bf16[384,1024]{1,0:T(8,128)(2,1)S(1)}, f32[1,1024]{1,0:T(1,128)S(1)}) custom-call(s32[1]{0:T(128)} %bitcast.refs_0_, bf16[1024,1536]{1,0:T(8,128)(2,1)} %copy-done.1, bf16[1024,1536]{1,0:T(8,128)(2,1)} %get-tuple-element.88.refs_2_.refs_33_, ...), custom_call_target="tpu_custom_call" | custom-call | flops 3019898880 | bytes 14352384 | tf_op jit(solution)/shard_map/pallas_call | solution.py:156
  199.5 1.1 copy-done.8
  200.7 18.1 %shard_map.278 = (bf16[1024,1536]{1,0:T(8,128)(2,1)}, bf16[576,1024]{1,0:T(8,128)(2,1)S(1)}, bf16[1152,1024]{1,0:T(8,128)(2,1)}, f32[3,1024]{1,0:T(4,128)S(1)}) custom-call(s32[3]{0:T(128)S(1)} %slice_bitcast_fusion.6.refs_0_, bf16[1024,1536]{1,0:T(8,128)(2,1)} %copy-done, bf16[1024,1536]{1,0:T(8,128)(2,1)} %get-tuple-element.94.refs_2_.refs_32_, ...), custom_call_target="tpu_custom_call" | custom-call | flops 9059696640 | bytes 17891328 | tf_op jit(solution)/shard_map/pallas_call | solution.py:156
  218.8 8.5 %shard_map.279 = (bf16[512,1536]{1,0:T(8,128)(2,1)S(1)}, bf16[512,1536]{1,0:T(8,128)(2,1)S(1)}, bf16[192,1024]{1,0:T(8,128)(2,1)S(1)}, bf16[384,1024]{1,0:T(8,128)(2,1)S(1)}, f32[1,1024]{1,0:T(1,128)S(1)}) custom-call(s32[1]{0:T(128)} %bitcast.refs_0_, bf16[1024,1536]{1,0:T(8,128)(2,1)} %copy-done, bf16[1024,1536]{1,0:T(8,128)(2,1)} %get-tuple-element.94.refs_2_.refs_32_, ...), custom_call_target="tpu_custom_call" | custom-call | flops 3019898880 | bytes 14352384 | tf_op jit(solution)/shard_map/pallas_call | solution.py:156
  227.3 0.7 fusion.23
  228.1 4.1 convolution_convert_fusion.refs_21_
  232.2 4.1 convolution_convert_fusion.1.refs_20_
  236.3 129.0 %shard_map.280 = (bf16[1024,1536]{1,0:T(8,128)(2,1)}, f32[256,1536]{1,0:T(8,128)}, f32[8,1536]{1,0:T(8,128)}, f32[1,1536]{1,0:T(1,128)}, bf16[1024,640]{1,0:T(8,...) custom-call(bf16[512,1536]{1,0:T(8,128)(2,1)} %copy-done.7, ...), custom_call_target="tpu_custom_call" | custom-call | flops 99999997952 | bytes 10000000 | tf_op jit(solution)/shard_map/pallas_call | solution.py:710
  365.3 0.8 scatter.6
  366.1 0.8 scatter.9.refs_5_
  367.6 134.0 %shard_map.281 = (bf16[1024,1536]{1,0:T(8,128)(2,1)}, bf16[1024,1536]{1,0:T(8,128)(2,1)}, f32[16,1536]{1,0:T(8,128)}, bf16[896,1536]{1,0:T(8,128)(2,1)}, bf16[3,...) custom-call(bf16[1024,640]{1,0:T(8,128)(2,1)} %get-tuple-element.116.refs_0_, ...), custom_call_target="tpu_custom_call" | custom-call | flops 99999997952 | bytes 10000000 | tf_op jit(solution)/shard_map/pallas_call | solution.py:935
  501.6 1.4 slice_bitcast_fusion.5
  503.1 1.5 slice_reduce_fusion
  504.6 3.1 convert_element_type.45
  507.7 1.2 fusion.1
  508.9 1.9 slice_bitcast_fusion.1
  510.8 1.2 copy-done.30
  512.0 2.0 slice_convert_fusion
  514.2 1.3 convert_bitcast_fusion.1
  515.5 3.0 copy.39
  518.5 1.3 convert_bitcast_fusion.2
  519.8 3.0 copy.38
  522.9 1.9 copy.37
  524.8 2.2 constant_dynamic-slice_fusion.3
  527.8 1.8 pad_maximum_fusion.1
  529.6 1.8 pad_maximum_fusion
  (103 shorter events, 6.2 us)
Async XLA Ops:
  0.6 4.8 copy-start.37
  0.7 5.0 copy-start.32
  2.3 5.7 %copy-start.5 = (f32[1,1536]{1,0:T(1,128)}, f32[1,1536]{1,0:T(1,128)S(1)}, u32[]{:S(2)}) copy-start(f32[1,1536]{1,0:T(1,128)S(1)} %broadcast_in_dim.18.refs_1_.refs_3_) | copy-start | bytes 18436
  3.0 55.4 %copy-start.6 = (f32[1,1536]{1,0:T(1,128)}, f32[1,1536]{1,0:T(1,128)S(1)}, u32[]{:S(2)}) copy-start(f32[1,1536]{1,0:T(1,128)S(1)} %broadcast_in_dim.19.refs_3_.refs_9_) | copy-start | bytes 18436
  3.0 2.4 copy-start.38
  5.5 53.0 %copy-start.4 = (bf16[256,1536]{1,0:T(8,128)(2,1)}, bf16[256,1536]{1,0:T(8,128)(2,1)S(1)}, u32[]{:S(2)}) copy-start(bf16[256,1536]{1,0:T(8,128)(2,1)S(1)} %get-tuple-element.210.refs_2_) | copy-start | bytes 2359300
  5.5 1.7 copy-start.33
  5.5 2.1 copy-start.34
  5.5 2.4 copy-start.35
  5.6 2.4 copy-start.16
  5.6 2.6 copy-start.17
  8.2 49.4 %copy-start.2 = (bf16[576,1536]{1,0:T(8,128)(2,1)}, bf16[576,1536]{1,0:T(8,128)(2,1)S(1)}, u32[]{:S(2)}) copy-start(bf16[576,1536]{1,0:T(8,128)(2,1)S(1)} %pad_maximum_fusion.4.refs_7_.refs_4_) | copy-start | bytes 5308420
  8.2 50.3 %copy-start.11 = (bf16[384,1536]{1,0:T(8,128)(2,1)S(1)}, bf16[384,1536]{1,0:T(8,128)(2,1)}, u32[]{:S(2)}) copy-start(bf16[384,1536]{1,0:T(8,128)(2,1)} %refs_11_.1) | copy-start | bytes 3538948
  57.6 0.8 copy-start.23
  58.4 66.5 %copy-start.20 = (bf16[1024,384]{1,0:T(8,128)(2,1)}, bf16[1024,384]{1,0:T(8,128)(2,1)S(1)}, u32[]{:S(2)}) copy-start(bf16[1024,384]{1,0:T(8,128)(2,1)S(1)} %get-tuple-element.85.refs_0_.refs_8_) | copy-start | bytes 2359300
  58.4 66.5 %copy-start.21 = (bf16[1024,384]{1,0:T(8,128)(2,1)}, bf16[1024,384]{1,0:T(8,128)(2,1)S(1)}, u32[]{:S(2)}) copy-start(bf16[1024,384]{1,0:T(8,128)(2,1)S(1)} %get-tuple-element.102.refs_12_) | copy-start | bytes 2359300
  58.4 66.6 %copy-start.24 = (bf16[1024,128]{1,0:T(8,128)(2,1)}, bf16[1024,128]{1,0:T(8,128)(2,1)S(1)}, u32[]{:S(2)}) copy-start(bf16[1024,128]{1,0:T(8,128)(2,1)S(1)} %get-tuple-element.103.refs_13_) | copy-start | bytes 786436
  58.4 66.6 %copy-start.25 = (bf16[1024,128]{1,0:T(8,128)(2,1)}, bf16[1024,128]{1,0:T(8,128)(2,1)S(1)}, u32[]{:S(2)}) copy-start(bf16[1024,128]{1,0:T(8,128)(2,1)S(1)} %get-tuple-element.104.refs_14_) | copy-start | bytes 786436
  58.5 71.7 %copy-start.39 = (bf16[1536,8]{0,1:T(8,128)(2,1)S(1)}, bf16[1536,8]{0,1:T(8,128)(2,1)}, u32[]{:S(2)}) copy-start(bf16[1536,8]{0,1:T(8,128)(2,1)} %param.32) | copy-start | bytes 73732
  125.0 1.7 copy-start.1
  126.7 1.2 copy-start.22
  127.9 6.1 %copy-start = (bf16[1024,1536]{1,0:T(8,128)(2,1)}, bf16[1024,1536]{1,0:T(8,128)(2,1)S(1)}, u32[]{:S(2)}) copy-start(bf16[1024,1536]{1,0:T(8,128)(2,1)S(1)} %get-tuple-element.93.refs_1_.refs_30_) | copy-start | bytes 9437188
  127.9 42.3 %collective-permute-start = (bf16[576,1536]{1,0:T(8,128)(2,1)}, bf16[576,1536]{1,0:T(8,128)(2,1)}, u32[]{:S(2)}, u32[]{:S(2)}) collective-permute-start(bf16[576,1536]{1,0:T(8,128)(2,1)} %get-tuple-element.90), channel_id=1, source_target_pairs={{8,0},{12,4},{16,24},{20,28},{9,1},{13,5},{17,25},{21,29},{10,2},{... | collective-permute-start | bytes 5308424 | tf_op jit(solution)/shard_map/ppermute | solution.py:1025
  133.0 3.0 copy-start.41
  139.8 30.4 %copy-start.26 = (bf16[2,576,1536]{2,1,0:T(8,128)(2,1)S(1)}, bf16[2,576,1536]{2,1,0:T(8,128)(2,1)}, u32[]{:S(2)}) copy-start(bf16[2,576,1536]{2,1,0:T(8,128)(2,1)} %get-tuple-element.86.refs_4_) | copy-start | bytes 10616836
  143.7 29.9 %copy-start.3 = (bf16[576,1536]{1,0:T(8,128)(2,1)S(1)}, bf16[576,1536]{1,0:T(8,128)(2,1)}, u32[]{:S(2)}) copy-start(bf16[576,1536]{1,0:T(8,128)(2,1)} %copy-done.2) | copy-start | bytes 5308420
  172.4 1.2 copy-start.29
  191.3 36.7 %copy-start.18 = (bf16[576,1024]{1,0:T(8,128)(2,1)}, bf16[576,1024]{1,0:T(8,128)(2,1)S(1)}, u32[]{:S(2)}) copy-start(bf16[576,1024]{1,0:T(8,128)(2,1)S(1)} %get-tuple-element.110.refs_25_) | copy-start | bytes 3538948
  199.5 1.2 copy-start.8
  200.6 18.1 %copy-start.7 = (bf16[512,1536]{1,0:T(8,128)(2,1)}, bf16[512,1536]{1,0:T(8,128)(2,1)S(1)}, u32[]{:S(2)}) copy-start(bf16[512,1536]{1,0:T(8,128)(2,1)S(1)} %get-tuple-element.92.refs_0_) | copy-start | bytes 4718596
  200.7 18.1 %copy-start.12 = (bf16[384,1024]{1,0:T(8,128)(2,1)}, bf16[384,1024]{1,0:T(8,128)(2,1)S(1)}, u32[]{:S(2)}) copy-start(bf16[384,1024]{1,0:T(8,128)(2,1)S(1)} %get-tuple-element.115.refs_27_) | copy-start | bytes 2359300
  200.7 27.4 %copy-start.14 = (bf16[192,1024]{1,0:T(8,128)(2,1)}, bf16[192,1024]{1,0:T(8,128)(2,1)S(1)}, u32[]{:S(2)}) copy-start(bf16[192,1024]{1,0:T(8,128)(2,1)S(1)} %get-tuple-element.111.refs_29_) | copy-start | bytes 1179652
  218.7 13.5 %copy-start.19 = (bf16[576,1024]{1,0:T(8,128)(2,1)}, bf16[576,1024]{1,0:T(8,128)(2,1)S(1)}, u32[]{:S(2)}) copy-start(bf16[576,1024]{1,0:T(8,128)(2,1)S(1)} %get-tuple-element.108.refs_24_) | copy-start | bytes 3538948
  218.8 9.3 %copy-start.36 = (bf16[1,192,1536]{2,1,0:T(8,128)(2,1)S(1)}, bf16[1,192,1536]{2,1,0:T(8,128)(2,1)}, u32[]{:S(2)}) copy-start(bf16[1,192,1536]{2,1,0:T(8,128)(2,1)} %param.35) | copy-start | bytes 1769476
  227.2 5.0 copy-start.9
  227.2 4.9 copy-start.10
  227.3 4.9 copy-start.13
  227.3 4.9 copy-start.15
  366.9 0.6 copy-start.40
  504.6 3.1 copy-start.27
  508.9 3.1 copy-start.30
  512.0 2.0 copy-start.31
  524.8 2.8 copy-start.28
